TPU v7x, 32 devices: a whole 2x2x4 slice. The times are simulated.
32 devices in a mesh: dp: 4 (over z), row: 4 (over y, x), col: 2 (over core).
Axes of the slice: x: 2, y: 2, z: 4, core: 2. Of those that a mesh axis runs over, the one named last changes fastest.
Arguments:
- tokens: bfloat16 [9232, 1024], P('dp', ('row', 'col')), may hold values from -80 to 80
- projector: bfloat16 [3, 1024, 1024], P(None, 'row', 'col'), may hold values from -0.25 to 0.25
- offsets: float32 [2, 1024], P(None, 'col'), may hold values from -3 to 3
- combiner: bfloat16 [1024, 1024], P('col', 'row'), may hold values from -0.25 to 0.25
- baseline: float32 [1024], P(('row', 'col')), may hold values from -2 to 2
- widener: bfloat16 [1024, 4096], P('row', 'col'), may hold values from -0.1875 to 0.1875
- thresholds: float32 [4096], P('col'), may hold values from -3 to 3
- narrower: bfloat16 [4096, 1024], P('col', 'row'), may hold values from -0.125 to 0.125
- residue: float32 [1024], P(('row', 'col')), may hold values from -2 to 2
- stretch: float32 [1024], P(('row', 'col')), may hold values from 0.5 to 1.5
- lifting: float32 [1024], P(('row', 'col')), may hold values from -2 to 2
- dilation: float32 [1024], P(('row', 'col')), may hold values from 0.5 to 1.5
- elevation: float32 [1024], P(('row', 'col')), may hold values from -2 to 2
- cotangent: bfloat16 [9232, 1024], P('dp', ('row', 'col')), may hold values from -6 to 6
Outputs:
- layer_output: float32 [9232, 1024], P('dp', ('row', 'col'))
- tokens_delta: float32 [9232, 1024], P('dp', ('row', 'col'))
- projector_delta: float32 [3, 1024, 1024], P(None, 'row', 'col')
- offsets_delta: float32 [2, 1024], P(None, 'col')
- combiner_delta: float32 [1024, 1024], P('col', 'row')
- baseline_delta: float32 [1024], P(('row', 'col'))
- widener_delta: float32 [1024, 4096], P('row', 'col')
- thresholds_delta: float32 [4096], P('col')
- narrower_delta: float32 [4096, 1024], P('col', 'row')
- residue_delta: float32 [1024], P(('row', 'col'))
- stretch_delta: float32 [1024], P(('row', 'col'))
- lifting_delta: float32 [1024], P(('row', 'col'))
- dilation_delta: float32 [1024], P(('row', 'col'))
- elevation_delta: float32 [1024], P(('row', 'col'))
All inputs are finite; a program needn't handle non-finite values.
Results may differ from a plain program's by a relative error of at most 0.015.
Values may be sent and summed in bfloat16 or wider, within the bound.
No kernel may reach another device: no remote copies, remote signals or barrier semaphores. Data moves between devices by JAX's collectives and lax.ppermute only.
A program may use at most 128 MiB of HBM per device.

v0:
```python
import jax
import jax.numpy as jnp
from jax import lax
from jax.sharding import PartitionSpec as P

D = 1024
HD = 64
SEQ = 577


NORM_EPSILON = 1e-05
SIGMOID_SLOPE = 1.702


def feature_totals(left_term, right_term):
    return lax.psum((jnp.sum(left_term, axis=1), jnp.sum(right_term, axis=1)), ("row", "col"))


def norm_forward(residual, gain_vector, shift_vector):
    summed, squares = feature_totals(residual, residual * residual)
    average = summed / D
    reciprocal = lax.rsqrt(squares / D - average * average + NORM_EPSILON)
    standard = (residual - average[:, None]) * reciprocal[:, None]
    return (standard, reciprocal, (standard * gain_vector + shift_vector).astype(jnp.bfloat16))


def norm_backward(upstream, standard, reciprocal, gain_vector):
    scaled = upstream * gain_vector
    summed, along = feature_totals(scaled, scaled * standard)
    return reciprocal[:, None] * (scaled - summed[:, None] / D - standard * (along[:, None] / D))


def widen_rows(narrow_part):
    return lax.all_gather(narrow_part, "col", axis=1, tiled=True)


def narrow_sum(partial_value):
    return lax.psum_scatter(partial_value, "col", scatter_dimension=1, tiled=True)


def image_scores(queries, key_rows):
    return jnp.einsum(
        "qhd,khd->hqk", queries, key_rows, preferred_element_type=jnp.float32
    ) * HD ** (-0.5)


def attend_image(inputs):
    queries, key_rows, values = inputs
    scores = image_scores(queries, key_rows)
    row_top = jnp.max(scores, axis=2, keepdims=True)
    weights = jnp.exp(scores - row_top)
    row_total = jnp.sum(weights, axis=2, keepdims=True)
    rounded = (weights / row_total).astype(jnp.bfloat16)
    mixed_heads = jnp.einsum("hqk,khd->qhd", rounded, values, preferred_element_type=jnp.float32)
    return (mixed_heads.astype(jnp.bfloat16), row_top, row_total)


def attend_backward(inputs):
    queries, key_rows, values, row_top, row_total, upstream = inputs
    scores = image_scores(queries, key_rows)
    weights = jnp.exp(scores - row_top) / row_total
    rounded = weights.astype(jnp.bfloat16)
    value_grad = jnp.einsum("hqk,qhd->khd", rounded, upstream, preferred_element_type=jnp.float32)
    weight_grad = jnp.einsum("qhd,khd->hqk", upstream, values, preferred_element_type=jnp.float32)
    score_grad = (
        weights * (weight_grad - jnp.sum(weights * weight_grad, axis=2, keepdims=True))
    ).astype(jnp.bfloat16)
    query_grad = jnp.einsum(
        "hqk,khd->qhd", score_grad, key_rows, preferred_element_type=jnp.float32
    ) * HD ** (-0.5)
    key_grad = jnp.einsum(
        "hqk,qhd->khd", score_grad, queries, preferred_element_type=jnp.float32
    ) * HD ** (-0.5)
    return jnp.stack([query_grad, key_grad, value_grad], axis=1).astype(jnp.bfloat16)


def per_device(
    tokens,
    projector,
    offsets,
    combiner,
    baseline,
    widener,
    thresholds,
    narrower,
    residue,
    stretch,
    lifting,
    dilation,
    elevation,
    cotangent,
):
    group_rows = tokens.shape[0]
    row_number = lax.axis_size("row")
    share_rows = group_rows // row_number
    images = share_rows // SEQ
    width_col = projector.shape[2]
    heads_here = width_col // HD
    residual = tokens.astype(jnp.float32)
    bias_triple = jnp.stack([offsets[0], jnp.zeros((width_col,), jnp.float32), offsets[1]])
    standard_one, recip_one, normed_one = norm_forward(residual, stretch, lifting)
    wide_one = widen_rows(normed_one)
    row_block = wide_one
    projected = lax.psum_scatter(
        jnp.einsum("td,sde->tse", row_block, projector, preferred_element_type=jnp.float32).reshape(
            share_rows * lax.axis_size("row"), 3 * width_col
        ),
        "row",
        scatter_dimension=0,
        tiled=True,
    ).reshape(share_rows, 3, width_col)
    triple = (projected + bias_triple).astype(jnp.bfloat16)
    split_triple = triple.reshape(images, SEQ, 3, heads_here, HD)
    queries = split_triple[:, :, 0]
    key_rows = split_triple[:, :, 1]
    values = split_triple[:, :, 2]
    mixed, row_tops, row_totals = lax.map(attend_image, (queries, key_rows, values))
    mixed_share = mixed.reshape(share_rows, width_col)
    mixed_all = lax.all_gather(mixed_share, "row", axis=0, tiled=True)
    attn_part = jnp.dot(mixed_all, combiner, preferred_element_type=jnp.float32)
    resid_two = residual + narrow_sum(attn_part) + baseline
    standard_two, recip_two, normed_two = norm_forward(resid_two, dilation, elevation)
    wide_two = widen_rows(normed_two)
    row_block = wide_two
    expanded = lax.psum_scatter(
        jnp.dot(row_block, widener, preferred_element_type=jnp.float32),
        "row",
        scatter_dimension=0,
        tiled=True,
    )
    expanded = expanded + thresholds
    sigmoid_gate = jax.nn.sigmoid(SIGMOID_SLOPE * expanded)
    hidden = (expanded * sigmoid_gate).astype(jnp.bfloat16)
    hidden_all = lax.all_gather(hidden, "row", axis=0, tiled=True)
    ffn_part = jnp.dot(hidden_all, narrower, preferred_element_type=jnp.float32)
    layer_output = resid_two + narrow_sum(ffn_part) + residue
    upstream = cotangent.astype(jnp.float32)
    residue_delta = jnp.sum(upstream, axis=0)
    upstream_wide = widen_rows(cotangent)
    narrower_delta = jnp.einsum(
        "tf,td->fd", hidden_all, upstream_wide, preferred_element_type=jnp.float32
    )
    row_block = upstream_wide
    grad_hidden = lax.psum_scatter(
        jnp.einsum("td,fd->tf", row_block, narrower, preferred_element_type=jnp.float32),
        "row",
        scatter_dimension=0,
        tiled=True,
    )
    slope_factor = sigmoid_gate + SIGMOID_SLOPE * expanded * sigmoid_gate * (1.0 - sigmoid_gate)
    grad_expanded = (grad_hidden * slope_factor).astype(jnp.bfloat16)
    expanded_all = lax.all_gather(grad_expanded, "row", axis=0, tiled=True)
    thresholds_delta = jnp.sum(expanded_all, axis=0, dtype=jnp.float32)
    widener_delta = jnp.einsum(
        "td,tf->df", wide_two, expanded_all, preferred_element_type=jnp.float32
    )
    grad_two = narrow_sum(
        jnp.einsum("tf,df->td", expanded_all, widener, preferred_element_type=jnp.float32)
    )
    dilation_delta = jnp.sum(grad_two * standard_two, axis=0)
    elevation_delta = jnp.sum(grad_two, axis=0)
    grad_resid = upstream + norm_backward(grad_two, standard_two, recip_two, dilation)
    baseline_delta = jnp.sum(grad_resid, axis=0)
    grad_attn = grad_resid.astype(jnp.bfloat16)
    attn_wide = widen_rows(grad_attn)
    combiner_delta = jnp.einsum(
        "th,td->hd", mixed_all, attn_wide, preferred_element_type=jnp.float32
    )
    row_block = attn_wide
    grad_mixed = lax.psum_scatter(
        jnp.einsum("td,hd->th", row_block, combiner, preferred_element_type=jnp.float32),
        "row",
        scatter_dimension=0,
        tiled=True,
    ).astype(jnp.bfloat16)
    grad_triple = lax.map(
        attend_backward,
        (
            queries,
            key_rows,
            values,
            row_tops,
            row_totals,
            grad_mixed.reshape(images, SEQ, heads_here, HD),
        ),
    )
    grad_triple = grad_triple.reshape(share_rows, 3, width_col)
    triple_gathered = lax.all_gather(
        grad_triple.reshape(share_rows, 3 * width_col), "row", axis=0, tiled=True
    ).reshape(group_rows, 3, width_col)
    triple_sums = jnp.sum(triple_gathered, axis=0, dtype=jnp.float32)
    offsets_delta = jnp.stack([triple_sums[0], triple_sums[2]])
    projector_delta = jnp.einsum(
        "td,tse->sde", wide_one, triple_gathered, preferred_element_type=jnp.float32
    )
    grad_one = narrow_sum(
        jnp.einsum("tse,sde->td", triple_gathered, projector, preferred_element_type=jnp.float32)
    )
    stretch_delta = jnp.sum(grad_one * standard_one, axis=0)
    lifting_delta = jnp.sum(grad_one, axis=0)
    tokens_delta = grad_resid + norm_backward(grad_one, standard_one, recip_one, stretch)
    summed_grads = (
        lax.psum(projector_delta.astype(jnp.bfloat16), "dp").astype(jnp.float32),
        lax.psum(offsets_delta.astype(jnp.bfloat16), "dp").astype(jnp.float32),
        lax.psum(combiner_delta.astype(jnp.bfloat16), "dp").astype(jnp.float32),
        lax.psum(baseline_delta.astype(jnp.bfloat16), "dp").astype(jnp.float32),
        lax.psum(widener_delta.astype(jnp.bfloat16), "dp").astype(jnp.float32),
        lax.psum(thresholds_delta.astype(jnp.bfloat16), "dp").astype(jnp.float32),
        lax.psum(narrower_delta.astype(jnp.bfloat16), "dp").astype(jnp.float32),
        lax.psum(residue_delta.astype(jnp.bfloat16), "dp").astype(jnp.float32),
        lax.psum(stretch_delta.astype(jnp.bfloat16), "dp").astype(jnp.float32),
        lax.psum(lifting_delta.astype(jnp.bfloat16), "dp").astype(jnp.float32),
        lax.psum(dilation_delta.astype(jnp.bfloat16), "dp").astype(jnp.float32),
        lax.psum(elevation_delta.astype(jnp.bfloat16), "dp").astype(jnp.float32),
    )
    return (
        layer_output,
        tokens_delta,
        summed_grads[0],
        summed_grads[1],
        summed_grads[2],
        summed_grads[3],
        summed_grads[4],
        summed_grads[5],
        summed_grads[6],
        summed_grads[7],
        summed_grads[8],
        summed_grads[9],
        summed_grads[10],
        summed_grads[11],
    )


def solution(mesh):
    return jax.shard_map(
        per_device,
        mesh=mesh,
        in_specs=(
            P("dp", ("row", "col")),
            P(None, "row", "col"),
            P(None, "col"),
            P("col", "row"),
            P(("row", "col")),
            P("row", "col"),
            P("col"),
            P("col", "row"),
            P(("row", "col")),
            P(("row", "col")),
            P(("row", "col")),
            P(("row", "col")),
            P(("row", "col")),
            P("dp", ("row", "col")),
        ),
        out_specs=(
            P("dp", ("row", "col")),
            P("dp", ("row", "col")),
            P(None, "row", "col"),
            P(None, "col"),
            P("col", "row"),
            P(("row", "col")),
            P("row", "col"),
            P("col"),
            P("col", "row"),
            P(("row", "col")),
            P(("row", "col")),
            P(("row", "col")),
            P(("row", "col")),
            P(("row", "col")),
        ),
        check_vma=False,
    )
```

profile of v0, /device:TPU:0, one launch (start us, length us, event | category | flops | bytes accessed | tf_op | source)
XLA Modules:
  0.0 1539.6 jit_solution(6490173316681552587)
XLA Ops:
  9.0 25.5 %all-reduce.10 = (f32[2308]{0:T(1024)S(1)}, f32[2308]{0:T(1024)S(1)}) all-reduce(f32[2308]{0:T(1024)S(1)} %get-tuple-element.112, f32[2308]{0:T(1024)S(1)} %get-tuple-element.111), channel_id=1, replica_groups=mesh['dp'=4,'row'=4,'col'=2] {'row','col'}, use_global_device_ids=true, to_apply=%region_3.0 | all-reduce | flops 4616 | bytes 36928 | tf_op jit(solution)/shard_map/psum | solution.py:16
  38.2 8.6 all-gather.13.cloned.1.call-done
  46.9 8.8 fusion.46
  57.7 277.3 %all-reduce.16.cloned.1.call-done = f32[2308,1536]{0,1:T(8,128)} async-done(((f32[2308,1536]{0,1:T(8,128)}), f32[2308,1536]{0,1:T(8,128)}) %all-reduce.16.cloned.1.call-update) | async-done | bytes 14180368
  354.5 37.3 %all-gather.21.cloned.1.call-done = bf16[4,577,512]{2,1,0:T(8,128)(2,1)} async-done(((bf16[1,577,512]{2,1,0:T(8,128)(2,1)}), bf16[4,577,512]{2,1,0:T(8,128)(2,1)}) %all-gather.21.cloned.1.call-update) | async-done | bytes 2363408 | tf_op jit(solution)/shard_map/all_gather | solution.py:119
  402.4 11.4 fusion.61
  418.3 24.7 %all-reduce.9 = (f32[2308]{0:T(1024)S(1)}, f32[2308]{0:T(1024)S(1)}) all-reduce(f32[2308]{0:T(1024)S(1)} %get-tuple-element.110, f32[2308]{0:T(1024)S(1)} %get-tuple-element.109), channel_id=1, replica_groups=mesh['dp'=4,'row'=4,'col'=2] {'row','col'}, use_global_device_ids=true, to_apply=%region_11.12 | all-reduce | flops 4616 | bytes 36928 | tf_op jit(solution)/shard_map/psum | solution.py:16
  446.2 186.9 %fusion.1 = f32[592,2048]{1,0:T(8,128)} fusion(f32[2308,2048]{1,0:T(8,128)} %fusion.61), kind=kCustom, calls=%all-reduce-scatter.1 | all-reduce-scatter fusion | flops 4849665 | bytes 23757312
  638.1 9.1 fusion.59
  647.3 187.2 %fusion = f32[592,2048]{1,0:T(8,128)} fusion(f32[2308,2048]{1,0:T(8,128)} %fusion.59), kind=kCustom, calls=%all-reduce-scatter | all-reduce-scatter fusion | flops 4849665 | bytes 23757312
  840.1 14.4 concatenate.1
  854.5 14.5 concatenate
  869.1 6.7 fusion.14
  876.8 95.9 %all-gather.25.cloned.1.call-done = bf16[4,577,2048]{2,1,0:T(8,128)(2,1)} async-done(((bf16[1,577,2048]{2,1,0:T(8,128)(2,1)}), bf16[4,577,2048]{2,1,0:T(8,128)(2,1)}) %all-gather.25.cloned.1.call-update) | async-done | bytes 9453584 | tf_op jit(solution)/shard_map/all_gather | solution.py:152
  972.7 10.5 reshape.108
  983.2 9.0 fusion.62
  992.3 79.8 %all-gather.23.cloned.1.call-done = bf16[4,577,2048]{2,1,0:T(8,128)(2,1)} async-done(((bf16[1,577,2048]{2,1,0:T(8,128)(2,1)}), bf16[4,577,2048]{2,1,0:T(8,128)(2,1)}) %all-gather.23.cloned.1.call-update) | async-done | bytes 9453584 | tf_op jit(solution)/shard_map/all_gather | solution.py:134
  1072.1 10.2 reshape.106
  1082.3 7.6 fusion.60
  1093.0 22.9 %all-reduce.8 = (f32[2308]{0:T(1024)S(1)}, f32[2308]{0:T(1024)S(1)}) all-reduce(f32[2308]{0:T(1024)S(1)} %get-tuple-element.102, f32[2308]{0:T(1024)S(1)} %get-tuple-element.106), channel_id=1, replica_groups=mesh['dp'=4,'row'=4,'col'=2] {'row','col'}, use_global_device_ids=true, to_apply=%region_19.20 | all-reduce | flops 4616 | bytes 36928 | tf_op jit(solution)/shard_map/psum | solution.py:16
  1122.9 8.9 all-gather.19.cloned.1.call-done
  1136.0 63.2 %fusion.2 = f32[592,512]{1,0:T(8,128)} fusion(f32[2308,512]{1,0:T(8,128)} %fusion.63), kind=kCustom, calls=%all-reduce-scatter.2 | all-reduce-scatter fusion | flops 1212417 | bytes 5939712
  1219.7 8.5 multiply_reduce_fusion
  1242.6 8.0 convolution_convert_fusion.1
  1250.7 8.5 convolution_convert_fusion
  1260.8 61.1 %all-gather.27.cloned.1.call-done = bf16[4,577,1536]{2,1,0:T(8,128)(2,1)} async-done(((bf16[1,577,1536]{2,1,0:T(8,128)(2,1)}), bf16[4,577,1536]{2,1,0:T(8,128)(2,1)}) %all-gather.27.cloned.1.call-update) | async-done | bytes 7090192 | tf_op jit(solution)/shard_map/all_gather | solution.py:188
  1321.9 9.7 reshape.116
  1331.6 15.8 %copy.63 = bf16[2308,3,512]{0,2,1:T(8,128)(2,1)} copy(bf16[2308,3,512]{2,1,0:T(4,128)(2,1)} %reshape.116) | data formatting | bytes 14180352 | tf_op jit(solution)/shard_map/reshape | solution.py:190
  1354.7 6.7 convolution_bitcast_fusion
  1371.2 104.7 %all-reduce.18.cloned.1.call-done = (bf16[3,256,512]{1,2,0:T(8,128)(2,1)}, bf16[512,256]{1,0:T(8,128)(2,1)}, bf16[256,2048]{1,0:T(8,128)(2,1)}, bf16[2048,256]{1,0:T(8,128)(2,1)}) async-done(((bf16[3,256,512]{1,2,0:T(8,128)(2,1)}, bf16[512,256]{1,0:T(8,128)(2,1)}, bf16[256,2048]{1,0:T(8,128)(2,1)}, bf16[2048,256]{1,0:T(8,128)(2,1)}), (bf16[3,256,512]{1,2,0:T(8,128)(2,1)}, bf16[512,256]{1,0:T(8,128)(2,1)}, ...) | async-done | bytes 3145744 | tf_op jit(solution)/shard_map/psum | solution.py:203
  1489.6 12.3 all-reduce.11
  1506.2 22.5 %all-reduce.7 = (f32[2308]{0:T(1024)S(1)}, f32[2308]{0:T(1024)S(1)}) all-reduce(f32[2308]{0:T(1024)S(1)} %get-tuple-element.104, f32[2308]{0:T(1024)S(1)} %get-tuple-element.105), channel_id=1, replica_groups=mesh['dp'=4,'row'=4,'col'=2] {'row','col'}, use_global_device_ids=true, to_apply=%region_26.27 | all-reduce | flops 4616 | bytes 36928 | tf_op jit(solution)/shard_map/psum | solution.py:16
  (167 shorter events, 145.6 us)
Async XLA Ops:
  7.2 630.9 %copy-start = (bf16[256,2048]{1,0:T(8,128)(2,1)S(1)}, bf16[256,2048]{1,0:T(8,128)(2,1)}, u32[]{:S(2)}) copy-start(bf16[256,2048]{1,0:T(8,128)(2,1)} %param.19) | copy-start | bytes 3145732
  7.2 39.7 %copy-start.15 = (bf16[3,256,512]{2,1,0:T(8,128)(2,1)S(1)}, bf16[3,256,512]{2,1,0:T(8,128)(2,1)}, u32[]{:S(2)}) copy-start(bf16[3,256,512]{2,1,0:T(8,128)(2,1)} %param.15) | copy-start | bytes 2359300
  7.2 39.7 %all-gather.13.cloned.1.call-start = ((), (), s32[]{:S(2)}) async-start(), calls=%async_computation.4 | async-start | bytes 1775616 | tf_op jit(solution)/shard_map/all_gather | solution.py:34
  38.2 296.8 %all-reduce.16.cloned.1.call-start = ((), (), s32[]{:S(2)}) async-start(), calls=%async_computation.16 | async-start | bytes 29884416
  55.7 336.1 %all-gather.21.cloned.1.call-start = ((), (), s32[]{:S(2)}) async-start(), calls=%async_computation.12 | async-start | bytes 2990080 | tf_op jit(solution)/shard_map/all_gather | solution.py:119
  353.9 48.5 %all-gather.17.cloned.1.call-start = ((), (), s32[]{:S(2)}) async-start(), calls=%async_computation.8 | async-start | bytes 1775616 | tf_op jit(solution)/shard_map/all_gather | solution.py:34
  354.5 61.2 %reduce-scatter.12.cloned.1.call-start = ((), (), s32[]{:S(2)}) async-start(), calls=%async_computation.5 | async-start | bytes 3551232 | tf_op jit(solution)/shard_map/reduce_scatter | solution.py:38
  397.3 18.4 %copy-start.28 = (f32[128]{0:T(128)S(1)}, f32[128]{0:T(128)}, u32[]{:S(2)}) copy-start(f32[128]{0:T(128)} %param.18) | copy-start | bytes 1540
  397.3 240.8 %all-gather.15.cloned.1.call-start = ((), (), s32[]{:S(2)}) async-start(), calls=%async_computation.6 | async-start | bytes 1775616 | tf_op jit(solution)/shard_map/all_gather | solution.py:34
  413.8 29.2 %copy-start.24 = (f32[128]{0:T(128)S(1)}, f32[128]{0:T(128)}, u32[]{:S(2)}) copy-start(f32[128]{0:T(128)} %param.25) | copy-start | bytes 1540
  413.8 29.2 %copy-start.29 = (f32[128]{0:T(128)S(1)}, f32[128]{0:T(128)}, u32[]{:S(2)}) copy-start(f32[128]{0:T(128)} %param.26) | copy-start | bytes 1540
  446.2 526.5 %all-gather.25.cloned.1.call-start = ((), (), s32[]{:S(2)}) async-start(), calls=%async_computation.14 | async-start | bytes 11960320 | tf_op jit(solution)/shard_map/all_gather | solution.py:152
  634.9 205.2 %collective-permute-start.1 = (f32[45,2048]{1,0:T(8,128)}, f32[45,2048]{1,0:T(8,128)}, u32[]{:S(2)}, u32[]{:S(2)}) collective-permute-start(f32[45,2048]{1,0:T(8,128)} %slice.44), channel_id=1, source_target_pairs={{0,2},{2,4},{4,6},{1,3},{3,5},{5,7},{8,10},{10,12},{12,14},{9,11},... | collective-permute-start | bytes 1105928
  836.2 18.3 %collective-permute-start = (f32[45,2048]{1,0:T(8,128)}, f32[45,2048]{1,0:T(8,128)}, u32[]{:S(2)}, u32[]{:S(2)}) collective-permute-start(f32[45,2048]{1,0:T(8,128)} %slice.43), channel_id=1, source_target_pairs={{0,2},{2,4},{4,6},{1,3},{3,5},{5,7},{8,10},{10,12},{12,14},{9,11},... | collective-permute-start | bytes 1105928
  854.5 14.6 copy-start.22
  875.8 196.3 %all-gather.23.cloned.1.call-start = ((), (), s32[]{:S(2)}) async-start(), calls=%async_computation.13 | async-start | bytes 11960320 | tf_op jit(solution)/shard_map/all_gather | solution.py:134
  876.6 213.4 %reduce-scatter.16.cloned.1.call-start = ((), (), s32[]{:S(2)}) async-start(), calls=%async_computation.9 | async-start | bytes 3551232 | tf_op jit(solution)/shard_map/reduce_scatter | solution.py:38
  992.3 90.0 %copy-start.13 = (bf16[2048,256]{1,0:T(8,128)(2,1)S(1)}, bf16[2048,256]{1,0:T(8,128)(2,1)}, u32[]{:S(2)}) copy-start(bf16[2048,256]{1,0:T(8,128)(2,1)} %param.21) | copy-start | bytes 3145732
  992.3 123.7 %reduce-scatter.14.cloned.1.call-start = ((), (), s32[]{:S(2)}) async-start(), calls=%async_computation.7 | async-start | bytes 3551232 | tf_op jit(solution)/shard_map/reduce_scatter | solution.py:38
  1089.9 26.0 %copy-start.8 = (bf16[2308,128]{1,0:T(8,128)(2,1)S(1)}, bf16[2308,128]{1,0:T(8,128)(2,1)}, u32[]{:S(2)}) copy-start(bf16[2308,128]{1,0:T(8,128)(2,1)} %param.27) | copy-start | bytes 1772548
  1089.9 26.1 %copy-start.27 = (f32[128]{0:T(128)S(1)}, f32[128]{0:T(128)}, u32[]{:S(2)}) copy-start(f32[128]{0:T(128)} %param.22) | copy-start | bytes 1540
  1089.9 41.9 %all-gather.19.cloned.1.call-start = ((), (), s32[]{:S(2)}) async-start(), calls=%async_computation.10 | async-start | bytes 1775616 | tf_op jit(solution)/shard_map/all_gather | solution.py:34
  1120.5 11.3 copy-start.14
  1122.4 199.4 %all-gather.27.cloned.1.call-start = ((), (), s32[]{:S(2)}) async-start(), calls=%async_computation.15 | async-start | bytes 8970240 | tf_op jit(solution)/shard_map/all_gather | solution.py:188
  1200.2 4.2 collective-permute-start.2
  1213.0 15.1 slice-start
  1213.0 15.1 slice-start.1
  1242.4 233.5 %all-reduce.18.cloned.1.call-start = ((), (), s32[]{:S(2)}) async-start(), calls=%async_computation.17 | async-start | bytes 6291456 | tf_op jit(solution)/shard_map/psum | solution.py:203
  1250.7 8.6 copy-start.5
  1331.6 15.8 %copy-start.10 = (bf16[2308,256]{1,0:T(8,128)(2,1)S(1)}, bf16[2308,256]{1,0:T(8,128)(2,1)}, u32[]{:S(2)}) copy-start(bf16[2308,256]{1,0:T(8,128)(2,1)} %all-gather.13.cloned.1.call-done) | copy-start | bytes 3545092
  1353.6 133.4 %reduce-scatter.18.cloned.1.call-start = ((), (), s32[]{:S(2)}) async-start(), calls=%async_computation.11 | async-start | bytes 3551232 | tf_op jit(solution)/shard_map/reduce_scatter | solution.py:38
  1481.9 46.8 %copy-start.4 = (f32[2308,128]{1,0:T(8,128)S(1)}, f32[2308,128]{1,0:T(8,128)}, u32[]{:S(2)}) copy-start(f32[2308,128]{1,0:T(8,128)} %copy-done.3) | copy-start | bytes 3545092
  (18 other events, 71.9 us)
Sparse Core Ops, SparseCore 0:
  38.3 8.5 all-gather.12
  55.8 279.1 all-reduce.15
  354.0 37.7 all-gather.20
  393.2 9.1 all-gather.16
  404.5 11.1 reduce-scatter.11
  446.3 8.2 all-gather.14
  875.9 96.6 all-gather.24
  974.6 97.4 all-gather.22
  1074.5 9.9 reduce-scatter.15
  1090.1 9.8 reduce-scatter.13
  1122.6 9.2 all-gather.18
  1242.5 79.3 all-gather.26
  1353.8 122.0 all-reduce.17
  1478.1 8.8 reduce-scatter.17
where the time goes:
time: 1550 us; the launch traced here: 1540 us
  waiting for transfers between devices  687 us (44%)
  blocking collectives  545 us (35%)
  matrix products  115 us (7%)
  local copies, waits for them, and re-layouts  106 us (7%)
  other arithmetic  59.1 us (4%)
  between operations  15.8 us (1%)
    unnamed x3, blocking collectives  437 us
    unnamed x18, waiting for transfers between devices  280 us
    psum x1, waiting for transfers between devices, per_device(): lax.psum(projector_delta.astype(jnp.bfloat16), 'dp').astype(jnp.float32)  105 us
    all_gather x1, waiting for transfers between devices, per_device(): expanded_all = lax.all_gather(grad_expanded, 'row', axis=0, tiled=True)  95.9 us
    psum x4, blocking collectives, feature_totals(): lax.psum((jnp.sum(left_term, axis=1), jnp.sum(right_term, axis=1)), ('row...  95.5 us
    all_gather x1, waiting for transfers between devices, per_device(): hidden_all = lax.all_gather(hidden, 'row', axis=0, tiled=True)  79.8 us
    unnamed x81, local copies, waits for them, and re-layouts  78.6 us
    all_gather x1, waiting for transfers between devices, per_device(): lax.all_gather(grad_triple.reshape(share_rows, 3 * width_col), 'row', axi...  61.1 us
  transfers between devices with their start and end apart: 17, of which 12 were waited for; matrix products, arithmetic and copies ran while one was open for 33% of the time, Pallas kernels for 0%

commit v1 on v0

v1 whole, which is shorter than its diff:
```python
import functools

import jax
import jax.numpy as jnp
from jax import lax
from jax.experimental import pallas as pl
from jax.experimental.pallas import tpu as pltpu
from jax.sharding import PartitionSpec as P

D = 1024
HD = 64
SEQ = 577
PAD = 592
RB = 4
KB = D // RB

NORM_EPSILON = 1e-05
SIGMOID_SLOPE = 1.702
F32 = jnp.float32
BF16 = jnp.bfloat16
VMEM_LIMIT = 60 * 1024 * 1024

STRETCH, LIFTING, BASELINE, DILATION, ELEVATION, RESIDUE = range(6)


def mm(a, b):
    return lax.dot_general(a, b, (((1,), (0,)), ((), ())), preferred_element_type=F32)


def mm_nt(a, b):
    return lax.dot_general(a, b, (((1,), (1,)), ((), ())), preferred_element_type=F32)


def mm_tn(a, b):
    return lax.dot_general(a, b, (((0,), (0,)), ((), ())), preferred_element_type=F32)


def sds(shape, dtype=BF16):
    return jax.ShapeDtypeStruct(shape, dtype)


def whole(shape):
    return pl.BlockSpec(shape, lambda *_: (0,) * len(shape))


def call(body, grid, in_specs, out_specs, out_shape, flops, nbytes, scratch=(), transcendentals=0):
    return pl.pallas_call(
        body,
        grid=grid,
        in_specs=in_specs,
        out_specs=out_specs,
        out_shape=out_shape,
        scratch_shapes=list(scratch),
        compiler_params=pltpu.CompilerParams(
            vmem_limit_bytes=VMEM_LIMIT, dimension_semantics=("arbitrary",) * len(grid)
        ),
        cost_estimate=pl.CostEstimate(
            flops=int(flops), bytes_accessed=int(nbytes), transcendentals=int(transcendentals)
        ),
    )


def row_mask(shape):
    return lax.broadcasted_iota(jnp.int32, shape, 0) < SEQ


def standardize(value):
    average = jnp.mean(value, axis=1, keepdims=True)
    centred = value - average
    spread = jnp.mean(centred * centred, axis=1, keepdims=True)
    reciprocal = lax.rsqrt(spread + NORM_EPSILON)
    return centred * reciprocal, reciprocal


def norm_backward(upstream, standard, reciprocal, gain):
    scaled = upstream * gain
    mean_scaled = jnp.mean(scaled, axis=1, keepdims=True)
    mean_along = jnp.mean(scaled * standard, axis=1, keepdims=True)
    return reciprocal * (scaled - mean_scaled - standard * mean_along)


def qkv_kernel(x, vec, w0, w1, w2, w3, bias, normed_t, qkv, normed):
    @pl.when(pl.program_id(0) == 0)
    def _():
        standard, _r = standardize(x[...].astype(F32))
        value = standard * vec[STRETCH : STRETCH + 1] + vec[LIFTING : LIFTING + 1]
        normed[...] = value.astype(BF16)
        normed_t[...] = value.T.astype(BF16)

    total = bias[0]
    for k, w in enumerate((w0, w1, w2, w3)):
        total = total + mm(normed[:, k * KB : (k + 1) * KB], w[0])
    qkv[...] = total.astype(BF16)


def qkv_call(x, vec, blocks, bias):
    width = blocks[0].shape[2]
    wspec = pl.BlockSpec((1, KB, width), lambda j: (j, 0, 0))
    return call(
        qkv_kernel,
        (3,),
        [whole((PAD, D)), whole(vec.shape)] + [wspec] * 4 + [pl.BlockSpec((1, 1, width), lambda j: (j, 0, 0))],
        [whole((D, PAD)), pl.BlockSpec((PAD, width), lambda j: (0, j))],
        [sds((D, PAD)), sds((PAD, 3 * width))],
        2 * PAD * D * 3 * width,
        2 * D * 3 * width + 4 * PAD * D + 6 * PAD * width,
        [pltpu.VMEM((PAD, D), BF16)],
    )(x, vec, *blocks, bias)


def head_mask(i, shape):
    lane = lax.broadcasted_iota(jnp.int32, shape, 1)
    return (lane >= i * HD) & (lane < (i + 1) * HD)


def attend_kernel(q, k, v, mixed, probs):
    queries = q[...]
    keys = k[...]
    values_t = v[...].astype(F32).T.astype(BF16)
    outs = []
    for i in range(2):
        picked = jnp.where(head_mask(i, queries.shape), queries.astype(F32) * HD ** (-0.5), 0.0)
        scores = mm_nt(keys, picked.astype(BF16))
        scores = jnp.where(row_mask(scores.shape), scores, -1e30)
        top = jnp.max(scores, axis=0, keepdims=True)
        weights = jnp.exp(scores - top)
        total = jnp.sum(weights, axis=0, keepdims=True)
        rounded = (weights * (1.0 / total)).astype(BF16)
        probs[i] = rounded
        outs.append(mm(values_t[i * HD : (i + 1) * HD], rounded))
    mixed[...] = jnp.concatenate(outs, axis=0).T.astype(BF16)


def attend_call(qkv):
    width = qkv.shape[1] // 3
    pairs = width // 128
    spec = lambda j: pl.BlockSpec((PAD, 128), lambda h, j=j: (0, j * pairs + h))
    return call(
        attend_kernel,
        (pairs,),
        [spec(0), spec(1), spec(2)],
        [pl.BlockSpec((PAD, 128), lambda h: (0, h)), pl.BlockSpec((2, PAD, PAD), lambda h: (h, 0, 0))],
        [sds((PAD, width)), sds((2 * pairs, PAD, PAD))],
        pairs * 2 * 2 * 2 * PAD * PAD * 128,
        pairs * 2 * PAD * PAD * 2,
        transcendentals=pairs * 2 * PAD * PAD,
    )(qkv, qkv, qkv)


def combine_kernel(mixed, w0, w1, w2, w3, part):
    for k, w in enumerate((w0, w1, w2, w3)):
        part[:, k * KB : (k + 1) * KB] = mm(mixed[...], w[...]).astype(BF16)


def combine_call(mixed, blocks):
    width = mixed.shape[1]
    return call(
        combine_kernel,
        (1,),
        [whole((PAD, width))] + [whole((width, KB))] * 4,
        whole((PAD, D)),
        sds((PAD, D)),
        2 * PAD * D * width,
        2 * (PAD * D + width * D + PAD * width),
    )(mixed, *blocks)


def split_lanes(value, refs):
    refs[0][...] = value[:, :KB].astype(BF16)
    for k in range(1, RB):
        for h in range(2):
            lo = k * KB + h * (KB // 2)
            refs[1 + 2 * (k - 1) + h][...] = value[:, lo : lo + KB // 2].astype(BF16)


def split_rows(value, refs, at=None):
    refs[0][...] = value[:KB].astype(BF16)
    for k in range(1, RB):
        for h in range(2):
            lo = k * KB + h * (KB // 2)
            refs[1 + 2 * (k - 1) + h][...] = value[lo : lo + KB // 2].astype(BF16)


def forward_kernel(tile, x, part, sib, vec, w0, w1, w2, w3, thresholds, cot, *rest):
    resid, normed_t, hidden, slope = rest[:4]
    deltas = rest[4:11]
    normed = rest[11]

    @pl.when(pl.program_id(0) == 0)
    def _():
        total = x[...].astype(F32) + (part[...].astype(F32) + sib[...].astype(F32)) + vec[BASELINE : BASELINE + 1]
        total = jnp.where(row_mask(total.shape), total, 0.0)
        resid[...] = total
        standard, _r = standardize(total)
        value = standard * vec[DILATION : DILATION + 1] + vec[ELEVATION : ELEVATION + 1]
        normed[...] = value.astype(BF16)
        normed_t[...] = value.T.astype(BF16)

    expanded = thresholds[...]
    for k, w in enumerate((w0, w1, w2, w3)):
        expanded = expanded + mm(normed[:, k * KB : (k + 1) * KB], w[...])
    gate = jax.nn.sigmoid(SIGMOID_SLOPE * expanded)
    active = (expanded * gate).astype(BF16)
    hidden[...] = active
    slope[...] = (gate + SIGMOID_SLOPE * expanded * gate * (1.0 - gate)).astype(BF16)
    split_lanes(mm_tn(active, cot[...]), deltas)


def forward_call(x, part, sib, vec, blocks, thresholds, cot):
    width = blocks[0].shape[1]
    tile = min(512, width)
    cols = pl.BlockSpec((PAD, tile), lambda t: (0, t))
    wspec = pl.BlockSpec((KB, tile), lambda t: (0, t))
    half = KB // 2
    return call(
        functools.partial(forward_kernel, tile),
        (width // tile,),
        [whole((PAD, D))] * 3
        + [whole(vec.shape)]
        + [wspec] * 4
        + [pl.BlockSpec((1, tile), lambda t: (0, t)), whole((PAD, D))],
        [whole((PAD, D)), whole((D, PAD)), cols, cols]
        + [pl.BlockSpec((tile, KB), lambda t: (t, 0))]
        + [pl.BlockSpec((tile, half), lambda t: (t, 0))] * 6,
        [sds((PAD, D), F32), sds((D, PAD)), sds((PAD, width)), sds((PAD, width)), sds((width, KB))]
        + [sds((width, half))] * 6,
        4 * PAD * D * width,
        4 * D * width + 14 * PAD * D + 4 * PAD * width,
        [pltpu.VMEM((PAD, D), BF16)],
        transcendentals=PAD * width,
    )(x, part, sib, vec, *blocks, thresholds, cot)


def backward_kernel(cot, n0, n1, n2, n3, slope, normed_t, w0, w1, w2, w3, *rest):
    part, thresholds_sum = rest[:2]
    deltas = rest[2:9]
    total = rest[9]
    step = pl.program_id(0)
    grad = None
    for k, n in enumerate((n0, n1, n2, n3)):
        term = mm_nt(cot[:, k * KB : (k + 1) * KB], n[...])
        grad = term if grad is None else grad + term
    grad = (grad * slope[...].astype(F32)).astype(BF16)
    thresholds_sum[...] = jnp.sum(grad.astype(F32), axis=0, keepdims=True)
    split_rows(mm(normed_t[...], grad), deltas)
    for k, w in enumerate((w0, w1, w2, w3)):
        at = slice(k * KB, (k + 1) * KB)
        term = mm_nt(grad, w[...])

        @pl.when(step == 0)
        def _():
            total[:, at] = term

        @pl.when(step > 0)
        def _():
            total[:, at] += term

    @pl.when(step == pl.num_programs(0) - 1)
    def _():
        part[...] = total[...].astype(BF16)


def backward_call(cot, narrow_blocks, slope, normed_t, wide_blocks):
    width = slope.shape[1]
    tile = min(512, width)
    half = KB // 2
    return call(
        backward_kernel,
        (width // tile,),
        [whole((PAD, D))]
        + [pl.BlockSpec((tile, KB), lambda t: (t, 0))] * 4
        + [pl.BlockSpec((PAD, tile), lambda t: (0, t)), whole((D, PAD))]
        + [pl.BlockSpec((KB, tile), lambda t: (0, t))] * 4,
        [whole((PAD, D)), pl.BlockSpec((1, tile), lambda t: (0, t)), pl.BlockSpec((KB, tile), lambda t: (0, t))]
        + [pl.BlockSpec((half, tile), lambda t: (0, t))] * 6,
        [sds((PAD, D)), sds((1, width), F32), sds((KB, width))] + [sds((half, width))] * 6,
        6 * PAD * D * width,
        6 * D * width + 6 * PAD * D + 2 * PAD * width,
        [pltpu.VMEM((PAD, D), F32)],
    )(cot, *narrow_blocks, slope, normed_t, *wide_blocks)


def narrow_kernel(hidden, n0, n1, n2, n3, part, total):
    step = pl.program_id(0)
    for k, n in enumerate((n0, n1, n2, n3)):
        at = slice(k * KB, (k + 1) * KB)
        term = mm(hidden[...], n[...])

        @pl.when(step == 0)
        def _():
            total[:, at] = term

        @pl.when(step > 0)
        def _():
            total[:, at] += term

    @pl.when(step == pl.num_programs(0) - 1)
    def _():
        part[...] = total[...].astype(BF16)


def narrow_call(hidden, blocks):
    width = hidden.shape[1]
    tile = min(512, width)
    return call(
        narrow_kernel,
        (width // tile,),
        [pl.BlockSpec((PAD, tile), lambda t: (0, t))] + [pl.BlockSpec((tile, KB), lambda t: (t, 0))] * 4,
        whole((PAD, D)),
        sds((PAD, D)),
        2 * PAD * D * width,
        2 * D * width + 2 * PAD * D + 2 * PAD * width,
        [pltpu.VMEM((PAD, D), F32)],
    )(hidden, *blocks)


def resid_kernel(part, sib, resid, cot, vec, mixed, w0, w1, w2, w3, *rest):
    grad_resid, grad_mixed, sums = rest[:3]
    deltas = rest[3:10]
    upstream = part[...].astype(F32) + sib[...].astype(F32)
    standard, reciprocal = standardize(resid[...])
    sums[0:1] = jnp.sum(upstream * standard, axis=0, keepdims=True)
    sums[1:2] = jnp.sum(upstream, axis=0, keepdims=True)
    grad = cot[...].astype(F32) + norm_backward(upstream, standard, reciprocal, vec[DILATION : DILATION + 1])
    sums[2:3] = jnp.sum(grad, axis=0, keepdims=True)
    sums[3:4] = jnp.sum(cot[...].astype(F32), axis=0, keepdims=True)
    sums[4:8] = jnp.zeros((4, D), F32)
    grad_resid[...] = grad
    rounded = grad.astype(BF16)
    total = None
    for k, w in enumerate((w0, w1, w2, w3)):
        term = mm_nt(rounded[:, k * KB : (k + 1) * KB], w[...])
        total = term if total is None else total + term
    grad_mixed[...] = total.astype(BF16)
    split_lanes(mm_tn(mixed[...], rounded), deltas)


def resid_call(part, sib, resid, cot, vec, mixed, blocks):
    width = mixed.shape[1]
    half = KB // 2
    return call(
        resid_kernel,
        (1,),
        [whole((PAD, D))] * 4 + [whole(vec.shape), whole((PAD, width))] + [whole((width, KB))] * 4,
        [whole((PAD, D)), whole((PAD, width)), whole((8, D)), whole((width, KB))] + [whole((width, half))] * 6,
        [sds((PAD, D), F32), sds((PAD, width)), sds((8, D), F32), sds((width, KB))] + [sds((width, half))] * 6,
        4 * PAD * D * width,
        14 * PAD * D + 4 * width * D + 4 * PAD * width,
    )(part, sib, resid, cot, vec, mixed, *blocks)


def attend_back_kernel(q, k, v, upstream, probs, grad_q, grad_k, grad_v):
    scaled = (q[...].astype(F32) * HD ** (-0.5)).astype(BF16)
    keys_t = (k[...].astype(F32) * HD ** (-0.5)).T.astype(BF16)
    values = v[...]
    up = upstream[...]
    grads_q = []
    kept_k = None
    kept_v = None
    for i in range(2):
        mask = head_mask(i, values.shape)
        rounded = probs[i]
        weights = rounded.astype(F32)
        picked = jnp.where(mask, values.astype(F32), 0.0).astype(BF16)
        weight_grad = mm_nt(picked, up)
        along = jnp.sum(weights * weight_grad, axis=0, keepdims=True)
        score_grad = (weights * (weight_grad - along)).astype(BF16)
        value_grad = mm(rounded, up)
        key_grad = mm(score_grad, scaled)
        kept_v = value_grad if i == 0 else jnp.where(mask, value_grad, kept_v)
        kept_k = key_grad if i == 0 else jnp.where(mask, key_grad, kept_k)
        grads_q.append(mm(keys_t[i * HD : (i + 1) * HD], score_grad))
    grad_q[...] = jnp.concatenate(grads_q, axis=0).T.astype(BF16)
    grad_k[...] = kept_k.astype(BF16)
    grad_v[...] = kept_v.astype(BF16)


def attend_back_call(qkv, upstream, probs):
    width = qkv.shape[1] // 3
    pairs = width // 128
    spec = lambda j: pl.BlockSpec((PAD, 128), lambda h, j=j: (0, j * pairs + h))
    return call(
        attend_back_kernel,
        (pairs,),
        [spec(0), spec(1), spec(2), spec(0), pl.BlockSpec((2, PAD, PAD), lambda h: (h, 0, 0))],
        [spec(0)] * 3,
        [sds((PAD, width))] * 3,
        pairs * 2 * 4 * 2 * PAD * PAD * 128,
        pairs * 2 * PAD * PAD * 2,
    )(qkv, qkv, qkv, upstream, probs)


def project_kernel(gq, gk, gv, normed_t, w0, w1, w2, w3, *rest):
    part, sums = rest[:2]
    deltas = rest[2:9]
    total = rest[9]
    step = pl.program_id(0)

    def one(g):
        grad = g[...]
        sums[0] = jnp.sum(grad.astype(F32), axis=0, keepdims=True)
        split_rows(mm(normed_t[...], grad), deltas)
        for k, w in enumerate((w0, w1, w2, w3)):
            at = slice(k * KB, (k + 1) * KB)
            term = mm_nt(grad, w[0])
            if g is gq:
                total[:, at] = term
            elif g is gk:
                total[:, at] += term
            else:
                part[:, at] = (total[:, at] + term).astype(BF16)

    for j, g in enumerate((gq, gk, gv)):
        pl.when(step == j)(lambda g=g: one(g))


def project_call(grads, normed_t, blocks):
    width = grads[0].shape[1]
    half = KB // 2
    return call(
        project_kernel,
        (3,),
        [whole((PAD, width))] * 3
        + [whole((D, PAD))]
        + [pl.BlockSpec((1, KB, width), lambda j: (j, 0, 0))] * 4,
        [whole((PAD, D)), pl.BlockSpec((1, 1, width), lambda j: (j, 0, 0)), pl.BlockSpec((KB, width), lambda j: (0, j))]
        + [pl.BlockSpec((half, width), lambda j: (0, j))] * 6,
        [sds((PAD, D)), sds((3, 1, width), F32), sds((KB, 3 * width))] + [sds((half, 3 * width))] * 6,
        4 * PAD * D * 3 * width,
        4 * D * 3 * width + 4 * PAD * D + 6 * PAD * width,
        [pltpu.VMEM((PAD, D), F32)],
    )(*grads, normed_t, *blocks)


def tokens_kernel(part, sib, x, grad_resid, cot, vec, delta, sums):
    upstream = part[...].astype(F32) + sib[...].astype(F32)
    standard, reciprocal = standardize(x[...].astype(F32))
    sums[0:1] = jnp.sum(upstream * standard, axis=0, keepdims=True)
    sums[1:2] = jnp.sum(upstream, axis=0, keepdims=True)
    sums[2:8] = jnp.zeros((6, D), F32)
    grad = grad_resid[...] + norm_backward(upstream, standard, reciprocal, vec[STRETCH : STRETCH + 1])
    delta[...] = (grad - cot[...].astype(F32)).astype(BF16)


def tokens_call(part, sib, x, grad_resid, cot, vec):
    return call(
        tokens_kernel,
        (1,),
        [whole((PAD, D))] * 5 + [whole(vec.shape)],
        [whole((PAD, D)), whole((8, D))],
        [sds((PAD, D)), sds((8, D), F32)],
        20 * PAD * D,
        14 * PAD * D,
    )(part, sib, x, grad_resid, cot, vec)


def swap(value, k):
    return lax.ppermute(value, "row", [(i, i ^ k) for i in range(RB)])


def after(value, *earlier):
    return lax.optimization_barrier((value,) + earlier)[0]


def sibling(part):
    size = lax.axis_size("col")
    if size == 2:
        return lax.ppermute(part, "col", [(0, 1), (1, 0)])
    total = None
    for s in range(1, size):
        term = lax.ppermute(part, "col", [(i, (i + s) % size) for i in range(size)]).astype(F32)
        total = term if total is None else total + term
    return total.astype(BF16)


def col_gather(value):
    size = lax.axis_size("col")
    if size == 2:
        other = lax.ppermute(value, "col", [(0, 1), (1, 0)])
        first = lax.axis_index("col") == 0
        return jnp.stack([jnp.where(first, value, other), jnp.where(first, other, value)], axis=-2)
    return lax.all_gather(value, "col", axis=value.ndim - 1)


def gather_blocks(block, axis, earlier):
    block = after(block, *earlier)
    near_x = swap(block, 1)
    near_y = swap(block, 2)
    size = block.shape[axis] // 2
    first = lax.slice_in_dim(near_x, 0, size, axis=axis)
    second = lax.slice_in_dim(near_y, size, 2 * size, axis=axis)
    far = jnp.concatenate([swap(first, 2), swap(second, 1)], axis=axis)
    return (block, near_x, near_y, far), (near_x, near_y)


def add(*terms):
    total = terms[0].astype(F32)
    for term in terms[1:]:
        total = total + term.astype(F32)
    return total.astype(terms[0].dtype)


def dp_sum(value):
    size = lax.axis_size("dp")
    if size == 1:
        return value
    if size % 2:
        return lax.psum(value, "dp")
    half = size // 2
    where = lax.axis_index("dp")
    for s in range(half - 1):
        value = add(value, lax.ppermute(value, "dp", [(s, s + 1), (size - 1 - s, size - 2 - s)]))
    value = add(value, lax.ppermute(value, "dp", [(half - 1, half), (half, half - 1)]))
    for s in reversed(range(half - 1)):
        moved = lax.ppermute(value, "dp", [(s + 1, s), (size - 2 - s, size - 1 - s)])
        value = jnp.where((where == s) | (where == size - 1 - s), moved, value)
    return value


def reduce_blocks(blocks, axis):
    own, x0, x1, y0, y1, far0, far1 = blocks
    via_x = swap(far0, 1)
    via_y = swap(far1, 2)
    half = own.shape[axis] // 2
    halves = (lax.slice_in_dim(own, 0, half, axis=axis), lax.slice_in_dim(own, half, 2 * half, axis=axis))
    first = add(halves[0], swap(x0, 1), swap(add(y0, via_x), 2))
    second = add(halves[1], swap(y1, 2), swap(add(x1, via_y), 1))
    return jnp.concatenate([dp_sum(first), dp_sum(second)], axis=axis).astype(F32)


def per_device(
    tokens,
    projector,
    offsets,
    combiner,
    baseline,
    widener,
    thresholds,
    narrower,
    residue,
    stretch,
    lifting,
    dilation,
    elevation,
    cotangent,
):
    row = lax.axis_index("row")
    columns = lax.axis_size("col")
    features = tokens.shape[1]
    width = projector.shape[2]

    def pick(stack, index):
        return lax.dynamic_index_in_dim(stack, index, 0, keepdims=False)

    def padded(value):
        return jnp.pad(value.reshape(RB, SEQ, features), ((0, 0), (0, PAD - SEQ), (0, 0)))

    def image_in(stack):
        near = jnp.stack([pick(stack, row)] + [swap(pick(stack, row ^ k), k) for k in range(1, RB)], axis=1)
        return col_gather(near).reshape(PAD, D)

    def image_out(value):
        mine = lax.dynamic_index_in_dim(
            value.reshape(PAD, RB, columns, features), lax.axis_index("col"), 2, keepdims=False
        )
        got = jnp.stack([mine[:SEQ, 0]] + [swap(mine[:SEQ, k], k) for k in range(1, RB)])
        return jnp.concatenate([pick(got, row ^ j) for j in range(RB)], axis=0)

    vectors = jnp.stack([stretch, lifting, baseline, dilation, elevation, residue, residue, residue])
    vec = jnp.stack([vectors] + [swap(vectors, k) for k in range(1, RB)], axis=1)
    vec = col_gather(vec).reshape(8, D)
    x = image_in(padded(tokens))
    project_w, sent = gather_blocks(projector, 1, (x,))
    combine_w, sent = gather_blocks(combiner, 0, sent)
    cot = image_in(padded(after(cotangent, *sent)))
    wide_w, sent = gather_blocks(widener, 0, sent)
    narrow_w, sent = gather_blocks(narrower, 0, sent)

    bias = jnp.stack([offsets[0], jnp.zeros((width,), F32), offsets[1]])[:, None]
    normed_one_t, qkv = qkv_call(x, vec, project_w, bias)
    mixed, probs = attend_call(qkv)
    part = combine_call(mixed, combine_w)
    out = forward_call(x, part, sibling(part), vec, wide_w, thresholds[None], cot)
    resid, normed_two_t, hidden, slope = out[:4]
    narrower_delta = reduce_blocks(out[4:11], 1)

    out = backward_call(cot, narrow_w, slope, normed_two_t, wide_w)
    part, thresholds_sum = out[:2]
    widener_delta = reduce_blocks(out[2:9], 0)
    out = resid_call(part, sibling(part), resid, cot, vec, mixed, combine_w)
    grad_resid, grad_mixed, sums_two = out[:3]
    combiner_delta = reduce_blocks(out[3:10], 1)
    grads = attend_back_call(qkv, grad_mixed, probs)
    out = project_call(grads, normed_one_t, project_w)
    part, grad_sums = out[:2]
    delta = reduce_blocks(out[2:9], 0)
    projector_delta = jnp.stack([delta[:, j * width : (j + 1) * width] for j in range(3)])
    delta, sums_one = tokens_call(part, sibling(part), x, grad_resid, cot, vec)
    tokens_delta = image_out(delta) + cotangent.astype(F32)

    ffn_part = narrow_call(hidden, narrow_w)
    ffn = ffn_part.astype(F32) + sibling(ffn_part).astype(F32) + vec[RESIDUE]
    layer_output = image_out((ffn + (resid - x.astype(F32))).astype(BF16)) + tokens.astype(F32)

    featured = jnp.concatenate([sums_one[:2], sums_two[:4]]).reshape(6, RB, columns, features)
    featured = lax.dynamic_index_in_dim(featured, lax.axis_index("col"), 2, keepdims=False)
    shared = jnp.concatenate([grad_sums[0, 0], grad_sums[2, 0], thresholds_sum[0]])
    pack = [jnp.concatenate([featured[:, k].reshape(-1), shared]) for k in range(RB)]
    small = dp_sum(add(pack[0], *[swap(pack[k], k) for k in range(1, RB)]))
    count = 6 * features
    vector = small[:count].reshape(6, features)
    offsets_delta = small[count : count + 2 * width].reshape(2, width)
    thresholds_delta = small[count + 2 * width :]
    return (
        layer_output,
        tokens_delta,
        projector_delta,
        offsets_delta,
        combiner_delta,
        vector[4],
        widener_delta,
        thresholds_delta,
        narrower_delta,
        vector[5],
        vector[0],
        vector[1],
        vector[2],
        vector[3],
    )


def solution(mesh):
    features = P(("row", "col"))
    specs = {
        "tokens": P("dp", ("row", "col")),
        "projector": P(None, "row", "col"),
        "offsets": P(None, "col"),
        "combiner": P("col", "row"),
        "baseline": features,
        "widener": P("row", "col"),
        "thresholds": P("col"),
        "narrower": P("col", "row"),
        "residue": features,
        "stretch": features,
        "lifting": features,
        "dilation": features,
        "elevation": features,
    }
    weights = tuple(specs.values())
    return jax.shard_map(
        per_device,
        mesh=mesh,
        in_specs=weights + (specs["tokens"],),
        out_specs=(specs["tokens"], specs["tokens"]) + weights[1:],
        check_vma=False,
    )
```

time: 1550 us -> 501 us (0.32)
  blocking collectives: 545 us -> 0 us
  waiting for transfers between devices: 687 us -> 187 us
  starting transfers between devices: 10.6 us -> 137 us
  matrix products: 115 us -> 0 us
  Pallas kernels: 0 us -> 99 us
  local copies, waits for them, and re-layouts: 106 us -> 43.9 us
  other arithmetic: 59.1 us -> 28.2 us
    unnamed x3 -> x0, blocking collectives: 437 us -> none
    all_gather x8 -> x0, waiting for transfers between devices: 296 us -> none  [the longest x1 95.9 us: per_device(): expanded_all = lax.all_gather(grad_expanded, 'row', axis=0, tiled=True)]
    unnamed x18 -> x0, waiting for transfers between devices: 280 us -> none
    ppermute x0 -> x92, waiting for transfers between devices: none -> 187 us  [the longest x58 139 us: swap(): return lax.ppermute(value, 'row', [(i, i ^ k) for i in range(RB)])]
    ppermute x0 -> x92, starting transfers between devices: none -> 137 us  [the longest x58 65 us: swap(): return lax.ppermute(value, 'row', [(i, i ^ k) for i in range(RB)])]
    dot_general x17 -> x0, matrix products: 109 us -> none  [the longest x1 11.4 us: per_device(): jnp.einsum('td,fd->tf', row_block, narrower, preferred_element_type=jnp.f...]
    psum x5 -> x0, blocking collectives: 108 us -> none  [the longest x4 95.5 us: feature_totals(): lax.psum((jnp.sum(left_term, axis=1), jnp.sum(right_term, axis=1)), ('row...]
    psum x1 -> x0, waiting for transfers between devices: 105 us -> none  [per_device(): lax.psum(projector_delta.astype(jnp.bfloat16), 'dp').astype(jnp.float32)]
  transfers between devices with their start and end apart: 17 -> 92, of which waited for: 12 -> 33; matrix products, arithmetic and copies ran while one was open for 33% -> 12% of each run, Pallas kernels for 0% -> 17%
where the time goes in v1:
time: 501 us; the launch traced here: 497 us
  waiting for transfers between devices  187 us (37%)
  starting transfers between devices  137 us (27%)
  Pallas kernels  99 us (20%)
  local copies, waits for them, and re-layouts  43.9 us (9%)
  other arithmetic  28.2 us (6%)
    ppermute x58, waiting for transfers between devices, swap(): return lax.ppermute(value, 'row', [(i, i ^ k) for i in range(RB)])  139 us
    ppermute x58, starting transfers between devices, swap(): return lax.ppermute(value, 'row', [(i, i ^ k) for i in range(RB)])  65 us
    ppermute x9, starting transfers between devices, dp_sum(): lax.ppermute(value, 'dp', [(s, s + 1), (size - 1 - s, size - 2 - s)])  52.5 us
    ppermute x9, waiting for transfers between devices, dp_sum(): lax.ppermute(value, 'dp', [(s + 1, s), (size - 2 - s, size - 1 - s)])  33.7 us
    pallas_call x1, Pallas kernels, backward_call(): call(backward_kernel, (width // tile,), [whole((PAD, D))] + [pl.BlockSpec...  19.7 us
    pallas_call x1, Pallas kernels, forward_call(): call(functools.partial(forward_kernel, tile), (width // tile,), [whole((P...  14.6 us
    convert_element_type x28, other arithmetic, add(): return total.astype(terms[0].dtype)  12.6 us
    ppermute x9, starting transfers between devices, dp_sum(): lax.ppermute(value, 'dp', [(s + 1, s), (size - 2 - s, size - 1 - s)])  11.6 us
  transfers between devices with their start and end apart: 92, of which 33 were waited for; matrix products, arithmetic and copies ran while one was open for 12% of the time, Pallas kernels for 17%

profile of v1, /device:TPU:0, one launch (start us, length us, event | category | flops | bytes accessed | tf_op | source)
XLA Modules:
  0.0 497.4 jit_solution(7562873236027838380)
XLA Ops:
  9.4 4.2 collective-permute-done.1
  25.1 14.2 %collective-permute-done.4 = f32[8,128]{1,0:T(8,128)S(1)} collective-permute-done((f32[8,128]{1,0:T(8,128)S(1)}, f32[8,128]{1,0:T(8,128)S(1)}, u32[]{:S(2)}, u32[]{:S(2)}) %collective-permute-start.4) | collective-permute-done | bytes 4128 | tf_op jit(solution)/shard_map/ppermute | solution.py:458
  55.1 4.2 collective-permute-done.10
  61.6 23.2 %collective-permute-done.14 = bf16[256,256]{1,0:T(8,128)(2,1)} collective-permute-done((bf16[256,256]{1,0:T(8,128)(2,1)}, bf16[256,256]{1,0:T(8,128)(2,1)}, u32[]{:S(2)}, u32[]{:S(2)}) %collective-permute-start.14) | collective-permute-done | bytes 131104 | tf_op jit(solution)/shard_map/ppermute | solution.py:458
  86.3 6.7 %shard_map.245 = (bf16[1024,592]{1,0:T(8,128)(2,1)}, bf16[592,1536]{1,0:T(8,128)(2,1)}) custom-call(bf16[592,1024]{1,0:T(8,128)(2,1)} %reshape.73.x, f32[8,1024]{1,0:T(8,128)} %bitcast.122, bf16[3,256,512]{2,1,0:T(8,128)(2,1)} %w0.5, bf16[3,256,512]{2,1,0:T(8,128)(2,1)} %copy-done.28, bf16[3,256,512]{2,1,0:T(8,128)(2,1)} %copy-done.29, ...), custom_call_target="tpu_custom_call" | custom-call | flops 1862270976 | bytes 7389184 | tf_op jit(solution)/shard_map/pallas_call | solution.py:99
  98.1 9.3 %shard_map.246 = (bf16[592,512]{1,0:T(8,128)(2,1)}, bf16[8,592,592]{2,1,0:T(8,128)(2,1)}) custom-call(bf16[592,1536]{1,0:T(8,128)(2,1)} %get-tuple-element.68.q.k.v, bf16[592,1536]{1,0:T(8,128)(2,1)} %get-tuple-element.68.q.k.v, bf16[592,1536]{1,0:T(8,128)(2,1)} %get-tuple-element.68.q.k.v), custom_call_target="tpu_custom_call" | custom-call | flops 1435500544 | bytes 5607424 | tf_op jit(solution)/shard_map/pallas_call | solution.py:138
  118.8 7.2 %collective-permute-done.19 = bf16[128,2048]{1,0:T(8,128)(2,1)S(1)} collective-permute-done((bf16[128,2048]{1,0:T(8,128)(2,1)S(1)}, bf16[128,2048]{1,0:T(8,128)(2,1)S(1)}, u32[]{:S(2)}, u32[]{:S(2)}) %collective-permute-start.19) | collective-permute-done | bytes 524320 | tf_op jit(solution)/shard_map/ppermute | solution.py:458
  130.1 14.6 %shard_map.248 = (f32[592,1024]{1,0:T(8,128)}, bf16[1024,592]{1,0:T(8,128)(2,1)}, bf16[592,2048]{1,0:T(8,128)(2,1)}, bf16[592,2048]{1,0:T(8,128)(2,1)}, bf16[204...) custom-call(bf16[592,1024]{1,0:T(8,128)(2,1)} %reshape.73.x, ...), custom_call_target="tpu_custom_call" | custom-call | flops 4966055936 | bytes 21725184 | tf_op jit(solution)/shard_map/pallas_call | solution.py:215
  149.6 10.2 %collective-permute-done.81 = bf16[2048,128]{1,0:T(8,128)(2,1)S(1)} collective-permute-done((bf16[2048,128]{1,0:T(8,128)(2,1)}, bf16[2048,128]{1,0:T(8,128)(2,1)S(1)}, u32[]{:S(2)}, u32[]{:S(2)}) %collective-permute-start.81) | collective-permute-done | bytes 524320 | tf_op jit(solution)/shard_map/ppermute | solution.py:458
  163.3 19.1 %collective-permute-done.25.n1 = bf16[2048,256]{1,0:T(8,128)(2,1)} collective-permute-done((bf16[2048,256]{1,0:T(8,128)(2,1)}, bf16[2048,256]{1,0:T(8,128)(2,1)}, u32[]{:S(2)}, u32[]{:S(2)}) %collective-permute-start.25) | collective-permute-done | bytes 1048608 | tf_op jit(solution)/shard_map/ppermute | solution.py:458
  187.0 6.6 %collective-permute-done.80 = bf16[2048,128]{1,0:T(8,128)(2,1)S(1)} collective-permute-done((bf16[2048,128]{1,0:T(8,128)(2,1)}, bf16[2048,128]{1,0:T(8,128)(2,1)S(1)}, u32[]{:S(2)}, u32[]{:S(2)}) %collective-permute-start.80) | collective-permute-done | bytes 524320 | tf_op jit(solution)/shard_map/ppermute | solution.py:458
  195.7 11.2 %collective-permute-done.82 = bf16[2048,128]{1,0:T(8,128)(2,1)} collective-permute-done((bf16[2048,128]{1,0:T(8,128)(2,1)S(1)}, bf16[2048,128]{1,0:T(8,128)(2,1)}, u32[]{:S(2)}, u32[]{:S(2)}) %collective-permute-start.82) | collective-permute-done | bytes 524320 | tf_op jit(solution)/shard_map/ppermute | solution.py:458
  216.9 19.7 %shard_map.250 = (bf16[592,1024]{1,0:T(8,128)(2,1)}, f32[1,2048]{1,0:T(1,128)}, bf16[256,2048]{1,0:T(8,128)(2,1)}, bf16[128,2048]{1,0:T(8,128)(2,1)}, bf16[128,2...) custom-call(bf16[592,1024]{1,0:T(8,128)(2,1)} %reshape.76.cot, ...), custom_call_target="tpu_custom_call" | custom-call | flops 7449083904 | bytes 18644992 | tf_op jit(solution)/shard_map/pallas_call | solution.py:267
  239.5 11.1 %shard_map.249 = bf16[592,1024]{1,0:T(8,128)(2,1)} custom-call(bf16[592,2048]{1,0:T(8,128)(2,1)} %get-tuple-element.73.hidden, bf16[2048,256]{1,0:T(8,128)(2,1)} %n0.1, bf16[2048,256]{1,0:T(8,128)(2,1)} %collective-permute-done.25.n1, bf16[2048,256]{1,0:T(8,128)(2,1)} %collective-permute-done.26.n2, bf16[2048,256]{1,0:T(8,128)(2,1)} %copy-done.26), custom_call_target="tpu_custom_call" | custom-call | flops 2483027968 | bytes 7831552 | tf_op jit(solution)/shard_map/pallas_call | solution.py:305
  254.2 6.3 %collective-permute-done.68 = bf16[128,2048]{1,0:T(8,128)(2,1)S(1)} collective-permute-done((bf16[128,2048]{1,0:T(8,128)(2,1)}, bf16[128,2048]{1,0:T(8,128)(2,1)S(1)}, u32[]{:S(2)}, u32[]{:S(2)}) %collective-permute-start.68) | collective-permute-done | bytes 524320 | tf_op jit(solution)/shard_map/ppermute | solution.py:458
  265.6 9.2 %collective-permute-done.76 = bf16[128,2048]{1,0:T(8,128)(2,1)S(1)} collective-permute-done((bf16[128,2048]{1,0:T(8,128)(2,1)S(1)}, bf16[128,2048]{1,0:T(8,128)(2,1)S(1)}, u32[]{:S(2)}, u32[]{:S(2)}) %collective-permute-start.76) | collective-permute-done | bytes 524320 | tf_op jit(solution)/shard_map/ppermute | solution.py:458
  278.5 7.9 %shard_map.251 = (f32[592,1024]{1,0:T(8,128)}, bf16[592,512]{1,0:T(8,128)(2,1)}, f32[8,1024]{1,0:T(8,128)}, bf16[512,256]{1,0:T(8,128)(2,1)}, bf16[512,128]{1,0:...) custom-call(bf16[592,1024]{1,0:T(8,128)(2,1)} %get-tuple-element.78., ...), custom_call_target="tpu_custom_call" | custom-call | flops 1241513984 | bytes 11796480 | tf_op jit(solution)/shard_map/pallas_call | solution.py:341
  298.8 11.4 %shard_map.252 = (bf16[592,512]{1,0:T(8,128)(2,1)}, bf16[592,512]{1,0:T(8,128)(2,1)}, bf16[592,512]{1,0:T(8,128)(2,1)}) custom-call(bf16[592,1536]{1,0:T(8,128)(2,1)} %get-tuple-element.68.q.k.v, bf16[592,1536]{1,0:T(8,128)(2,1)} %get-tuple-element.68.q.k.v, bf16[592,1536]{1,0:T(8,128)(2,1)} %get-tuple-element.68.q.k.v, ...), custom_call_target="tpu_custom_call" | custom-call | flops 2871001088 | bytes 5607424 | tf_op jit(solution)/shard_map/pallas_call | solution.py:382
  310.3 8.8 %shard_map.253 = (bf16[592,1024]{1,0:T(8,128)(2,1)}, f32[3,1,512]{2,1,0:T(1,128)}, bf16[256,1536]{1,0:T(8,128)(2,1)}, bf16[128,1536]{1,0:T(8,128)(2,1)}, bf16[12...) custom-call(bf16[592,512]{1,0:T(8,128)(2,1)} %get-tuple-element.81.g, ...), custom_call_target="tpu_custom_call" | custom-call | flops 3724541952 | bytes 10534912 | tf_op jit(solution)/shard_map/pallas_call | solution.py:420
  323.2 4.9 collective-permute-done.31
  332.3 11.2 %collective-permute-start.71 = (bf16[128,2048]{1,0:T(8,128)(2,1)S(1)}, bf16[128,2048]{1,0:T(8,128)(2,1)S(1)}, u32[]{:S(2)}, u32[]{:S(2)}) collective-permute-start(bf16[128,2048]{1,0:T(8,128)(2,1)S(1)} %copy-done.7), channel_id=1, source_target_pairs={{0,8},{24,16},{1,9},{25,17},{2,10},{26,18},{3,11},{27,19},{4,12},{... | collective-permute-start | bytes 1572872 | tf_op jit(solution)/shard_map/ppermute | solution.py:512
  353.3 6.1 %collective-permute-done.77 = bf16[128,2048]{1,0:T(8,128)(2,1)S(1)} collective-permute-done((bf16[128,2048]{1,0:T(8,128)(2,1)S(1)}, bf16[128,2048]{1,0:T(8,128)(2,1)S(1)}, u32[]{:S(2)}, u32[]{:S(2)}) %collective-permute-start.77) | collective-permute-done | bytes 524320 | tf_op jit(solution)/shard_map/ppermute | solution.py:512
  359.4 4.4 collective-permute-start.59
  366.3 4.3 collective-permute-start.65
  378.9 11.4 %collective-permute-done.61 = bf16[512,128]{1,0:T(8,128)(2,1)S(1)} collective-permute-done((bf16[512,128]{1,0:T(8,128)(2,1)S(1)}, bf16[512,128]{1,0:T(8,128)(2,1)S(1)}, u32[]{:S(2)}, u32[]{:S(2)}) %collective-permute-start.61) | collective-permute-done | bytes 131104 | tf_op jit(solution)/shard_map/ppermute | solution.py:515
  391.6 5.5 %collective-permute-done.67 = bf16[512,128]{1,0:T(8,128)(2,1)S(1)} collective-permute-done((bf16[512,128]{1,0:T(8,128)(2,1)S(1)}, bf16[512,128]{1,0:T(8,128)(2,1)S(1)}, u32[]{:S(2)}, u32[]{:S(2)}) %collective-permute-start.67) | collective-permute-done | bytes 131104 | tf_op jit(solution)/shard_map/ppermute | solution.py:515
  399.9 6.0 %collective-permute-start.41 = (bf16[128,1536]{1,0:T(8,128)(2,1)S(1)}, bf16[128,1536]{1,0:T(8,128)(2,1)S(1)}, u32[]{:S(2)}, u32[]{:S(2)}) collective-permute-start(bf16[128,1536]{1,0:T(8,128)(2,1)S(1)} %get-tuple-element.135), channel_id=1, source_target_pairs={{0,8},{24,16},{1,9},{25,17},{2,10},{26,18},{3,11},{27,19},{4,12},{... | collective-permute-start | bytes 1179656 | tf_op jit(solution)/shard_map/ppermute | solution.py:512
  409.8 6.3 %shard_map.254 = (bf16[592,1024]{1,0:T(8,128)(2,1)}, f32[8,1024]{1,0:T(8,128)}) custom-call(bf16[592,1024]{1,0:T(8,128)(2,1)} %get-tuple-element.85.part, bf16[592,1024]{1,0:T(8,128)(2,1)} %copy-done.12, bf16[592,1024]{1,0:T(8,128)(2,1)} %reshape.73.x, f32[592,1024]{1,0:T(8,128)} %get-tuple-element.86.grad_resid, bf16[592,1024]{1,0:T(8,128)(2,1)} %reshape.76.cot, ...), custom_call_target="tpu_custom_call" | custom-call | flops 12124160 | bytes 8486912 | tf_op jit(solution)/shard_map/pallas_call | solution.py:446
  425.0 18.2 %collective-permute-start.53 = (f32[3840]{0:T(1024)S(1)}, f32[3840]{0:T(1024)S(1)}, u32[]{:S(2)}, u32[]{:S(2)}) collective-permute-start(f32[3840]{0:T(1024)S(1)} %fusion.10), channel_id=1, source_target_pairs={{0,8},{24,16},{1,9},{25,17},{2,10},{26,18},{3,11},{27,19},{4,12},{... | collective-permute-start | bytes 46088 | tf_op jit(solution)/shard_map/ppermute | solution.py:512
  462.7 4.3 concatenate.55
  481.3 10.1 %collective-permute-done.43 = bf16[128,1536]{1,0:T(8,128)(2,1)S(1)} collective-permute-done((bf16[128,1536]{1,0:T(8,128)(2,1)S(1)}, bf16[128,1536]{1,0:T(8,128)(2,1)S(1)}, u32[]{:S(2)}, u32[]{:S(2)}) %collective-permute-start.43) | collective-permute-done | bytes 393248 | tf_op jit(solution)/shard_map/ppermute | solution.py:515
  491.4 4.2 collective-permute-done.49
  (369 shorter events, 193.0 us)
Async XLA Ops:
  51.0 59.6 %collective-permute-start.17 = (bf16[256,2048]{1,0:T(8,128)(2,1)}, bf16[256,2048]{1,0:T(8,128)(2,1)}, u32[]{:S(2)}, u32[]{:S(2)}) collective-permute-start(bf16[256,2048]{1,0:T(8,128)(2,1)} %w0.3), channel_id=1, source_target_pairs={{0,2},{2,0},{4,6},{6,4},{1,3},{3,1},{5,7},{7,5},{8,10},{10,8},{12,... | collective-permute-start | bytes 3145736 | tf_op jit(solution)/shard_map/ppermute | solution.py:458
  52.2 60.7 %collective-permute-start.18 = (bf16[256,2048]{1,0:T(8,128)(2,1)}, bf16[256,2048]{1,0:T(8,128)(2,1)}, u32[]{:S(2)}, u32[]{:S(2)}) collective-permute-start(bf16[256,2048]{1,0:T(8,128)(2,1)} %w0.3), channel_id=1, source_target_pairs={{0,4},{2,6},{4,0},{6,2},{1,5},{3,7},{5,1},{7,3},{8,12},{10,14},{12... | collective-permute-start | bytes 3145736 | tf_op jit(solution)/shard_map/ppermute | solution.py:458
  53.7 31.1 %collective-permute-start.14 = (bf16[256,256]{1,0:T(8,128)(2,1)}, bf16[256,256]{1,0:T(8,128)(2,1)}, u32[]{:S(2)}, u32[]{:S(2)}) collective-permute-start(bf16[256,256]{1,0:T(8,128)(2,1)} %slice.200), channel_id=1, source_target_pairs={{0,4},{2,6},{4,0},{6,2},{1,5},{3,7},{5,1},{7,3},{8,12},{10,14},{12... | collective-permute-start | bytes 393224 | tf_op jit(solution)/shard_map/ppermute | solution.py:458
  59.4 33.6 %collective-permute-start.21 = (bf16[592,128]{1,0:T(8,128)(2,1)S(1)}, bf16[592,128]{1,0:T(8,128)(2,1)S(1)}, u32[]{:S(2)}, u32[]{:S(2)}) collective-permute-start(bf16[592,128]{1,0:T(8,128)(2,1)S(1)} %get-tuple-element.154), channel_id=1, source_target_pairs={{0,2},{2,0},{4,6},{6,4},{1,3},{3,1},{5,7},{7,5},{8,10},{10,8},{12,... | collective-permute-start | bytes 454664 | tf_op jit(solution)/shard_map/ppermute | solution.py:458
  60.7 34.8 %collective-permute-start.22 = (bf16[592,128]{1,0:T(8,128)(2,1)S(1)}, bf16[592,128]{1,0:T(8,128)(2,1)S(1)}, u32[]{:S(2)}, u32[]{:S(2)}) collective-permute-start(bf16[592,128]{1,0:T(8,128)(2,1)S(1)} %get-tuple-element.155), channel_id=1, source_target_pairs={{0,4},{2,6},{4,0},{6,2},{1,5},{3,7},{5,1},{7,3},{8,12},{10,14},{12... | collective-permute-start | bytes 454664 | tf_op jit(solution)/shard_map/ppermute | solution.py:458
  145.6 36.8 %collective-permute-start.25 = (bf16[2048,256]{1,0:T(8,128)(2,1)}, bf16[2048,256]{1,0:T(8,128)(2,1)}, u32[]{:S(2)}, u32[]{:S(2)}) collective-permute-start(bf16[2048,256]{1,0:T(8,128)(2,1)} %n0.1), channel_id=1, source_target_pairs={{0,2},{2,0},{4,6},{6,4},{1,3},{3,1},{5,7},{7,5},{8,10},{10,8},{12,... | collective-permute-start | bytes 3145736 | tf_op jit(solution)/shard_map/ppermute | solution.py:458
  147.6 36.8 %collective-permute-start.26 = (bf16[2048,256]{1,0:T(8,128)(2,1)}, bf16[2048,256]{1,0:T(8,128)(2,1)}, u32[]{:S(2)}, u32[]{:S(2)}) collective-permute-start(bf16[2048,256]{1,0:T(8,128)(2,1)} %n0.1), channel_id=1, source_target_pairs={{0,4},{2,6},{4,0},{6,2},{1,5},{3,7},{5,1},{7,3},{8,12},{10,14},{12... | collective-permute-start | bytes 3145736 | tf_op jit(solution)/shard_map/ppermute | solution.py:458
  148.8 44.7 %collective-permute-start.80 = (bf16[2048,128]{1,0:T(8,128)(2,1)}, bf16[2048,128]{1,0:T(8,128)(2,1)S(1)}, u32[]{:S(2)}, u32[]{:S(2)}) collective-permute-start(bf16[2048,128]{1,0:T(8,128)(2,1)} %get-tuple-element.114), channel_id=1, source_target_pairs={{0,2},{2,0},{4,6},{6,4},{1,3},{3,1},{5,7},{7,5},{8,10},{10,8},{12,... | collective-permute-start | bytes 1572872 | tf_op jit(solution)/shard_map/ppermute | solution.py:458
  159.8 35.8 %collective-permute-start.86 = (bf16[2048,128]{1,0:T(8,128)(2,1)}, bf16[2048,128]{1,0:T(8,128)(2,1)}, u32[]{:S(2)}, u32[]{:S(2)}) collective-permute-start(bf16[2048,128]{1,0:T(8,128)(2,1)} %get-tuple-element.117), channel_id=1, source_target_pairs={{0,4},{2,6},{4,0},{6,2},{1,5},{3,7},{5,1},{7,3},{8,12},{10,14},{12... | collective-permute-start | bytes 1572872 | tf_op jit(solution)/shard_map/ppermute | solution.py:458
  161.9 45.0 %collective-permute-start.82 = (bf16[2048,128]{1,0:T(8,128)(2,1)S(1)}, bf16[2048,128]{1,0:T(8,128)(2,1)}, u32[]{:S(2)}, u32[]{:S(2)}) collective-permute-start(bf16[2048,128]{1,0:T(8,128)(2,1)S(1)} %add_convert_fusion.8), channel_id=1, source_target_pairs={{0,4},{2,6},{4,0},{6,2},{1,5},{3,7},{5,1},{7,3},{8,12},{10,14},{12... | collective-permute-start | bytes 1572872 | tf_op jit(solution)/shard_map/ppermute | solution.py:458
  182.4 24.5 %collective-permute-start.88 = (bf16[2048,128]{1,0:T(8,128)(2,1)S(1)}, bf16[2048,128]{1,0:T(8,128)(2,1)}, u32[]{:S(2)}, u32[]{:S(2)}) collective-permute-start(bf16[2048,128]{1,0:T(8,128)(2,1)S(1)} %add_convert_fusion.4), channel_id=1, source_target_pairs={{0,2},{2,0},{4,6},{6,4},{1,3},{3,1},{5,7},{7,5},{8,10},{10,8},{12,... | collective-permute-start | bytes 1572872 | tf_op jit(solution)/shard_map/ppermute | solution.py:458
  184.4 31.4 %collective-permute-start.27 = (bf16[1024,256]{1,0:T(8,128)(2,1)S(1)}, bf16[1024,256]{1,0:T(8,128)(2,1)S(1)}, u32[]{:S(2)}, u32[]{:S(2)}) collective-permute-start(bf16[1024,256]{1,0:T(8,128)(2,1)S(1)} %slice.204), channel_id=1, source_target_pairs={{0,4},{2,6},{4,0},{6,2},{1,5},{3,7},{5,1},{7,3},{8,12},{10,14},{12... | collective-permute-start | bytes 1572872 | tf_op jit(solution)/shard_map/ppermute | solution.py:458
  193.5 22.4 %collective-permute-start.28 = (bf16[1024,256]{1,0:T(8,128)(2,1)S(1)}, bf16[1024,256]{1,0:T(8,128)(2,1)S(1)}, u32[]{:S(2)}, u32[]{:S(2)}) collective-permute-start(bf16[1024,256]{1,0:T(8,128)(2,1)S(1)} %slice.205), channel_id=1, source_target_pairs={{0,2},{2,0},{4,6},{6,4},{1,3},{3,1},{5,7},{7,5},{8,10},{10,8},{12,... | collective-permute-start | bytes 1572872 | tf_op jit(solution)/shard_map/ppermute | solution.py:458
  208.7 41.9 %collective-permute-start.83 = (bf16[2048,128]{1,0:T(8,128)(2,1)S(1)}, bf16[2048,128]{1,0:T(8,128)(2,1)S(1)}, u32[]{:S(2)}, u32[]{:S(2)}) collective-permute-start(bf16[2048,128]{1,0:T(8,128)(2,1)S(1)} %get-tuple-element.131), channel_id=1, source_target_pairs={{0,8},{24,16},{1,9},{25,17},{2,10},{26,18},{3,11},{27,19},{4,12},{... | collective-permute-start | bytes 1572872 | tf_op jit(solution)/shard_map/ppermute | solution.py:512
  212.2 39.8 %collective-permute-start.89 = (bf16[2048,128]{1,0:T(8,128)(2,1)S(1)}, bf16[2048,128]{1,0:T(8,128)(2,1)S(1)}, u32[]{:S(2)}, u32[]{:S(2)}) collective-permute-start(bf16[2048,128]{1,0:T(8,128)(2,1)S(1)} %get-tuple-element.132), channel_id=1, source_target_pairs={{0,8},{24,16},{1,9},{25,17},{2,10},{26,18},{3,11},{27,19},{4,12},{... | collective-permute-start | bytes 1572872 | tf_op jit(solution)/shard_map/ppermute | solution.py:512
  253.9 23.6 %collective-permute-start.33 = (bf16[592,1024]{1,0:T(8,128)(2,1)S(1)}, bf16[592,1024]{1,0:T(8,128)(2,1)S(1)}, u32[]{:S(2)}, u32[]{:S(2)}) collective-permute-start(bf16[592,1024]{1,0:T(8,128)(2,1)S(1)} %copy-done.13), channel_id=1, source_target_pairs={{0,1},{1,0},{2,3},{3,2},{4,5},{5,4},{6,7},{7,6},{8,9},{9,8},{10,11... | collective-permute-start | bytes 3637256 | tf_op jit(solution)/shard_map/ppermute | solution.py:468
  260.4 28.6 %collective-permute-start.29 = (bf16[592,1024]{1,0:T(8,128)(2,1)}, bf16[592,1024]{1,0:T(8,128)(2,1)}, u32[]{:S(2)}, u32[]{:S(2)}) collective-permute-start(bf16[592,1024]{1,0:T(8,128)(2,1)} %shard_map.249), channel_id=1, source_target_pairs={{0,1},{1,0},{2,3},{3,2},{4,5},{5,4},{6,7},{7,6},{8,9},{9,8},{10,11... | collective-permute-start | bytes 3637256 | tf_op jit(solution)/shard_map/ppermute | solution.py:468
  264.3 82.7 %collective-permute-start.85 = (bf16[2048,128]{1,0:T(8,128)(2,1)}, bf16[2048,128]{1,0:T(8,128)(2,1)}, u32[]{:S(2)}, u32[]{:S(2)}) collective-permute-start(bf16[2048,128]{1,0:T(8,128)(2,1)} %add_convert_fusion.5), channel_id=1, source_target_pairs={{8,0},{16,24},{9,1},{17,25},{10,2},{18,26},{11,3},{19,27},{12,4},{... | collective-permute-start | bytes 1572872 | tf_op jit(solution)/shard_map/ppermute | solution.py:515
  286.4 32.8 %collective-permute-start.63 = (bf16[512,128]{1,0:T(8,128)(2,1)}, bf16[512,128]{1,0:T(8,128)(2,1)S(1)}, u32[]{:S(2)}, u32[]{:S(2)}) collective-permute-start(bf16[512,128]{1,0:T(8,128)(2,1)} %get-tuple-element.105), channel_id=1, source_target_pairs={{0,4},{2,6},{4,0},{6,2},{1,5},{3,7},{5,1},{7,3},{8,12},{10,14},{12... | collective-permute-start | bytes 393224 | tf_op jit(solution)/shard_map/ppermute | solution.py:458
  287.0 33.1 %collective-permute-start.57 = (bf16[512,128]{1,0:T(8,128)(2,1)}, bf16[512,128]{1,0:T(8,128)(2,1)S(1)}, u32[]{:S(2)}, u32[]{:S(2)}) collective-permute-start(bf16[512,128]{1,0:T(8,128)(2,1)} %get-tuple-element.102), channel_id=1, source_target_pairs={{0,2},{2,0},{4,6},{6,4},{1,3},{3,1},{5,7},{7,5},{8,10},{10,8},{12,... | collective-permute-start | bytes 393224 | tf_op jit(solution)/shard_map/ppermute | solution.py:458
  288.2 42.8 %collective-permute-start.56 = (bf16[512,128]{1,0:T(8,128)(2,1)}, bf16[512,128]{1,0:T(8,128)(2,1)S(1)}, u32[]{:S(2)}, u32[]{:S(2)}) collective-permute-start(bf16[512,128]{1,0:T(8,128)(2,1)} %get-tuple-element.100), channel_id=1, source_target_pairs={{0,2},{2,0},{4,6},{6,4},{1,3},{3,1},{5,7},{7,5},{8,10},{10,8},{12,... | collective-permute-start | bytes 393224 | tf_op jit(solution)/shard_map/ppermute | solution.py:458
  297.6 24.1 %collective-permute-start.30 = (bf16[577,128]{1,0:T(8,128)(2,1)S(1)}, bf16[577,128]{1,0:T(8,128)(2,1)S(1)}, u32[]{:S(2)}, u32[]{:S(2)}) collective-permute-start(bf16[577,128]{1,0:T(8,128)(2,1)S(1)} %get-tuple-element.144), channel_id=1, source_target_pairs={{0,2},{2,0},{4,6},{6,4},{1,3},{3,1},{5,7},{7,5},{8,10},{10,8},{12,... | collective-permute-start | bytes 443144 | tf_op jit(solution)/shard_map/ppermute | solution.py:458
  345.8 28.1 %collective-permute-start.45 = (bf16[128,1536]{1,0:T(8,128)(2,1)}, bf16[128,1536]{1,0:T(8,128)(2,1)S(1)}, u32[]{:S(2)}, u32[]{:S(2)}) collective-permute-start(bf16[128,1536]{1,0:T(8,128)(2,1)} %get-tuple-element.94), channel_id=1, source_target_pairs={{0,4},{2,6},{4,0},{6,2},{1,5},{3,7},{5,1},{7,3},{8,12},{10,14},{12... | collective-permute-start | bytes 1179656 | tf_op jit(solution)/shard_map/ppermute | solution.py:458
  347.1 27.6 %collective-permute-start.39 = (bf16[128,1536]{1,0:T(8,128)(2,1)S(1)}, bf16[128,1536]{1,0:T(8,128)(2,1)S(1)}, u32[]{:S(2)}, u32[]{:S(2)}) collective-permute-start(bf16[128,1536]{1,0:T(8,128)(2,1)S(1)} %copy-done.44), channel_id=1, source_target_pairs={{0,2},{2,0},{4,6},{6,4},{1,3},{3,1},{5,7},{7,5},{8,10},{10,8},{12,... | collective-permute-start | bytes 1179656 | tf_op jit(solution)/shard_map/ppermute | solution.py:458
  349.3 48.7 %collective-permute-start.38 = (bf16[128,1536]{1,0:T(8,128)(2,1)S(1)}, bf16[128,1536]{1,0:T(8,128)(2,1)S(1)}, u32[]{:S(2)}, u32[]{:S(2)}) collective-permute-start(bf16[128,1536]{1,0:T(8,128)(2,1)S(1)} %copy-done.43), channel_id=1, source_target_pairs={{0,2},{2,0},{4,6},{6,4},{1,3},{3,1},{5,7},{7,5},{8,10},{10,8},{12,... | collective-permute-start | bytes 1179656 | tf_op jit(solution)/shard_map/ppermute | solution.py:458
  352.4 46.2 %collective-permute-start.44 = (bf16[128,1536]{1,0:T(8,128)(2,1)S(1)}, bf16[128,1536]{1,0:T(8,128)(2,1)S(1)}, u32[]{:S(2)}, u32[]{:S(2)}) collective-permute-start(bf16[128,1536]{1,0:T(8,128)(2,1)S(1)} %copy-done.42), channel_id=1, source_target_pairs={{0,4},{2,6},{4,0},{6,2},{1,5},{3,7},{5,1},{7,3},{8,12},{10,14},{12... | collective-permute-start | bytes 1179656 | tf_op jit(solution)/shard_map/ppermute | solution.py:458
  374.7 24.9 %collective-permute-start.46 = (bf16[128,1536]{1,0:T(8,128)(2,1)S(1)}, bf16[128,1536]{1,0:T(8,128)(2,1)S(1)}, u32[]{:S(2)}, u32[]{:S(2)}) collective-permute-start(bf16[128,1536]{1,0:T(8,128)(2,1)S(1)} %add_convert_fusion.20), channel_id=1, source_target_pairs={{0,2},{2,0},{4,6},{6,4},{1,3},{3,1},{5,7},{7,5},{8,10},{10,8},{12,... | collective-permute-start | bytes 1179656 | tf_op jit(solution)/shard_map/ppermute | solution.py:458
  375.7 23.9 %collective-permute-start.40 = (bf16[128,1536]{1,0:T(8,128)(2,1)S(1)}, bf16[128,1536]{1,0:T(8,128)(2,1)S(1)}, u32[]{:S(2)}, u32[]{:S(2)}) collective-permute-start(bf16[128,1536]{1,0:T(8,128)(2,1)S(1)} %add_convert_fusion.24), channel_id=1, source_target_pairs={{0,4},{2,6},{4,0},{6,2},{1,5},{3,7},{5,1},{7,3},{8,12},{10,14},{12... | collective-permute-start | bytes 1179656 | tf_op jit(solution)/shard_map/ppermute | solution.py:458
  405.9 37.4 %collective-permute-start.47 = (bf16[128,1536]{1,0:T(8,128)(2,1)S(1)}, bf16[128,1536]{1,0:T(8,128)(2,1)S(1)}, u32[]{:S(2)}, u32[]{:S(2)}) collective-permute-start(bf16[128,1536]{1,0:T(8,128)(2,1)S(1)} %get-tuple-element.136), channel_id=1, source_target_pairs={{0,8},{24,16},{1,9},{25,17},{2,10},{26,18},{3,11},{27,19},{4,12},{... | collective-permute-start | bytes 1179656 | tf_op jit(solution)/shard_map/ppermute | solution.py:512
  407.3 65.2 %collective-permute-start.73 = (bf16[128,2048]{1,0:T(8,128)(2,1)S(1)}, bf16[128,2048]{1,0:T(8,128)(2,1)}, u32[]{:S(2)}, u32[]{:S(2)}) collective-permute-start(bf16[128,2048]{1,0:T(8,128)(2,1)S(1)} %add_convert_fusion.13), channel_id=1, source_target_pairs={{8,0},{16,24},{9,1},{17,25},{10,2},{18,26},{11,3},{19,27},{12,4},{... | collective-permute-start | bytes 1572872 | tf_op jit(solution)/shard_map/ppermute | solution.py:515
  422.5 51.2 %collective-permute-start.79 = (bf16[128,2048]{1,0:T(8,128)(2,1)S(1)}, bf16[128,2048]{1,0:T(8,128)(2,1)}, u32[]{:S(2)}, u32[]{:S(2)}) collective-permute-start(bf16[128,2048]{1,0:T(8,128)(2,1)S(1)} %add_convert_fusion.9), channel_id=1, source_target_pairs={{8,0},{16,24},{9,1},{17,25},{10,2},{18,26},{11,3},{19,27},{12,4},{... | collective-permute-start | bytes 1572872 | tf_op jit(solution)/shard_map/ppermute | solution.py:515
  425.0 22.5 %collective-permute-start.53 = (f32[3840]{0:T(1024)S(1)}, f32[3840]{0:T(1024)S(1)}, u32[]{:S(2)}, u32[]{:S(2)}) collective-permute-start(f32[3840]{0:T(1024)S(1)} %fusion.10), channel_id=1, source_target_pairs={{0,8},{24,16},{1,9},{25,17},{2,10},{26,18},{3,11},{27,19},{4,12},{... | collective-permute-start | bytes 46088 | tf_op jit(solution)/shard_map/ppermute | solution.py:512
  (106 other events, 1231.6 us)

commit v2 on v1

v2 whole, which is shorter than its diff:
```python
import jax
import jax.numpy as jnp
from jax import lax
from jax.experimental import pallas as pl
from jax.experimental.pallas import tpu as pltpu
from jax.sharding import PartitionSpec as P

D = 1024
HD = 64
SEQ = 577
PAD = 592
RB = 4
KB = D // RB

NORM_EPSILON = 1e-05
SIGMOID_SLOPE = 1.702
F32 = jnp.float32
BF16 = jnp.bfloat16
VMEM_LIMIT = 60 * 1024 * 1024
SHRINK = 64
DEPTH = 2

STRETCH, LIFTING, BASELINE, DILATION, ELEVATION, RESIDUE = range(6)


def mm(a, b):
    return lax.dot_general(a, b, (((1,), (0,)), ((), ())), preferred_element_type=F32)


def mm_nt(a, b):
    return lax.dot_general(a, b, (((1,), (1,)), ((), ())), preferred_element_type=F32)


def mm_tn(a, b):
    return lax.dot_general(a, b, (((0,), (0,)), ((), ())), preferred_element_type=F32)


def sds(shape, dtype=BF16):
    return jax.ShapeDtypeStruct(shape, dtype)


def whole(shape):
    return pl.BlockSpec(shape, lambda *_: (0,) * len(shape))


def call(body, grid, in_specs, out_specs, out_shape, flops, nbytes, scratch=(), transcendentals=0):
    return pl.pallas_call(
        body,
        grid=grid,
        in_specs=in_specs,
        out_specs=out_specs,
        out_shape=out_shape,
        scratch_shapes=list(scratch),
        compiler_params=pltpu.CompilerParams(
            vmem_limit_bytes=VMEM_LIMIT, dimension_semantics=("arbitrary",) * len(grid)
        ),
        cost_estimate=pl.CostEstimate(
            flops=int(flops) // SHRINK, bytes_accessed=int(nbytes) // SHRINK, transcendentals=int(transcendentals) // SHRINK
        ),
    )


def row_mask(shape):
    return lax.broadcasted_iota(jnp.int32, shape, 0) < SEQ


def standardize(value):
    average = jnp.mean(value, axis=1, keepdims=True)
    centred = value - average
    spread = jnp.mean(centred * centred, axis=1, keepdims=True)
    reciprocal = lax.rsqrt(spread + NORM_EPSILON)
    return centred * reciprocal, reciprocal


def norm_backward(upstream, standard, reciprocal, gain):
    scaled = upstream * gain
    mean_scaled = jnp.mean(scaled, axis=1, keepdims=True)
    mean_along = jnp.mean(scaled * standard, axis=1, keepdims=True)
    return reciprocal * (scaled - mean_scaled - standard * mean_along)


def qkv_kernel(x, vec, *rest):
    weights, (bias, normed_t, qkv, normed) = rest[:5], rest[5:]

    @pl.when(pl.program_id(0) == 0)
    def _():
        standard, _r = standardize(x[...].astype(F32))
        value = standard * vec[STRETCH : STRETCH + 1] + vec[LIFTING : LIFTING + 1]
        normed[...] = value.astype(BF16)
        normed_t[...] = value.T.astype(BF16)

    total = bias[0]
    for k, w in enumerate(joined(weights)):
        total = total + mm(normed[:, k * KB : (k + 1) * KB], w)
    qkv[...] = total.astype(BF16)


def attn_specs(width, at):
    full = pl.BlockSpec((1, KB, width), lambda j: (at(j), 0, 0))
    half = pl.BlockSpec((1, KB // 2, width), lambda j: (at(j), 0, 0))
    return [full] * 3 + [half] * 2


def joined(weights):
    blocks = [w[...].reshape(w.shape[-2:]) for w in weights]
    return blocks[:3] + [jnp.concatenate(blocks[3:], axis=0)]


def qkv_call(x, vec, blocks, bias):
    width = blocks[0].shape[2]
    return call(
        qkv_kernel,
        (3,),
        [whole((PAD, D)), whole(vec.shape)]
        + attn_specs(width, lambda j: j)
        + [pl.BlockSpec((1, 1, width), lambda j: (j, 0, 0))],
        [whole((D, PAD)), pl.BlockSpec((PAD, width), lambda j: (0, j))],
        [sds((D, PAD)), sds((PAD, 3 * width))],
        2 * PAD * D * 3 * width,
        2 * D * 3 * width + 4 * PAD * D + 6 * PAD * width,
        [pltpu.VMEM((PAD, D), BF16)],
    )(x, vec, *blocks, bias)


def head_mask(i, shape):
    lane = lax.broadcasted_iota(jnp.int32, shape, 1)
    return (lane >= i * HD) & (lane < (i + 1) * HD)


def attend_kernel(q, k, v, mixed, probs):
    queries = q[...]
    keys = k[...]
    values_t = v[...].astype(F32).T.astype(BF16)
    outs = []
    for i in range(2):
        picked = jnp.where(head_mask(i, queries.shape), queries.astype(F32) * HD ** (-0.5), 0.0)
        scores = mm_nt(keys, picked.astype(BF16))
        scores = jnp.where(row_mask(scores.shape), scores, -1e30)
        top = jnp.max(scores, axis=0, keepdims=True)
        weights = jnp.exp(scores - top)
        total = jnp.sum(weights, axis=0, keepdims=True)
        rounded = (weights * (1.0 / total)).astype(BF16)
        probs[i] = rounded
        outs.append(mm(values_t[i * HD : (i + 1) * HD], rounded))
    mixed[...] = jnp.concatenate(outs, axis=0).T.astype(BF16)


def attend_call(qkv):
    width = qkv.shape[1] // 3
    pairs = width // 128
    spec = lambda j: pl.BlockSpec((PAD, 128), lambda h, j=j: (0, j * pairs + h))
    return call(
        attend_kernel,
        (pairs,),
        [spec(0), spec(1), spec(2)],
        [pl.BlockSpec((PAD, 128), lambda h: (0, h)), pl.BlockSpec((2, PAD, PAD), lambda h: (h, 0, 0))],
        [sds((PAD, width)), sds((2 * pairs, PAD, PAD))],
        pairs * 2 * 2 * 2 * PAD * PAD * 128,
        pairs * 2 * PAD * PAD * 2,
        transcendentals=pairs * 2 * PAD * PAD,
    )(qkv, qkv, qkv)


def combine_kernel(mixed, *rest):
    part = rest[5]
    for k, w in enumerate(joined(rest[:5])):
        part[:, k * KB : (k + 1) * KB] = mm_nt(mixed[...], w).astype(BF16)


def combine_call(mixed, blocks):
    width = mixed.shape[1]
    return call(
        combine_kernel,
        (1,),
        [whole((PAD, width))] + attn_specs(width, lambda i: 3),
        whole((PAD, D)),
        sds((PAD, D)),
        2 * PAD * D * width,
        2 * (PAD * D + width * D + PAD * width),
    )(mixed, *blocks)


def split_rows(value, refs):
    own, first_x, first_y, later_x, later_y = refs
    half = KB // 2
    value = value.astype(BF16)
    own[...] = value[:KB]
    first_x[:half] = value[6 * half : 7 * half]
    first_x[half:] = value[2 * half : 3 * half]
    first_y[:half] = value[7 * half :]
    first_y[half:] = value[5 * half : 6 * half]
    later_x[...] = value[3 * half : 4 * half]
    later_y[...] = value[4 * half : 5 * half]


def delta_specs(tile, at):
    half = KB // 2
    return [pl.BlockSpec((KB, tile), at)] * 3 + [pl.BlockSpec((half, tile), at)] * 2


def delta_shapes(width):
    half = KB // 2
    return [sds((KB, width))] * 3 + [sds((half, width))] * 2


def forward_kernel(x, part, sib, vec, *rest):
    weights, (thresholds, cot), rest = rest[:5], rest[5:7], rest[7:]
    resid, normed_t, hidden, slope = rest[:4]
    deltas = rest[4:9]
    normed, cot_t = rest[9:]

    @pl.when(pl.program_id(0) == 0)
    def _():
        total = x[...].astype(F32) + (part[...].astype(F32) + sib[...].astype(F32)) + vec[BASELINE : BASELINE + 1]
        total = jnp.where(row_mask(total.shape), total, 0.0)
        resid[...] = total
        standard, _r = standardize(total)
        value = standard * vec[DILATION : DILATION + 1] + vec[ELEVATION : ELEVATION + 1]
        normed[...] = value.astype(BF16)
        normed_t[...] = value.T.astype(BF16)
        cot_t[...] = cot[...].astype(F32).T.astype(BF16)

    expanded = thresholds[...]
    for k, w in enumerate(joined(weights)):
        expanded = expanded + mm(normed[:, k * KB : (k + 1) * KB], w)
    gate = jax.nn.sigmoid(SIGMOID_SLOPE * expanded)
    active = (expanded * gate).astype(BF16)
    hidden[...] = active
    slope[...] = (gate + SIGMOID_SLOPE * expanded * gate * (1.0 - gate)).astype(BF16)
    split_rows(mm(cot_t[...], active), deltas)


def forward_call(x, part, sib, vec, blocks, thresholds, cot):
    width = blocks[0].shape[1]
    tile = min(512, width)
    cols = pl.BlockSpec((PAD, tile), lambda t: (0, t))
    half = pl.BlockSpec((KB // 2, tile), lambda t: (0, t))
    wspecs = [pl.BlockSpec((KB, tile), lambda t: (0, t))] * 3 + [half] * 2
    return call(
        forward_kernel,
        (width // tile,),
        [whole((PAD, D))] * 3
        + [whole(vec.shape)]
        + wspecs
        + [pl.BlockSpec((1, tile), lambda t: (0, t)), whole((PAD, D))],
        [whole((PAD, D)), whole((D, PAD)), cols, cols] + delta_specs(tile, lambda t: (0, t)),
        [sds((PAD, D), F32), sds((D, PAD)), sds((PAD, width)), sds((PAD, width))] + delta_shapes(width),
        4 * PAD * D * width,
        4 * D * width + 14 * PAD * D + 4 * PAD * width,
        [pltpu.VMEM((PAD, D), BF16), pltpu.VMEM((D, PAD), BF16)],
        transcendentals=PAD * width,
    )(x, part, sib, vec, *blocks, thresholds, cot)


def backward_kernel(cot, *rest):
    narrow, (slope, normed_t), wide, rest = rest[:5], rest[5:7], rest[7:12], rest[12:]
    part, thresholds_sum = rest[:2]
    deltas = rest[2:7]
    total = rest[7]
    step = pl.program_id(0)
    grad = None
    for k, n in enumerate(narrow[:3]):
        term = mm_nt(cot[:, k * KB : (k + 1) * KB], n[...])
        grad = term if grad is None else grad + term
    far = jnp.concatenate([narrow[3][...], narrow[4][...]], axis=1)
    grad = grad + mm_nt(cot[:, 3 * KB :], far)
    grad = (grad * slope[...].astype(F32)).astype(BF16)
    thresholds_sum[...] = jnp.sum(grad.astype(F32), axis=0, keepdims=True)
    split_rows(mm(normed_t[...], grad), deltas)
    for k, w in enumerate(joined(wide)):
        at = slice(k * KB, (k + 1) * KB)
        term = mm_nt(grad, w)

        @pl.when(step == 0)
        def _():
            total[:, at] = term

        @pl.when(step > 0)
        def _():
            total[:, at] += term

    @pl.when(step == pl.num_programs(0) - 1)
    def _():
        part[...] = total[...].astype(BF16)


def narrow_specs(tile):
    half = pl.BlockSpec((tile, KB // 2), lambda t: (t, 0))
    return [pl.BlockSpec((tile, KB), lambda t: (t, 0))] * 3 + [half] * 2


def backward_call(cot, narrow_blocks, slope, normed_t, wide_blocks):
    width = slope.shape[1]
    tile = min(512, width)
    return call(
        backward_kernel,
        (width // tile,),
        [whole((PAD, D))]
        + narrow_specs(tile)
        + [pl.BlockSpec((PAD, tile), lambda t: (0, t)), whole((D, PAD))]
        + [pl.BlockSpec((KB, tile), lambda t: (0, t))] * 3
        + [pl.BlockSpec((KB // 2, tile), lambda t: (0, t))] * 2,
        [whole((PAD, D)), pl.BlockSpec((1, tile), lambda t: (0, t))] + delta_specs(tile, lambda t: (0, t)),
        [sds((PAD, D)), sds((1, width), F32)] + delta_shapes(width),
        6 * PAD * D * width,
        6 * D * width + 6 * PAD * D + 2 * PAD * width,
        [pltpu.VMEM((PAD, D), F32)],
    )(cot, *narrow_blocks, slope, normed_t, *wide_blocks)


def narrow_kernel(hidden, *rest):
    weights, (part, total) = rest[:5], rest[5:]
    step = pl.program_id(0)
    blocks = [n[...] for n in weights]
    blocks = blocks[:3] + [jnp.concatenate(blocks[3:], axis=1)]
    for k, n in enumerate(blocks):
        at = slice(k * KB, (k + 1) * KB)
        term = mm(hidden[...], n)

        @pl.when(step == 0)
        def _():
            total[:, at] = term

        @pl.when(step > 0)
        def _():
            total[:, at] += term

    @pl.when(step == pl.num_programs(0) - 1)
    def _():
        part[...] = total[...].astype(BF16)


def narrow_call(hidden, blocks):
    width = hidden.shape[1]
    tile = min(512, width)
    return call(
        narrow_kernel,
        (width // tile,),
        [pl.BlockSpec((PAD, tile), lambda t: (0, t))] + narrow_specs(tile),
        whole((PAD, D)),
        sds((PAD, D)),
        2 * PAD * D * width,
        2 * D * width + 2 * PAD * D + 2 * PAD * width,
        [pltpu.VMEM((PAD, D), F32)],
    )(hidden, *blocks)


def resid_kernel(part, sib, resid, cot, vec, *rest):
    weights, (grad_resid, grad_mixed, grad_t, sums) = rest[:5], rest[5:]
    upstream = part[...].astype(F32) + sib[...].astype(F32)
    standard, reciprocal = standardize(resid[...])
    sums[0:1] = jnp.sum(upstream * standard, axis=0, keepdims=True)
    sums[1:2] = jnp.sum(upstream, axis=0, keepdims=True)
    grad = cot[...].astype(F32) + norm_backward(upstream, standard, reciprocal, vec[DILATION : DILATION + 1])
    sums[2:3] = jnp.sum(grad, axis=0, keepdims=True)
    sums[3:4] = jnp.sum(cot[...].astype(F32), axis=0, keepdims=True)
    sums[4:8] = jnp.zeros((4, D), F32)
    grad_resid[...] = grad
    rounded = grad.astype(BF16)
    total = None
    for k, w in enumerate(joined(weights)):
        term = mm(rounded[:, k * KB : (k + 1) * KB], w)
        total = term if total is None else total + term
    grad_mixed[...] = total.astype(BF16)
    grad_t[...] = grad.T.astype(BF16)


def resid_call(part, sib, resid, cot, vec, blocks):
    width = blocks[0].shape[2]
    return call(
        resid_kernel,
        (1,),
        [whole((PAD, D))] * 4 + [whole(vec.shape)] + attn_specs(width, lambda i: 3),
        [whole((PAD, D)), whole((PAD, width)), whole((D, PAD)), whole((8, D))],
        [sds((PAD, D), F32), sds((PAD, width)), sds((D, PAD)), sds((8, D), F32)],
        2 * PAD * D * width,
        16 * PAD * D + 2 * width * D + 2 * PAD * width,
    )(part, sib, resid, cot, vec, *blocks)


def attend_back_kernel(q, k, v, upstream, probs, grad_q, grad_k, grad_v):
    scaled = (q[...].astype(F32) * HD ** (-0.5)).astype(BF16)
    keys_t = (k[...].astype(F32) * HD ** (-0.5)).T.astype(BF16)
    values = v[...]
    up = upstream[...]
    grads_q = []
    kept_k = None
    kept_v = None
    for i in range(2):
        mask = head_mask(i, values.shape)
        rounded = probs[i]
        weights = rounded.astype(F32)
        picked = jnp.where(mask, values.astype(F32), 0.0).astype(BF16)
        weight_grad = mm_nt(picked, up)
        along = jnp.sum(weights * weight_grad, axis=0, keepdims=True)
        score_grad = (weights * (weight_grad - along)).astype(BF16)
        value_grad = mm(rounded, up)
        key_grad = mm(score_grad, scaled)
        kept_v = value_grad if i == 0 else jnp.where(mask, value_grad, kept_v)
        kept_k = key_grad if i == 0 else jnp.where(mask, key_grad, kept_k)
        grads_q.append(mm(keys_t[i * HD : (i + 1) * HD], score_grad))
    grad_q[...] = jnp.concatenate(grads_q, axis=0).T.astype(BF16)
    grad_k[...] = kept_k.astype(BF16)
    grad_v[...] = kept_v.astype(BF16)


def attend_back_call(qkv, upstream, probs):
    width = qkv.shape[1] // 3
    pairs = width // 128
    spec = lambda j: pl.BlockSpec((PAD, 128), lambda h, j=j: (0, j * pairs + h))
    return call(
        attend_back_kernel,
        (pairs,),
        [spec(0), spec(1), spec(2), spec(0), pl.BlockSpec((2, PAD, PAD), lambda h: (h, 0, 0))],
        [spec(0)] * 3,
        [sds((PAD, width))] * 3,
        pairs * 2 * 4 * 2 * PAD * PAD * 128,
        pairs * 2 * PAD * PAD * 2,
    )(qkv, qkv, qkv, upstream, probs)


def project_kernel(gq, gk, gv, normed_t, grad_t, mixed, *rest):
    weights, (part, sums), deltas, total = rest[:5], rest[5:7], rest[7:12], rest[12]
    step = pl.program_id(0)

    def one(j, g):
        grad = g[...]
        sums[0] = jnp.sum(grad.astype(F32), axis=0, keepdims=True)
        split_rows(mm(normed_t[...], grad), deltas)
        for k, w in enumerate(joined(weights)):
            at = slice(k * KB, (k + 1) * KB)
            term = mm_nt(grad, w)
            if j == 0:
                total[:, at] = term
            elif j == 1:
                total[:, at] += term
            else:
                part[:, at] = (total[:, at] + term).astype(BF16)

    for j, g in enumerate((gq, gk, gv)):
        pl.when(step == j)(lambda j=j, g=g: one(j, g))

    @pl.when(step == 3)
    def _():
        split_rows(mm(grad_t[...], mixed[...]), deltas)


def project_call(grads, normed_t, grad_t, mixed, blocks):
    width = grads[0].shape[1]
    at = lambda j: jnp.minimum(j, 2)
    return call(
        project_kernel,
        (4,),
        [whole((PAD, width))] * 3 + [whole((D, PAD))] * 2 + [whole((PAD, width))] + attn_specs(width, at),
        [whole((PAD, D)), pl.BlockSpec((1, 1, width), lambda j: (at(j), 0, 0))]
        + delta_specs(width, lambda j: (0, j)),
        [sds((PAD, D)), sds((3, 1, width), F32)] + delta_shapes(4 * width),
        4 * PAD * D * 3 * width + 2 * PAD * D * width,
        4 * D * 4 * width + 6 * PAD * D + 6 * PAD * width,
        [pltpu.VMEM((PAD, D), F32)],
    )(*grads, normed_t, grad_t, mixed, *blocks)


def tokens_kernel(part, sib, x, grad_resid, cot, vec, delta, sums):
    upstream = part[...].astype(F32) + sib[...].astype(F32)
    standard, reciprocal = standardize(x[...].astype(F32))
    sums[0:1] = jnp.sum(upstream * standard, axis=0, keepdims=True)
    sums[1:2] = jnp.sum(upstream, axis=0, keepdims=True)
    sums[2:8] = jnp.zeros((6, D), F32)
    grad = grad_resid[...] + norm_backward(upstream, standard, reciprocal, vec[STRETCH : STRETCH + 1])
    delta[...] = (grad - cot[...].astype(F32)).astype(BF16)


def tokens_call(part, sib, x, grad_resid, cot, vec):
    return call(
        tokens_kernel,
        (1,),
        [whole((PAD, D))] * 5 + [whole(vec.shape)],
        [whole((PAD, D)), whole((8, D))],
        [sds((PAD, D)), sds((8, D), F32)],
        20 * PAD * D,
        14 * PAD * D,
    )(part, sib, x, grad_resid, cot, vec)


class Links:
    def __init__(self):
        self.sent = {1: [], 2: [], 3: [], "dp": []}

    def permute(self, value, axis, pairs, link):
        line = self.sent[link]
        if len(line) >= DEPTH:
            value = lax.optimization_barrier((value, line[-DEPTH]))[0]
        got = lax.ppermute(value, axis, pairs)
        line.append(got)
        return got

    def swap(self, value, k):
        return self.permute(value, "row", [(i, i ^ k) for i in range(RB)], k)

    def along(self, value, pairs):
        return self.permute(value, "dp", pairs, "dp")


def swap(value, k):
    return lax.ppermute(value, "row", [(i, i ^ k) for i in range(RB)])


def after(value, *earlier):
    return lax.optimization_barrier((value,) + earlier)[0]


def sibling(part):
    size = lax.axis_size("col")
    if size == 2:
        return lax.ppermute(part, "col", [(0, 1), (1, 0)])
    total = None
    for s in range(1, size):
        term = lax.ppermute(part, "col", [(i, (i + s) % size) for i in range(size)]).astype(F32)
        total = term if total is None else total + term
    return total.astype(BF16)


def col_gather(value):
    size = lax.axis_size("col")
    if size == 2:
        other = lax.ppermute(value, "col", [(0, 1), (1, 0)])
        first = lax.axis_index("col") == 0
        return jnp.stack([jnp.where(first, value, other), jnp.where(first, other, value)], axis=-2)
    return lax.all_gather(value, "col", axis=value.ndim - 1)


def gather_far(links, near, axis, *earlier):
    size = near[1].shape[axis] // 2
    near_x, near_y = [after(block, *earlier) for block in near[1:3]] if earlier else near[1:3]
    first = lax.slice_in_dim(near_x, 0, size, axis=axis)
    second = lax.slice_in_dim(near_y, size, 2 * size, axis=axis)
    return [links.swap(first, 2), links.swap(second, 1)]


def add(*terms):
    total = terms[0].astype(F32)
    for term in terms[1:]:
        total = total + term.astype(F32)
    return total.astype(terms[0].dtype)


def inward(values):
    size = lax.axis_size("dp")
    for s in range(size // 2 - 1):
        moved = [along(value, [(s, s + 1), (size - 1 - s, size - 2 - s)]) for value in values]
        values = [add(*pair) for pair in zip(values, moved)]
    return values


def across(values):
    half = lax.axis_size("dp") // 2
    moved = [along(value, [(half - 1, half), (half, half - 1)]) for value in values]
    return [add(*pair) for pair in zip(values, moved)]


def outward(values):
    size = lax.axis_size("dp")
    where = lax.axis_index("dp")
    for s in reversed(range(size // 2 - 1)):
        moved = [along(value, [(s + 1, s), (size - 2 - s, size - 1 - s)]) for value in values]
        outer = (where == s) | (where == size - 1 - s)
        values = [jnp.where(outer, new, value) for value, new in zip(values, moved)]
    return values


def along(self, value, pairs):
        return self.permute(value, "dp", pairs, "dp")


def swap(value, k):
    return lax.ppermute(value, "row", [(i, i ^ k) for i in range(RB)])


def after(value, *earlier):
    return lax.optimization_barrier((value,) + earlier)[0]


def sibling(part):
    size = lax.axis_size("col")
    if size == 2:
        return lax.ppermute(part, "col", [(0, 1), (1, 0)])
    total = None
    for s in range(1, size):
        term = lax.ppermute(part, "col", [(i, (i + s) % size) for i in range(size)]).astype(F32)
        total = term if total is None else total + term
    return total.astype(BF16)


def col_gather(value):
    size = lax.axis_size("col")
    if size == 2:
        other = lax.ppermute(value, "col", [(0, 1), (1, 0)])
        first = lax.axis_index("col") == 0
        return jnp.stack([jnp.where(first, value, other), jnp.where(first, other, value)], axis=-2)
    return lax.all_gather(value, "col", axis=value.ndim - 1)


def gather_far(links, near, axis, *earlier):
    size = near[1].shape[axis] // 2
    near_x, near_y = [after(block, *earlier) for block in near[1:3]] if earlier else near[1:3]
    first = lax.slice_in_dim(near_x, 0, size, axis=axis)
    second = lax.slice_in_dim(near_y, size, 2 * size, axis=axis)
    return [links.swap(first, 2), links.swap(second, 1)]


def add(*terms):
    total = terms[0].astype(F32)
    for term in terms[1:]:
        total = total + term.astype(F32)
    return total.astype(terms[0].dtype)


def dp_sum(values, permute):
    size = lax.axis_size("dp")
    if size == 1:
        return values
    if size % 2:
        return [lax.psum(value, "dp") for value in values]
    half = size // 2
    where = lax.axis_index("dp")
    for s in range(half - 1):
        moved = [permute(value, [(s, s + 1), (size - 1 - s, size - 2 - s)]) for value in values]
        values = [add(*pair) for pair in zip(values, moved)]
    moved = [permute(value, [(half - 1, half), (half, half - 1)]) for value in values]
    values = [add(*pair) for pair in zip(values, moved)]
    for s in reversed(range(half - 1)):
        moved = [permute(value, [(s + 1, s), (size - 2 - s, size - 1 - s)]) for value in values]
        outer = (where == s) | (where == size - 1 - s)
        values = [jnp.where(outer, new, value) for value, new in zip(values, moved)]
    return values


def along(value, pairs):
    return lax.ppermute(value, "dp", pairs)


def first_sends(blocks):
    return swap(blocks[1], 1), swap(blocks[2], 2)


def last_terms(blocks, came):
    return add(blocks[3], came[1][: KB // 2]), add(blocks[4], came[0][: KB // 2])


def last_sends(terms):
    return swap(terms[0], 1), swap(terms[1], 2)


def own_sums(blocks, came, last):
    half = KB // 2
    return add(blocks[0][:half], came[0][half:], last[1]), add(blocks[0][half:], came[1][half:], last[0])


def afters(values, *earlier):
    return [after(value, *earlier) for value in values]


def per_device(
    tokens,
    projector,
    offsets,
    combiner,
    baseline,
    widener,
    thresholds,
    narrower,
    residue,
    stretch,
    lifting,
    dilation,
    elevation,
    cotangent,
):
    row = lax.axis_index("row")
    columns = lax.axis_size("col")
    features = tokens.shape[1]
    width = projector.shape[2]

    links = Links()

    def pick(stack, index, axis=0):
        return lax.dynamic_index_in_dim(stack, index, axis, keepdims=False)

    def padded(value):
        return jnp.pad(value.reshape(RB, SEQ, features), ((0, 0), (0, PAD - SEQ), (0, 0)))

    def images_out(values):
        mine = pick(values.reshape(-1, PAD, RB, columns, features), lax.axis_index("col"), 3)
        mine = mine[:, :SEQ]
        got = jnp.stack([mine[:, :, 0]] + [swap(mine[:, :, k], k) for k in range(1, RB)])
        return jnp.concatenate([pick(got, row ^ j) for j in range(RB)], axis=1)

    vectors = jnp.stack([stretch, lifting, baseline, dilation, elevation, residue, residue, residue])
    vec = jnp.stack([vectors] + [links.swap(vectors, k) for k in range(1, RB)], axis=1)
    vec = col_gather(vec).reshape(8, D)
    both = jnp.stack([padded(tokens), padded(cotangent)])
    near = [pick(both, row, 1)] + [links.swap(pick(both, row ^ k, 1), k) for k in range(1, RB)]
    both = col_gather(jnp.stack(near, axis=2)).reshape(2, PAD, D)
    x, cot = both[0], both[1]
    attn = after(jnp.concatenate([projector, combiner.T[None]]), near[1], near[2])
    attn_w = [attn, links.swap(attn, 1), links.swap(attn, 2)]
    wide_w = [widener, links.swap(widener, 1), links.swap(widener, 2)]
    attn_w += gather_far(links, attn_w, 1)
    wide_w += gather_far(links, wide_w, 0)
    narrow_w = [narrower, links.swap(narrower, 1), links.swap(narrower, 2)]
    narrow_w += gather_far(links, narrow_w, 1)

    bias = jnp.stack([offsets[0], jnp.zeros((width,), F32), offsets[1]])[:, None]
    normed_one_t, qkv = qkv_call(x, vec, attn_w, bias)
    mixed, probs = attend_call(qkv)
    part = combine_call(mixed, attn_w)
    out = forward_call(x, part, sibling(after(part, *wide_w[3:])), vec, wide_w, thresholds[None], cot)
    resid, normed_two_t, hidden, slope = out[:4]
    blocks_n = afters(out[4:], *narrow_w[3:])
    came_n = first_sends(blocks_n)

    out = backward_call(cot, narrow_w, slope, normed_two_t, wide_w)
    part, thresholds_sum = out[:2]
    blocks_w = out[2:]
    terms_n = last_terms(blocks_n, afters(came_n, part))
    last_n = last_sends(terms_n)
    came_w = first_sends(afters(blocks_w, *terms_n))
    out = resid_call(part, sibling(after(part, *came_n)), resid, cot, vec, attn_w)
    grad_resid, grad_mixed, grad_t, sums_two = out
    halves_n = jnp.concatenate(own_sums(blocks_n, came_n, afters(last_n, grad_mixed)))
    sum_n = lax.psum(halves_n, "dp")
    grads = attend_back_call(qkv, after(grad_mixed, halves_n), probs)
    out = project_call(grads, normed_one_t, grad_t, mixed, attn_w)
    part, grad_sums = out[:2]
    came_w = afters(came_w, part)
    terms = last_terms(blocks_w, came_w)
    last_w = last_sends(terms)
    blocks_p = afters(out[2:], *terms)
    came_p = first_sends(blocks_p)
    halves_w = own_sums(blocks_w, came_w, afters(last_w, part))
    inner_w = inward([jnp.concatenate(halves_w)])
    middle_w = across(inner_w)
    widener_delta = outward(middle_w)[0].astype(F32)
    ffn_part = narrow_call(after(hidden, *halves_w), narrow_w)
    ffn_other = sibling(after(ffn_part, *inner_w))
    delta, sums_one = tokens_call(part, after(sibling(part), *came_p, *inner_w), x, grad_resid, cot, vec)
    last_p = last_sends(last_terms(blocks_p, came_p))
    halves_p = own_sums(blocks_p, came_p, last_p)

    featured = jnp.concatenate([sums_one[:2], sums_two[:4]]).reshape(6, RB, columns, features)
    featured = pick(featured, lax.axis_index("col"), 2)
    shared = jnp.concatenate([grad_sums[0, 0], grad_sums[2, 0], thresholds_sum[0]])
    pack = [jnp.concatenate([featured[:, k].reshape(-1), shared]) for k in range(RB)]
    small = add(pack[0], *[swap(after(pack[k], *halves_p), k) for k in range(1, RB)]).astype(BF16)
    size, line = small.shape[0], 4 * width
    lines = -(-size // (16 * line)) * 16
    small = jnp.pad(small, (0, lines * line - size)).reshape(lines, line)
    inner_p = inward([halves_p[0], jnp.concatenate([halves_p[1], small])])
    middle_p = across(inner_p)
    first, second = outward(middle_p)
    small = second[KB // 2 :].reshape(-1)[:size].astype(F32)
    total_p = jnp.concatenate([first, second[: KB // 2]]).astype(F32)
    projector_delta = jnp.stack([total_p[:, j * width : (j + 1) * width] for j in range(3)])
    combiner_delta = total_p[:, 3 * width :].T

    ffn = ffn_part.astype(F32) + ffn_other.astype(F32) + vec[RESIDUE]
    layer = (ffn + (resid - x.astype(F32))).astype(BF16)
    outs = images_out(after(jnp.stack([layer, delta]), *inner_p))
    layer_output = outs[0] + tokens.astype(F32)
    tokens_delta = outs[1] + cotangent.astype(F32)
    narrower_delta = after(sum_n, outs).astype(F32).T

    count = 6 * features
    vector = small[:count].reshape(6, features)
    offsets_delta = small[count : count + 2 * width].reshape(2, width)
    thresholds_delta = small[count + 2 * width :]
    return (
        layer_output,
        tokens_delta,
        projector_delta,
        offsets_delta,
        combiner_delta,
        vector[4],
        widener_delta,
        thresholds_delta,
        narrower_delta,
        vector[5],
        vector[0],
        vector[1],
        vector[2],
        vector[3],
    )


def solution(mesh):
    features = P(("row", "col"))
    specs = {
        "tokens": P("dp", ("row", "col")),
        "projector": P(None, "row", "col"),
        "offsets": P(None, "col"),
        "combiner": P("col", "row"),
        "baseline": features,
        "widener": P("row", "col"),
        "thresholds": P("col"),
        "narrower": P("col", "row"),
        "residue": features,
        "stretch": features,
        "lifting": features,
        "dilation": features,
        "elevation": features,
    }
    weights = tuple(specs.values())
    return jax.shard_map(
        per_device,
        mesh=mesh,
        in_specs=weights + (specs["tokens"],),
        out_specs=(specs["tokens"], specs["tokens"]) + weights[1:],
        check_vma=False,
    )
```

time: 501 us -> 401 us (0.80)
  starting transfers between devices: 137 us -> 57.1 us
  waiting for transfers between devices: 187 us -> 142 us
  between operations: 2.4 us -> 15.3 us
  other arithmetic: 28.2 us -> 38.3 us
    ppermute x58 -> x18, waiting for transfers between devices: 139 us -> 37.2 us  [swap(): return lax.ppermute(value, 'row', [(i, i ^ k) for i in range(RB)])]
    ppermute x27, waiting for transfers between devices: 45.2 us -> 104 us  [the longest x18 69.5 us: permute(): got = lax.ppermute(value, axis, pairs)]
    ppermute x58 -> x18, starting transfers between devices: 65 us -> 20.3 us  [swap(): return lax.ppermute(value, 'row', [(i, i ^ k) for i in range(RB)])]
    ppermute x27, starting transfers between devices: 72.1 us -> 36.6 us  [the longest x9 19.3 us: along(): return lax.ppermute(value, 'dp', pairs)]
    reshape x4 -> x2, local copies, waits for them, and re-layouts: 10.5 us -> 3.01 us  [the longest x1 2.97 us: images_out(): values.reshape(-1, PAD, RB, columns, features)]
    convert_element_type x28 -> x15, other arithmetic: 12.6 us -> 19.2 us  [add(): return total.astype(terms[0].dtype)]
  transfers between devices with their start and end apart: 92 -> 52, of which waited for: 33 -> 24; matrix products, arithmetic and copies ran while one was open for 12% -> 17% of each run, Pallas kernels for 17% -> 26%
where the time goes in v2:
time: 401 us; the launch traced here: 396 us
  waiting for transfers between devices  142 us (35%)
  Pallas kernels  102 us (25%)
  starting transfers between devices  57.1 us (14%)
  local copies, waits for them, and re-layouts  42.1 us (10%)
  other arithmetic  38.3 us (10%)
  between operations  15.3 us (4%)
    ppermute x18, waiting for transfers between devices, permute(): got = lax.ppermute(value, axis, pairs)  69.5 us
    ppermute x18, waiting for transfers between devices, swap(): return lax.ppermute(value, 'row', [(i, i ^ k) for i in range(RB)])  37.2 us
    ppermute x9, waiting for transfers between devices, along(): return lax.ppermute(value, 'dp', pairs)  34.8 us
    ppermute x18, starting transfers between devices, swap(): return lax.ppermute(value, 'row', [(i, i ^ k) for i in range(RB)])  20.3 us
    pallas_call x1, Pallas kernels, backward_call(): call(backward_kernel, (width // tile,), [whole((PAD, D))] + narrow_specs(...  20.2 us
    ppermute x9, starting transfers between devices, along(): return lax.ppermute(value, 'dp', pairs)  19.3 us
    convert_element_type x15, other arithmetic, add(): return total.astype(terms[0].dtype)  19.2 us
    ppermute x18, starting transfers between devices, permute(): got = lax.ppermute(value, axis, pairs)  17.3 us
  transfers between devices with their start and end apart: 52, of which 24 were waited for; matrix products, arithmetic and copies ran while one was open for 17% of the time, Pallas kernels for 26%

profile of v2, /device:TPU:0, one launch (start us, length us, event | category | flops | bytes accessed | tf_op | source)
XLA Modules:
  0.0 395.8 jit_solution(7543994014231993143)
XLA Ops:
  9.8 2.9 collective-permute-start
  15.1 4.9 %collective-permute-done = bf16[2,592,128]{2,1,0:T(8,128)(2,1)} collective-permute-done((bf16[2,592,128]{2,1,0:T(8,128)(2,1)S(1)}, bf16[2,592,128]{2,1,0:T(8,128)(2,1)}, u32[]{:S(2)}, u32[]{:S(2)}) %collective-permute-start) | collective-permute-done | bytes 303136 | tf_op jit(solution)/shard_map/ppermute | solution.py:494
  21.8 2.7 collective-permute-start.2
  24.9 3.1 collective-permute-done.5
  28.6 24.2 %collective-permute-done.2 = bf16[2,592,128]{2,1,0:T(8,128)(2,1)S(1)} collective-permute-done((bf16[2,592,128]{2,1,0:T(8,128)(2,1)}, bf16[2,592,128]{2,1,0:T(8,128)(2,1)S(1)}, u32[]{:S(2)}, u32[]{:S(2)}) %collective-permute-start.2) | collective-permute-done | bytes 303136 | tf_op jit(solution)/shard_map/ppermute | solution.py:494
  63.3 18.9 %collective-permute-done.13.rest_2_.rest_9_ = bf16[256,2048]{1,0:T(8,128)(2,1)} collective-permute-done((bf16[256,2048]{1,0:T(8,128)(2,1)}, bf16[256,2048]{1,0:T(8,128)(2,1)}, u32[]{:S(2)}, u32[]{:S(2)}) %collective-permute-start.13) | collective-permute-done | bytes 1048608 | tf_op jit(solution)/shard_map/ppermute | solution.py:494
  89.7 7.5 %collective-permute-done.11.rest_4_ = bf16[4,128,512]{2,1,0:T(8,128)(2,1)S(1)} collective-permute-done((bf16[4,128,512]{2,1,0:T(8,128)(2,1)S(1)}, bf16[4,128,512]{2,1,0:T(8,128)(2,1)S(1)}, u32[]{:S(2)}, u32[]{:S(2)}) %collective-permute-start.11) | collective-permute-done | bytes 524320 | tf_op jit(solution)/shard_map/ppermute | solution.py:494
  104.8 6.8 %shard_map.245 = (bf16[1024,592]{1,0:T(8,128)(2,1)}, bf16[592,1536]{1,0:T(8,128)(2,1)}) custom-call(bf16[592,1024]{1,0:T(8,128)(2,1)} %squeeze.67.x, f32[8,1024]{1,0:T(8,128)} %bitcast.108, bf16[4,256,512]{2,1,0:T(8,128)(2,1)} %copy-done.1, bf16[4,256,512]{2,1,0:T(8,128)(2,1)} %copy-done.2, bf16[4,256,512]{2,1,0:T(8,128)(2,1)} %copy-done.3, ...), custom_call_target="tpu_custom_call" | custom-call | flops 29097984 | bytes 115456 | tf_op jit(solution)/shard_map/pallas_call | solution.py:111
  111.6 9.2 %shard_map.246 = (bf16[592,512]{1,0:T(8,128)(2,1)}, bf16[8,592,592]{2,1,0:T(8,128)(2,1)}) custom-call(bf16[592,1536]{1,0:T(8,128)(2,1)} %get-tuple-element.99.q.k.v, bf16[592,1536]{1,0:T(8,128)(2,1)} %get-tuple-element.99.q.k.v, bf16[592,1536]{1,0:T(8,128)(2,1)} %get-tuple-element.99.q.k.v), custom_call_target="tpu_custom_call" | custom-call | flops 22429696 | bytes 87616 | tf_op jit(solution)/shard_map/pallas_call | solution.py:152
  120.8 3.3 shard_map.247.part
  124.1 5.1 %collective-permute-done.17.rest_1_ = bf16[2048,256]{1,0:T(8,128)(2,1)S(1)} collective-permute-done((bf16[2048,256]{1,0:T(8,128)(2,1)}, bf16[2048,256]{1,0:T(8,128)(2,1)S(1)}, u32[]{:S(2)}, u32[]{:S(2)}) %collective-permute-start.17) | collective-permute-done | bytes 1048608 | tf_op jit(solution)/shard_map/ppermute | solution.py:494
  135.1 14.9 %shard_map.248 = (f32[592,1024]{1,0:T(8,128)}, bf16[1024,592]{1,0:T(8,128)(2,1)}, bf16[592,2048]{1,0:T(8,128)(2,1)}, bf16[592,2048]{1,0:T(8,128)(2,1)}, bf16[256...) custom-call(bf16[592,1024]{1,0:T(8,128)(2,1)} %squeeze.67.x, ...), custom_call_target="tpu_custom_call" | custom-call | flops 77594624 | bytes 339456 | tf_op jit(solution)/shard_map/pallas_call | solution.py:239
  153.0 20.2 %shard_map.249 = (bf16[592,1024]{1,0:T(8,128)(2,1)}, f32[1,2048]{1,0:T(1,128)}, bf16[256,2048]{1,0:T(8,128)(2,1)}, bf16[256,2048]{1,0:T(8,128)(2,1)}, bf16[256,2...) custom-call(bf16[592,1024]{1,0:T(8,128)(2,1)} %squeeze.68.rest_6_.cot, ...), custom_call_target="tpu_custom_call" | custom-call | flops 116391936 | bytes 291328 | tf_op jit(solution)/shard_map/pallas_call | solution.py:295
  180.6 7.4 %shard_map.250 = (f32[592,1024]{1,0:T(8,128)}, bf16[592,512]{1,0:T(8,128)(2,1)}, bf16[1024,592]{1,0:T(8,128)(2,1)}, f32[8,1024]{1,0:T(8,128)}) custom-call(bf16[592,1024]{1,0:T(8,128)(2,1)} %get-tuple-element.127.part, bf16[592,1024]{1,0:T(8,128)(2,1)} %copy-done.19, f32[592,1024]{1,0:T(8,128)} %get-tuple-element.128.resid, ...), custom_call_target="tpu_custom_call" | custom-call | flops 9699328 | bytes 177408 | tf_op jit(solution)/shard_map/pallas_call | solution.py:370
  194.5 11.5 %shard_map.251 = (bf16[592,512]{1,0:T(8,128)(2,1)}, bf16[592,512]{1,0:T(8,128)(2,1)}, bf16[592,512]{1,0:T(8,128)(2,1)}) custom-call(bf16[592,1536]{1,0:T(8,128)(2,1)} %get-tuple-element.99.q.k.v, bf16[592,1536]{1,0:T(8,128)(2,1)} %get-tuple-element.99.q.k.v, bf16[592,1536]{1,0:T(8,128)(2,1)} %get-tuple-element.99.q.k.v, ...), custom_call_target="tpu_custom_call" | custom-call | flops 44859392 | bytes 87616 | tf_op jit(solution)/shard_map/pallas_call | solution.py:411
  206.0 10.7 %shard_map.252 = (bf16[592,1024]{1,0:T(8,128)(2,1)}, f32[3,1,512]{2,1,0:T(1,128)}, bf16[256,2048]{1,0:T(8,128)(2,1)}, bf16[256,2048]{1,0:T(8,128)(2,1)}, bf16[25...) custom-call(bf16[592,512]{1,0:T(8,128)(2,1)} %get-tuple-element.136.gq, ...), custom_call_target="tpu_custom_call" | custom-call | flops 67895296 | bytes 216320 | tf_op jit(solution)/shard_map/pallas_call | solution.py:451
  225.3 9.7 %collective-permute-done.27 = bf16[128,2048]{1,0:T(8,128)(2,1)} collective-permute-done((bf16[128,2048]{1,0:T(8,128)(2,1)S(1)}, bf16[128,2048]{1,0:T(8,128)(2,1)}, u32[]{:S(2)}, u32[]{:S(2)}) %collective-permute-start.27) | collective-permute-done | bytes 524320 | tf_op jit(solution)/shard_map/ppermute | solution.py:577
  235.0 2.7 collective-permute-done.29
  239.9 3.7 collective-permute-start.30
  243.6 13.8 %collective-permute-done.33 = bf16[256,2048]{1,0:T(8,128)(2,1)} collective-permute-done((bf16[256,2048]{1,0:T(8,128)(2,1)}, bf16[256,2048]{1,0:T(8,128)(2,1)}, u32[]{:S(2)}, u32[]{:S(2)}) %collective-permute-start.33) | collective-permute-done | bytes 1048608 | tf_op jit(solution)/shard_map/ppermute | solution.py:577
  262.1 6.3 %shard_map.254 = (bf16[592,1024]{1,0:T(8,128)(2,1)}, f32[8,1024]{1,0:T(8,128)}) custom-call(bf16[592,1024]{1,0:T(8,128)(2,1)} %get-tuple-element.141.part, bf16[592,1024]{1,0:T(8,128)(2,1)} %copy-done.15, bf16[592,1024]{1,0:T(8,128)(2,1)} %squeeze.67.x, f32[592,1024]{1,0:T(8,128)} %get-tuple-element.157.grad_resid, bf16[592,1024]{1,0:T(8,128)(2,1)} %squeeze.68.rest_6_.cot, ...), custom_call_target="tpu_custom_call" | custom-call | flops 189440 | bytes 132608 | tf_op jit(solution)/shard_map/pallas_call | solution.py:475
  277.7 6.2 %collective-permute-start.36 = (bf16[128,2048]{1,0:T(8,128)(2,1)S(1)}, bf16[128,2048]{1,0:T(8,128)(2,1)}, u32[]{:S(2)}, u32[]{:S(2)}) collective-permute-start(bf16[128,2048]{1,0:T(8,128)(2,1)S(1)} %get-tuple-element.229), channel_id=1, source_target_pairs={{0,8},{24,16},{1,9},{25,17},{2,10},{26,18},{3,11},{27,19},{4,12},{... | collective-permute-start | bytes 1572872 | tf_op jit(solution)/shard_map/ppermute | solution.py:640
  286.3 11.4 %shard_map.253 = bf16[592,1024]{1,0:T(8,128)(2,1)} custom-call(bf16[592,2048]{1,0:T(8,128)(2,1)} %get-tuple-element.150.hidden, bf16[2048,256]{1,0:T(8,128)(2,1)} %rest_0_.5, bf16[2048,256]{1,0:T(8,128)(2,1)} %copy-done.8, bf16[2048,256]{1,0:T(8,128)(2,1)} %copy-done.7, bf16[2048,128]{1,0:T(8,128)(2,1)} %collective-permute-done.19.rest_3_, ...), custom_call_target="tpu_custom_call" | custom-call | flops 38797312 | bytes 122368 | tf_op jit(solution)/shard_map/pallas_call | solution.py:336
  297.6 2.7 collective-permute-done.36
  302.4 16.6 %collective-permute-done.41 = bf16[144,2048]{1,0:T(8,128)(2,1)S(1)} collective-permute-done((bf16[144,2048]{1,0:T(8,128)(2,1)}, bf16[144,2048]{1,0:T(8,128)(2,1)S(1)}, u32[]{:S(2)}, u32[]{:S(2)}) %collective-permute-start.41) | collective-permute-done | bytes 589856 | tf_op jit(solution)/shard_map/ppermute | solution.py:640
  328.4 3.0 reshape.82
  331.4 4.2 %constant_dynamic-slice_fusion = bf16[2,592,4,1,128]{4,3,2,1,0:T(2,128)(2,1)S(1)} fusion(bf16[2,592,4,2,128]{4,3,2,1,0:T(2,128)(2,1)} %reshape.82, s32[]{:T(128)S(6)} %select_n.82), kind=kLoop, calls=%fused_computation.101 | loop fusion | bytes 2424836 | tf_op jit(solution)/shard_map/jit(dynamic_index_in_dim)/dynamic_slice | solution.py:688
  344.0 3.1 collective-permute-done.44
  350.3 8.4 %concatenate.47 = bf16[2,2308,128]{2,1,0:T(8,128)(2,1)S(1)} concatenate(bf16[2,577,128]{2,1,0:T(8,128)(2,1)} %get-tuple-element.225, bf16[2,577,128]{2,1,0:T(8,128)(2,1)} %get-tuple-element.224, bf16[2,577,128]{2,1,0:T(8,128)(2,1)} %get-tuple-element.223, bf16[2,577,128]{2,1,0:T(8,128)(2,1)} %get-tuple-element.222), dimensions={1} | concatenate | bytes 2363392 | tf_op jit(solution)/shard_map/concatenate | solution.py:697
  363.6 10.3 %collective-permute-done.46 = bf16[128,2048]{1,0:T(8,128)(2,1)} collective-permute-done((bf16[128,2048]{1,0:T(8,128)(2,1)}, bf16[128,2048]{1,0:T(8,128)(2,1)}, u32[]{:S(2)}, u32[]{:S(2)}) %collective-permute-start.46) | collective-permute-done | bytes 524320 | tf_op jit(solution)/shard_map/ppermute | solution.py:640
  375.1 5.2 %collective-permute-done.48 = bf16[144,2048]{1,0:T(8,128)(2,1)} collective-permute-done((bf16[144,2048]{1,0:T(8,128)(2,1)}, bf16[144,2048]{1,0:T(8,128)(2,1)}, u32[]{:S(2)}, u32[]{:S(2)}) %collective-permute-start.48) | collective-permute-done | bytes 589856 | tf_op jit(solution)/shard_map/ppermute | solution.py:640
  386.0 2.7 select_convert_fusion
  (257 shorter events, 117.5 us)
Async XLA Ops:
  7.2 353.2 %all-reduce.5.cloned.1.call-start = ((), (), s32[]{:S(2)}) async-start(), calls=%async_computation | async-start | bytes 2097152 | tf_op jit(solution)/shard_map/psum | solution.py:732
  21.5 39.0 %collective-permute-start.8 = (bf16[4,256,512]{2,1,0:T(8,128)(2,1)S(1)}, bf16[4,256,512]{2,1,0:T(8,128)(2,1)S(1)}, u32[]{:S(2)}, u32[]{:S(2)}) collective-permute-start(bf16[4,256,512]{2,1,0:T(8,128)(2,1)S(1)} %pad_maximum_fusion.5.rest_0_), channel_id=1, source_target_pairs={{0,2},{2,0},{4,6},{6,4},{1,3},{3,1},{5,7},{7,5},{8,10},{10,8},{12,... | collective-permute-start | bytes 3145736 | tf_op jit(solution)/shard_map/ppermute | solution.py:494
  21.8 30.9 %collective-permute-start.2 = (bf16[2,592,128]{2,1,0:T(8,128)(2,1)}, bf16[2,592,128]{2,1,0:T(8,128)(2,1)S(1)}, u32[]{:S(2)}, u32[]{:S(2)}) collective-permute-start(bf16[2,592,128]{2,1,0:T(8,128)(2,1)} %get-tuple-element.221), channel_id=1, source_target_pairs={{0,6},{2,4},{4,2},{6,0},{1,7},{3,5},{5,3},{7,1},{8,14},{10,12},{12... | collective-permute-start | bytes 909320 | tf_op jit(solution)/shard_map/ppermute | solution.py:494
  28.1 32.6 %collective-permute-start.9 = (bf16[4,256,512]{2,1,0:T(8,128)(2,1)S(1)}, bf16[4,256,512]{2,1,0:T(8,128)(2,1)S(1)}, u32[]{:S(2)}, u32[]{:S(2)}) collective-permute-start(bf16[4,256,512]{2,1,0:T(8,128)(2,1)S(1)} %pad_maximum_fusion.5.rest_0_), channel_id=1, source_target_pairs={{0,4},{2,6},{4,0},{6,2},{1,5},{3,7},{5,1},{7,3},{8,12},{10,14},{12... | collective-permute-start | bytes 3145736 | tf_op jit(solution)/shard_map/ppermute | solution.py:494
  55.1 43.4 %collective-permute-start.3 = (bf16[2,592,4,128]{3,1,0,2:T(8,128)(2,1)}, bf16[2,592,4,128]{3,1,0,2:T(8,128)(2,1)}, u32[]{:S(2)}, u32[]{:S(2)}) collective-permute-start(bf16[2,592,4,128]{3,1,0,2:T(8,128)(2,1)} %pad_maximum_fusion.3), channel_id=1, source_target_pairs={{0,1},{1,0},{2,3},{3,2},{4,5},{5,4},{6,7},{7,6},{8,9},{9,8},{10,11... | collective-permute-start | bytes 3637256 | tf_op jit(solution)/shard_map/ppermute | solution.py:598
  55.8 26.4 %collective-permute-start.13 = (bf16[256,2048]{1,0:T(8,128)(2,1)}, bf16[256,2048]{1,0:T(8,128)(2,1)}, u32[]{:S(2)}, u32[]{:S(2)}) collective-permute-start(bf16[256,2048]{1,0:T(8,128)(2,1)} %rest_7_.1), channel_id=1, source_target_pairs={{0,4},{2,6},{4,0},{6,2},{1,5},{3,7},{5,1},{7,3},{8,12},{10,14},{12... | collective-permute-start | bytes 3145736 | tf_op jit(solution)/shard_map/ppermute | solution.py:494
  59.7 26.4 %collective-permute-start.12 = (bf16[256,2048]{1,0:T(8,128)(2,1)}, bf16[256,2048]{1,0:T(8,128)(2,1)}, u32[]{:S(2)}, u32[]{:S(2)}) collective-permute-start(bf16[256,2048]{1,0:T(8,128)(2,1)} %rest_7_.1), channel_id=1, source_target_pairs={{0,2},{2,0},{4,6},{6,4},{1,3},{3,1},{5,7},{7,5},{8,10},{10,8},{12,... | collective-permute-start | bytes 3145736 | tf_op jit(solution)/shard_map/ppermute | solution.py:494
  60.8 36.5 %collective-permute-start.11 = (bf16[4,128,512]{2,1,0:T(8,128)(2,1)S(1)}, bf16[4,128,512]{2,1,0:T(8,128)(2,1)S(1)}, u32[]{:S(2)}, u32[]{:S(2)}) collective-permute-start(bf16[4,128,512]{2,1,0:T(8,128)(2,1)S(1)} %slice.256), channel_id=1, source_target_pairs={{0,2},{2,0},{4,6},{6,4},{1,3},{3,1},{5,7},{7,5},{8,10},{10,8},{12,... | collective-permute-start | bytes 1572872 | tf_op jit(solution)/shard_map/ppermute | solution.py:494
  62.1 35.1 %collective-permute-start.10 = (bf16[4,128,512]{2,1,0:T(8,128)(2,1)S(1)}, bf16[4,128,512]{2,1,0:T(8,128)(2,1)S(1)}, u32[]{:S(2)}, u32[]{:S(2)}) collective-permute-start(bf16[4,128,512]{2,1,0:T(8,128)(2,1)S(1)} %slice.255), channel_id=1, source_target_pairs={{0,4},{2,6},{4,0},{6,2},{1,5},{3,7},{5,1},{7,3},{8,12},{10,14},{12... | collective-permute-start | bytes 1572872 | tf_op jit(solution)/shard_map/ppermute | solution.py:494
  87.9 36.1 %collective-permute-start.14 = (bf16[128,2048]{1,0:T(8,128)(2,1)}, bf16[128,2048]{1,0:T(8,128)(2,1)}, u32[]{:S(2)}, u32[]{:S(2)}) collective-permute-start(bf16[128,2048]{1,0:T(8,128)(2,1)} %slice.257), channel_id=1, source_target_pairs={{0,4},{2,6},{4,0},{6,2},{1,5},{3,7},{5,1},{7,3},{8,12},{10,14},{12... | collective-permute-start | bytes 1572872 | tf_op jit(solution)/shard_map/ppermute | solution.py:494
  88.5 35.6 %collective-permute-start.15 = (bf16[128,2048]{1,0:T(8,128)(2,1)}, bf16[128,2048]{1,0:T(8,128)(2,1)}, u32[]{:S(2)}, u32[]{:S(2)}) collective-permute-start(bf16[128,2048]{1,0:T(8,128)(2,1)} %slice.258), channel_id=1, source_target_pairs={{0,2},{2,0},{4,6},{6,4},{1,3},{3,1},{5,7},{7,5},{8,10},{10,8},{12,... | collective-permute-start | bytes 1572872 | tf_op jit(solution)/shard_map/ppermute | solution.py:494
  97.2 33.4 %collective-permute-start.18 = (bf16[2048,256]{1,0:T(8,128)(2,1)}, bf16[2048,256]{1,0:T(8,128)(2,1)S(1)}, u32[]{:S(2)}, u32[]{:S(2)}) collective-permute-start(bf16[2048,256]{1,0:T(8,128)(2,1)} %rest_0_.5), channel_id=1, source_target_pairs={{0,4},{2,6},{4,0},{6,2},{1,5},{3,7},{5,1},{7,3},{8,12},{10,14},{12... | collective-permute-start | bytes 3145736 | tf_op jit(solution)/shard_map/ppermute | solution.py:494
  97.8 31.5 %collective-permute-start.17 = (bf16[2048,256]{1,0:T(8,128)(2,1)}, bf16[2048,256]{1,0:T(8,128)(2,1)S(1)}, u32[]{:S(2)}, u32[]{:S(2)}) collective-permute-start(bf16[2048,256]{1,0:T(8,128)(2,1)} %rest_0_.5), channel_id=1, source_target_pairs={{0,2},{2,0},{4,6},{6,4},{1,3},{3,1},{5,7},{7,5},{8,10},{10,8},{12,... | collective-permute-start | bytes 3145736 | tf_op jit(solution)/shard_map/ppermute | solution.py:494
  130.2 19.8 %collective-permute-start.19 = (bf16[2048,128]{1,0:T(8,128)(2,1)}, bf16[2048,128]{1,0:T(8,128)(2,1)}, u32[]{:S(2)}, u32[]{:S(2)}) collective-permute-start(bf16[2048,128]{1,0:T(8,128)(2,1)} %slice.259), channel_id=1, source_target_pairs={{0,4},{2,6},{4,0},{6,2},{1,5},{3,7},{5,1},{7,3},{8,12},{10,14},{12... | collective-permute-start | bytes 1572872 | tf_op jit(solution)/shard_map/ppermute | solution.py:494
  131.5 18.5 %collective-permute-start.20 = (bf16[2048,128]{1,0:T(8,128)(2,1)}, bf16[2048,128]{1,0:T(8,128)(2,1)}, u32[]{:S(2)}, u32[]{:S(2)}) collective-permute-start(bf16[2048,128]{1,0:T(8,128)(2,1)} %slice.260), channel_id=1, source_target_pairs={{0,2},{2,0},{4,6},{6,4},{1,3},{3,1},{5,7},{7,5},{8,10},{10,8},{12,... | collective-permute-start | bytes 1572872 | tf_op jit(solution)/shard_map/ppermute | solution.py:494
  150.0 23.2 %collective-permute-start.22 = (bf16[256,2048]{1,0:T(8,128)(2,1)}, bf16[256,2048]{1,0:T(8,128)(2,1)S(1)}, u32[]{:S(2)}, u32[]{:S(2)}) collective-permute-start(bf16[256,2048]{1,0:T(8,128)(2,1)} %get-tuple-element.124), channel_id=1, source_target_pairs={{0,2},{2,0},{4,6},{6,4},{1,3},{3,1},{5,7},{7,5},{8,10},{10,8},{12,... | collective-permute-start | bytes 3145736 | tf_op jit(solution)/shard_map/ppermute | solution.py:577
  151.4 22.8 %collective-permute-start.21 = (bf16[256,2048]{1,0:T(8,128)(2,1)}, bf16[256,2048]{1,0:T(8,128)(2,1)S(1)}, u32[]{:S(2)}, u32[]{:S(2)}) collective-permute-start(bf16[256,2048]{1,0:T(8,128)(2,1)} %get-tuple-element.118), channel_id=1, source_target_pairs={{0,4},{2,6},{4,0},{6,2},{1,5},{3,7},{5,1},{7,3},{8,12},{10,14},{12... | collective-permute-start | bytes 3145736 | tf_op jit(solution)/shard_map/ppermute | solution.py:577
  177.7 39.0 %collective-permute-start.28 = (bf16[256,2048]{1,0:T(8,128)(2,1)}, bf16[256,2048]{1,0:T(8,128)(2,1)S(1)}, u32[]{:S(2)}, u32[]{:S(2)}) collective-permute-start(bf16[256,2048]{1,0:T(8,128)(2,1)} %get-tuple-element.146), channel_id=1, source_target_pairs={{0,4},{2,6},{4,0},{6,2},{1,5},{3,7},{5,1},{7,3},{8,12},{10,14},{12... | collective-permute-start | bytes 3145736 | tf_op jit(solution)/shard_map/ppermute | solution.py:577
  178.2 38.5 %collective-permute-start.23 = (bf16[256,2048]{1,0:T(8,128)(2,1)}, bf16[256,2048]{1,0:T(8,128)(2,1)S(1)}, u32[]{:S(2)}, u32[]{:S(2)}) collective-permute-start(bf16[256,2048]{1,0:T(8,128)(2,1)} %get-tuple-element.126), channel_id=1, source_target_pairs={{0,2},{2,0},{4,6},{6,4},{1,3},{3,1},{5,7},{7,5},{8,10},{10,8},{12,... | collective-permute-start | bytes 3145736 | tf_op jit(solution)/shard_map/ppermute | solution.py:577
  224.3 33.1 %collective-permute-start.33 = (bf16[256,2048]{1,0:T(8,128)(2,1)}, bf16[256,2048]{1,0:T(8,128)(2,1)}, u32[]{:S(2)}, u32[]{:S(2)}) collective-permute-start(bf16[256,2048]{1,0:T(8,128)(2,1)} %get-tuple-element.153), channel_id=1, source_target_pairs={{0,2},{2,0},{4,6},{6,4},{1,3},{3,1},{5,7},{7,5},{8,10},{10,8},{12,... | collective-permute-start | bytes 3145736 | tf_op jit(solution)/shard_map/ppermute | solution.py:577
  224.8 36.3 %collective-permute-start.32 = (bf16[592,1024]{1,0:T(8,128)(2,1)S(1)}, bf16[592,1024]{1,0:T(8,128)(2,1)S(1)}, u32[]{:S(2)}, u32[]{:S(2)}) collective-permute-start(bf16[592,1024]{1,0:T(8,128)(2,1)S(1)} %copy-done.14), channel_id=1, source_target_pairs={{0,1},{1,0},{2,3},{3,2},{4,5},{5,4},{6,7},{7,6},{8,9},{9,8},{10,11... | collective-permute-start | bytes 3637256 | tf_op jit(solution)/shard_map/ppermute | solution.py:587
  224.8 34.2 %collective-permute-start.34 = (bf16[256,2048]{1,0:T(8,128)(2,1)}, bf16[256,2048]{1,0:T(8,128)(2,1)S(1)}, u32[]{:S(2)}, u32[]{:S(2)}) collective-permute-start(bf16[256,2048]{1,0:T(8,128)(2,1)} %get-tuple-element.155), channel_id=1, source_target_pairs={{0,4},{2,6},{4,0},{6,2},{1,5},{3,7},{5,1},{7,3},{8,12},{10,14},{12... | collective-permute-start | bytes 3145736 | tf_op jit(solution)/shard_map/ppermute | solution.py:577
  239.9 20.7 %collective-permute-start.30 = (bf16[256,2048]{1,0:T(8,128)(2,1)S(1)}, bf16[256,2048]{1,0:T(8,128)(2,1)S(1)}, u32[]{:S(2)}, u32[]{:S(2)}) collective-permute-start(bf16[256,2048]{1,0:T(8,128)(2,1)S(1)} %pad_maximum_fusion.7), channel_id=1, source_target_pairs={{0,8},{24,16},{1,9},{25,17},{2,10},{26,18},{3,11},{27,19},{4,12},{... | collective-permute-start | bytes 3145736 | tf_op jit(solution)/shard_map/ppermute | solution.py:640
  276.1 45.3 %collective-permute-start.49 = (bf16[256,2048]{1,0:T(8,128)(2,1)S(1)}, bf16[256,2048]{1,0:T(8,128)(2,1)}, u32[]{:S(2)}, u32[]{:S(2)}) collective-permute-start(bf16[256,2048]{1,0:T(8,128)(2,1)S(1)} %add_convert_fusion.2), channel_id=1, source_target_pairs={{8,16},{16,8},{9,17},{17,9},{10,18},{18,10},{11,19},{19,11},{12,20... | collective-permute-start | bytes 3145736 | tf_op jit(solution)/shard_map/ppermute | solution.py:640
  277.7 22.5 %collective-permute-start.36 = (bf16[128,2048]{1,0:T(8,128)(2,1)S(1)}, bf16[128,2048]{1,0:T(8,128)(2,1)}, u32[]{:S(2)}, u32[]{:S(2)}) collective-permute-start(bf16[128,2048]{1,0:T(8,128)(2,1)S(1)} %get-tuple-element.229), channel_id=1, source_target_pairs={{0,8},{24,16},{1,9},{25,17},{2,10},{26,18},{3,11},{27,19},{4,12},{... | collective-permute-start | bytes 1572872 | tf_op jit(solution)/shard_map/ppermute | solution.py:640
  284.9 34.1 %collective-permute-start.41 = (bf16[144,2048]{1,0:T(8,128)(2,1)}, bf16[144,2048]{1,0:T(8,128)(2,1)S(1)}, u32[]{:S(2)}, u32[]{:S(2)}) collective-permute-start(bf16[144,2048]{1,0:T(8,128)(2,1)} %pad_maximum_fusion.8), channel_id=1, source_target_pairs={{0,8},{24,16},{1,9},{25,17},{2,10},{26,18},{3,11},{27,19},{4,12},{... | collective-permute-start | bytes 1769480 | tf_op jit(solution)/shard_map/ppermute | solution.py:640
  297.6 29.2 %collective-permute-start.31 = (bf16[592,1024]{1,0:T(8,128)(2,1)}, bf16[592,1024]{1,0:T(8,128)(2,1)S(1)}, u32[]{:S(2)}, u32[]{:S(2)}) collective-permute-start(bf16[592,1024]{1,0:T(8,128)(2,1)} %shard_map.253), channel_id=1, source_target_pairs={{0,1},{1,0},{2,3},{3,2},{4,5},{5,4},{6,7},{7,6},{8,9},{9,8},{10,11... | collective-permute-start | bytes 3637256 | tf_op jit(solution)/shard_map/ppermute | solution.py:587
  301.4 23.2 %collective-permute-start.45 = (bf16[128,2048]{1,0:T(8,128)(2,1)S(1)}, bf16[128,2048]{1,0:T(8,128)(2,1)S(1)}, u32[]{:S(2)}, u32[]{:S(2)}) collective-permute-start(bf16[128,2048]{1,0:T(8,128)(2,1)S(1)} %add_convert_fusion.8), channel_id=1, source_target_pairs={{8,16},{16,8},{9,17},{17,9},{10,18},{18,10},{11,19},{19,11},{12,20... | collective-permute-start | bytes 1572872 | tf_op jit(solution)/shard_map/ppermute | solution.py:640
  319.9 19.1 %collective-permute-start.47 = (bf16[144,2048]{1,0:T(8,128)(2,1)}, bf16[144,2048]{1,0:T(8,128)(2,1)}, u32[]{:S(2)}, u32[]{:S(2)}) collective-permute-start(bf16[144,2048]{1,0:T(8,128)(2,1)} %add_convert_fusion.4), channel_id=1, source_target_pairs={{8,16},{16,8},{9,17},{17,9},{10,18},{18,10},{11,19},{19,11},{12,20... | collective-permute-start | bytes 1769480 | tf_op jit(solution)/shard_map/ppermute | solution.py:640
  323.2 62.8 %collective-permute-start.50 = (bf16[256,2048]{1,0:T(8,128)(2,1)S(1)}, bf16[256,2048]{1,0:T(8,128)(2,1)}, u32[]{:S(2)}, u32[]{:S(2)}) collective-permute-start(bf16[256,2048]{1,0:T(8,128)(2,1)S(1)} %add_convert_fusion.1), channel_id=1, source_target_pairs={{8,0},{16,24},{9,1},{17,25},{10,2},{18,26},{11,3},{19,27},{12,4},{... | collective-permute-start | bytes 3145736 | tf_op jit(solution)/shard_map/ppermute | solution.py:640
  325.5 48.4 %collective-permute-start.46 = (bf16[128,2048]{1,0:T(8,128)(2,1)}, bf16[128,2048]{1,0:T(8,128)(2,1)}, u32[]{:S(2)}, u32[]{:S(2)}) collective-permute-start(bf16[128,2048]{1,0:T(8,128)(2,1)} %add_convert_fusion.5), channel_id=1, source_target_pairs={{8,0},{16,24},{9,1},{17,25},{10,2},{18,26},{11,3},{19,27},{12,4},{... | collective-permute-start | bytes 1572872 | tf_op jit(solution)/shard_map/ppermute | solution.py:640
  342.7 37.6 %collective-permute-start.48 = (bf16[144,2048]{1,0:T(8,128)(2,1)}, bf16[144,2048]{1,0:T(8,128)(2,1)}, u32[]{:S(2)}, u32[]{:S(2)}) collective-permute-start(bf16[144,2048]{1,0:T(8,128)(2,1)} %add_convert_fusion.3), channel_id=1, source_target_pairs={{8,0},{16,24},{9,1},{17,25},{10,2},{18,26},{11,3},{19,27},{12,4},{... | collective-permute-start | bytes 1769480 | tf_op jit(solution)/shard_map/ppermute | solution.py:640
  (64 other events, 560.1 us)
Sparse Core Ops, SparseCore 0:
  286.4 68.2 all-reduce.4

commit v3 on v2

--- a/solution.py
+++ b/solution.py
@@ -252,36 +252,40 @@
     )(x, part, sib, vec, *blocks, thresholds, cot)
 
 
+def accumulate(total, at, term):
+    step = pl.program_id(0)
+
+    @pl.when(step == 0)
+    def _():
+        total[:, at] = term
+
+    @pl.when(step > 0)
+    def _():
+        total[:, at] += term
+
+
 def backward_kernel(cot, *rest):
-    narrow, (slope, normed_t), wide, rest = rest[:5], rest[5:7], rest[7:12], rest[12:]
-    part, thresholds_sum = rest[:2]
-    deltas = rest[2:7]
-    total = rest[7]
-    step = pl.program_id(0)
+    narrow, (slope, hidden, normed_t), wide, rest = rest[:5], rest[5:8], rest[8:13], rest[13:]
+    part, out, thresholds_sum = rest[:3]
+    deltas, (total, out_total) = rest[3:8], rest[8:]
     grad = None
-    for k, n in enumerate(narrow[:3]):
-        term = mm_nt(cot[:, k * KB : (k + 1) * KB], n[...])
+    blocks = [n[...] for n in narrow]
+    blocks = blocks[:3] + [jnp.concatenate(blocks[3:], axis=1)]
+    for k, n in enumerate(blocks):
+        at = slice(k * KB, (k + 1) * KB)
+        term = mm_nt(cot[:, at], n)
         grad = term if grad is None else grad + term
-    far = jnp.concatenate([narrow[3][...], narrow[4][...]], axis=1)
-    grad = grad + mm_nt(cot[:, 3 * KB :], far)
+        accumulate(out_total, at, mm(hidden[...], n))
     grad = (grad * slope[...].astype(F32)).astype(BF16)
     thresholds_sum[...] = jnp.sum(grad.astype(F32), axis=0, keepdims=True)
     split_rows(mm(normed_t[...], grad), deltas)
     for k, w in enumerate(joined(wide)):
-        at = slice(k * KB, (k + 1) * KB)
-        term = mm_nt(grad, w)
-
-        @pl.when(step == 0)
-        def _():
-            total[:, at] = term
-
-        @pl.when(step > 0)
-        def _():
-            total[:, at] += term
-
-    @pl.when(step == pl.num_programs(0) - 1)
+        accumulate(total, slice(k * KB, (k + 1) * KB), mm_nt(grad, w))
+
+    @pl.when(pl.program_id(0) == pl.num_programs(0) - 1)
     def _():
         part[...] = total[...].astype(BF16)
+        out[...] = out_total[...].astype(BF16)
 
 
 def narrow_specs(tile):
@@ -289,60 +293,24 @@
     return [pl.BlockSpec((tile, KB), lambda t: (t, 0))] * 3 + [half] * 2
 
 
-def backward_call(cot, narrow_blocks, slope, normed_t, wide_blocks):
+def backward_call(cot, narrow_blocks, slope, hidden, normed_t, wide_blocks):
     width = slope.shape[1]
     tile = min(512, width)
+    cols = pl.BlockSpec((PAD, tile), lambda t: (0, t))
     return call(
         backward_kernel,
         (width // tile,),
         [whole((PAD, D))]
         + narrow_specs(tile)
-        + [pl.BlockSpec((PAD, tile), lambda t: (0, t)), whole((D, PAD))]
+        + [cols, cols, whole((D, PAD))]
         + [pl.BlockSpec((KB, tile), lambda t: (0, t))] * 3
         + [pl.BlockSpec((KB // 2, tile), lambda t: (0, t))] * 2,
-        [whole((PAD, D)), pl.BlockSpec((1, tile), lambda t: (0, t))] + delta_specs(tile, lambda t: (0, t)),
-        [sds((PAD, D)), sds((1, width), F32)] + delta_shapes(width),
-        6 * PAD * D * width,
-        6 * D * width + 6 * PAD * D + 2 * PAD * width,
-        [pltpu.VMEM((PAD, D), F32)],
-    )(cot, *narrow_blocks, slope, normed_t, *wide_blocks)
-
-
-def narrow_kernel(hidden, *rest):
-    weights, (part, total) = rest[:5], rest[5:]
-    step = pl.program_id(0)
-    blocks = [n[...] for n in weights]
-    blocks = blocks[:3] + [jnp.concatenate(blocks[3:], axis=1)]
-    for k, n in enumerate(blocks):
-        at = slice(k * KB, (k + 1) * KB)
-        term = mm(hidden[...], n)
-
-        @pl.when(step == 0)
-        def _():
-            total[:, at] = term
-
-        @pl.when(step > 0)
-        def _():
-            total[:, at] += term
-
-    @pl.when(step == pl.num_programs(0) - 1)
-    def _():
-        part[...] = total[...].astype(BF16)
-
-
-def narrow_call(hidden, blocks):
-    width = hidden.shape[1]
-    tile = min(512, width)
-    return call(
-        narrow_kernel,
-        (width // tile,),
-        [pl.BlockSpec((PAD, tile), lambda t: (0, t))] + narrow_specs(tile),
-        whole((PAD, D)),
-        sds((PAD, D)),
-        2 * PAD * D * width,
-        2 * D * width + 2 * PAD * D + 2 * PAD * width,
-        [pltpu.VMEM((PAD, D), F32)],
-    )(hidden, *blocks)
+        [whole((PAD, D))] * 2 + [pl.BlockSpec((1, tile), lambda t: (0, t))] + delta_specs(tile, lambda t: (0, t)),
+        [sds((PAD, D))] * 2 + [sds((1, width), F32)] + delta_shapes(width),
+        8 * PAD * D * width,
+        6 * D * width + 8 * PAD * D + 4 * PAD * width,
+        [pltpu.VMEM((PAD, D), F32)] * 2,
+    )(cot, *narrow_blocks, slope, hidden, normed_t, *wide_blocks)
 
 
 def resid_kernel(part, sib, resid, cot, vec, *rest):
@@ -545,99 +513,49 @@
     return total.astype(terms[0].dtype)
 
 
-def inward(values):
-    size = lax.axis_size("dp")
-    for s in range(size // 2 - 1):
-        moved = [along(value, [(s, s + 1), (size - 1 - s, size - 2 - s)]) for value in values]
-        values = [add(*pair) for pair in zip(values, moved)]
-    return values
-
-
-def across(values):
-    half = lax.axis_size("dp") // 2
-    moved = [along(value, [(half - 1, half), (half, half - 1)]) for value in values]
-    return [add(*pair) for pair in zip(values, moved)]
-
-
-def outward(values):
-    size = lax.axis_size("dp")
-    where = lax.axis_index("dp")
-    for s in reversed(range(size // 2 - 1)):
-        moved = [along(value, [(s + 1, s), (size - 2 - s, size - 1 - s)]) for value in values]
-        outer = (where == s) | (where == size - 1 - s)
-        values = [jnp.where(outer, new, value) for value, new in zip(values, moved)]
-    return values
-
-
-def along(self, value, pairs):
-        return self.permute(value, "dp", pairs, "dp")
-
-
-def swap(value, k):
-    return lax.ppermute(value, "row", [(i, i ^ k) for i in range(RB)])
-
-
-def after(value, *earlier):
-    return lax.optimization_barrier((value,) + earlier)[0]
-
-
-def sibling(part):
-    size = lax.axis_size("col")
-    if size == 2:
-        return lax.ppermute(part, "col", [(0, 1), (1, 0)])
-    total = None
-    for s in range(1, size):
-        term = lax.ppermute(part, "col", [(i, (i + s) % size) for i in range(size)]).astype(F32)
-        total = term if total is None else total + term
-    return total.astype(BF16)
-
-
-def col_gather(value):
-    size = lax.axis_size("col")
-    if size == 2:
-        other = lax.ppermute(value, "col", [(0, 1), (1, 0)])
-        first = lax.axis_index("col") == 0
-        return jnp.stack([jnp.where(first, value, other), jnp.where(first, other, value)], axis=-2)
-    return lax.all_gather(value, "col", axis=value.ndim - 1)
-
-
-def gather_far(links, near, axis, *earlier):
-    size = near[1].shape[axis] // 2
-    near_x, near_y = [after(block, *earlier) for block in near[1:3]] if earlier else near[1:3]
-    first = lax.slice_in_dim(near_x, 0, size, axis=axis)
-    second = lax.slice_in_dim(near_y, size, 2 * size, axis=axis)
-    return [links.swap(first, 2), links.swap(second, 1)]
-
-
-def add(*terms):
-    total = terms[0].astype(F32)
-    for term in terms[1:]:
-        total = total + term.astype(F32)
-    return total.astype(terms[0].dtype)
-
-
-def dp_sum(values, permute):
-    size = lax.axis_size("dp")
-    if size == 1:
+class Clock:
+    def __init__(self):
+        self.last = ()
+
+    def __call__(self, *values):
+        values = lax.optimization_barrier(tuple(values) + self.last)[: len(values)]
+        self.last = values[:1]
         return values
-    if size % 2:
-        return [lax.psum(value, "dp") for value in values]
-    half = size // 2
-    where = lax.axis_index("dp")
-    for s in range(half - 1):
-        moved = [permute(value, [(s, s + 1), (size - 1 - s, size - 2 - s)]) for value in values]
-        values = [add(*pair) for pair in zip(values, moved)]
-    moved = [permute(value, [(half - 1, half), (half, half - 1)]) for value in values]
-    values = [add(*pair) for pair in zip(values, moved)]
-    for s in reversed(range(half - 1)):
-        moved = [permute(value, [(s + 1, s), (size - 2 - s, size - 1 - s)]) for value in values]
-        outer = (where == s) | (where == size - 1 - s)
-        values = [jnp.where(outer, new, value) for value, new in zip(values, moved)]
-    return values
-
-
-def along(value, pairs):
-    return lax.ppermute(value, "dp", pairs)
+
+
+class LineSum:
+    def __init__(self, clock, value):
+        size = lax.axis_size("dp")
+        half = size // 2
+        inward = [(s, s + 1) for s in range(half - 1)]
+        self.clock = clock
+        self.value = value
+        if size % 2:
+            self.value = lax.psum(value, "dp")
+            self.steps = []
+            return
+        self.steps = [(None, [pair, (size - 1 - pair[0], size - 1 - pair[1])]) for pair in inward]
+        self.steps.append((None, [(half - 1, half), (half, half - 1)]))
+        for s, t in reversed(inward):
+            self.steps.append((s, [(t, s), (size - 1 - t, size - 1 - s)]))
+        self.send()
+
+    def send(self):
+        if self.steps:
+            self.moved = lax.ppermute(self.value, "dp", self.steps[0][1])
+
+    def advance(self):
+        if not self.steps:
+            return
+        moved = self.clock(self.moved)[0]
+        outer, pairs = self.steps.pop(0)
+        if outer is None:
+            self.value = add(self.value, moved)
+        else:
+            where = lax.axis_index("dp")
+            far = lax.axis_size("dp") - 1 - outer
+            self.value = jnp.where((where == outer) | (where == far), moved, self.value)
+        self.send()
 
 
 def first_sends(blocks):
@@ -690,10 +608,11 @@
     def padded(value):
         return jnp.pad(value.reshape(RB, SEQ, features), ((0, 0), (0, PAD - SEQ), (0, 0)))
 
-    def images_out(values):
+    def images_out(values, clock):
         mine = pick(values.reshape(-1, PAD, RB, columns, features), lax.axis_index("col"), 3)
         mine = mine[:, :SEQ]
-        got = jnp.stack([mine[:, :, 0]] + [swap(mine[:, :, k], k) for k in range(1, RB)])
+        sent = clock(*[swap(mine[:, :, k], k) for k in range(1, RB)])
+        got = jnp.stack([mine[:, :, 0], *sent])
         return jnp.concatenate([pick(got, row ^ j) for j in range(RB)], axis=1)
 
     vectors = jnp.stack([stretch, lifting, baseline, dilation, elevation, residue, residue, residue])
@@ -720,56 +639,73 @@
     blocks_n = afters(out[4:], *narrow_w[3:])
     came_n = first_sends(blocks_n)
 
-    out = backward_call(cot, narrow_w, slope, normed_two_t, wide_w)
-    part, thresholds_sum = out[:2]
-    blocks_w = out[2:]
-    terms_n = last_terms(blocks_n, afters(came_n, part))
-    last_n = last_sends(terms_n)
-    came_w = first_sends(afters(blocks_w, *terms_n))
-    out = resid_call(part, sibling(after(part, *came_n)), resid, cot, vec, attn_w)
-    grad_resid, grad_mixed, grad_t, sums_two = out
-    halves_n = jnp.concatenate(own_sums(blocks_n, came_n, afters(last_n, grad_mixed)))
-    sum_n = lax.psum(halves_n, "dp")
-    grads = attend_back_call(qkv, after(grad_mixed, halves_n), probs)
+    clock = Clock()
+    out = backward_call(cot, narrow_w, slope, hidden, normed_two_t, wide_w)
+    part, ffn_part, thresholds_sum = out[:3]
+    blocks_w = out[3:]
+    *came_n, part = clock(*came_n, part)
+    terms = last_terms(blocks_n, came_n)
+    last_n = last_sends(terms)
+    came_w = first_sends(afters(blocks_w, *terms))
+    grad_resid, grad_mixed, grad_t, sums_two = resid_call(part, sibling(part), resid, cot, vec, attn_w)
+    *last_n, grad_mixed = clock(*last_n, grad_mixed)
+    halves = jnp.concatenate(own_sums(blocks_n, came_n, last_n))
+    sum_n = LineSum(clock, halves)
+    grads = attend_back_call(qkv, after(grad_mixed, halves), probs)
     out = project_call(grads, normed_one_t, grad_t, mixed, attn_w)
     part, grad_sums = out[:2]
-    came_w = afters(came_w, part)
+    *came_w, part = clock(*came_w, part)
     terms = last_terms(blocks_w, came_w)
     last_w = last_sends(terms)
+    sum_n.advance()
     blocks_p = afters(out[2:], *terms)
     came_p = first_sends(blocks_p)
-    halves_w = own_sums(blocks_w, came_w, afters(last_w, part))
-    inner_w = inward([jnp.concatenate(halves_w)])
-    middle_w = across(inner_w)
-    widener_delta = outward(middle_w)[0].astype(F32)
-    ffn_part = narrow_call(after(hidden, *halves_w), narrow_w)
-    ffn_other = sibling(after(ffn_part, *inner_w))
-    delta, sums_one = tokens_call(part, after(sibling(part), *came_p, *inner_w), x, grad_resid, cot, vec)
+    last_w = clock(*last_w)
+    sum_w = LineSum(clock, jnp.concatenate(own_sums(blocks_w, came_w, last_w)))
+    other = sibling(after(part, *last_w))
+    sum_n.advance()
+    came_p = clock(*came_p)
     last_p = last_sends(last_terms(blocks_p, came_p))
+    other = clock(other)[0]
+    delta, sums_one = tokens_call(part, other, x, grad_resid, cot, vec)
+    sum_w.advance()
+    last_p = clock(*last_p)
     halves_p = own_sums(blocks_p, came_p, last_p)
+    sum_p = [LineSum(clock, halves_p[0])]
 
     featured = jnp.concatenate([sums_one[:2], sums_two[:4]]).reshape(6, RB, columns, features)
     featured = pick(featured, lax.axis_index("col"), 2)
     shared = jnp.concatenate([grad_sums[0, 0], grad_sums[2, 0], thresholds_sum[0]])
     pack = [jnp.concatenate([featured[:, k].reshape(-1), shared]) for k in range(RB)]
-    small = add(pack[0], *[swap(after(pack[k], *halves_p), k) for k in range(1, RB)]).astype(BF16)
+    sent = clock(*[swap(after(pack[k], *halves_p), k) for k in range(1, RB)])
+    small = add(pack[0], *sent).astype(BF16)
     size, line = small.shape[0], 4 * width
     lines = -(-size // (16 * line)) * 16
     small = jnp.pad(small, (0, lines * line - size)).reshape(lines, line)
-    inner_p = inward([halves_p[0], jnp.concatenate([halves_p[1], small])])
-    middle_p = across(inner_p)
-    first, second = outward(middle_p)
+    sum_p.append(LineSum(clock, jnp.concatenate([halves_p[1], small])))
+    ffn_other = sibling(after(ffn_part, *sent))
+    sum_n.advance()
+    sum_p[0].advance()
+    sum_w.advance()
+    sum_p[1].advance()
+    ffn_other = clock(ffn_other)[0]
+    ffn = ffn_part.astype(F32) + ffn_other.astype(F32) + vec[RESIDUE]
+    layer = (ffn + (resid - x.astype(F32))).astype(BF16)
+    sum_p[0].advance()
+    sum_p[1].advance()
+    outs = images_out(jnp.stack([layer, delta]), clock)
+    layer_output = outs[0] + tokens.astype(F32)
+    tokens_delta = outs[1] + cotangent.astype(F32)
+    for line_sum in (sum_n, sum_w, *sum_p):
+        while line_sum.steps:
+            line_sum.advance()
+    narrower_delta = sum_n.value.astype(F32).T
+    widener_delta = sum_w.value.astype(F32)
+    first, second = [line_sum.value for line_sum in sum_p]
     small = second[KB // 2 :].reshape(-1)[:size].astype(F32)
     total_p = jnp.concatenate([first, second[: KB // 2]]).astype(F32)
     projector_delta = jnp.stack([total_p[:, j * width : (j + 1) * width] for j in range(3)])
     combiner_delta = total_p[:, 3 * width :].T
-
-    ffn = ffn_part.astype(F32) + ffn_other.astype(F32) + vec[RESIDUE]
-    layer = (ffn + (resid - x.astype(F32))).astype(BF16)
-    outs = images_out(after(jnp.stack([layer, delta]), *inner_p))
-    layer_output = outs[0] + tokens.astype(F32)
-    tokens_delta = outs[1] + cotangent.astype(F32)
-    narrower_delta = after(sum_n, outs).astype(F32).T
 
     count = 6 * features
     vector = small[:count].reshape(6, features)

time: 401 us -> 371 us (0.925)
  waiting for transfers between devices: 142 us -> 111 us
  between operations: 15.3 us -> 1.91 us
  other arithmetic: 38.3 us -> 47.8 us
  starting transfers between devices: 57.1 us -> 64.8 us
    ppermute x9 -> x12, waiting for transfers between devices: 34.8 us -> 19.3 us  [send(): self.moved = lax.ppermute(self.value, 'dp', self.steps[0][1])]
    pallas_call x1 -> x0, Pallas kernels: 11.4 us -> none  [narrow_call(): call(narrow_kernel, (width // tile,), [pl.BlockSpec((PAD, tile), lambda t...]
    convert_element_type x15 -> x17, other arithmetic: 19.2 us -> 28.2 us  [add(): return total.astype(terms[0].dtype)]
    pallas_call x1, Pallas kernels: 20.2 us -> 28.3 us  [backward_call(): call(backward_kernel, (width // tile,), [whole((PAD, D))] + narrow_specs(...]
    ppermute x18, waiting for transfers between devices: 37.2 us -> 29.5 us  [swap(): return lax.ppermute(value, 'row', [(i, i ^ k) for i in range(RB)])]
    ppermute x9 -> x12, starting transfers between devices: 19.3 us -> 26.8 us  [send(): self.moved = lax.ppermute(self.value, 'dp', self.steps[0][1])]
    ppermute x18, waiting for transfers between devices: 69.5 us -> 62.2 us  [permute(): got = lax.ppermute(value, axis, pairs)]
    another operation x1 -> x5, local copies, waits for them, and re-layouts: 0.08 us -> 5.68 us  [the longest x4 5.59 us: per_device(): outs = images_out(jnp.stack([layer, delta]), clock)]
  transfers between devices with their start and end apart: 52 -> 54, of which waited for: 24 -> 21; matrix products, arithmetic and copies ran while one was open for 17% -> 21% of each run, Pallas kernels for 26% -> 27%
where the time goes in v3:
time: 371 us; the launch traced here: 366 us
  waiting for transfers between devices  111 us (30%)
  Pallas kernels  98.3 us (26%)
  starting transfers between devices  64.8 us (17%)
  other arithmetic  47.8 us (13%)
  local copies, waits for them, and re-layouts  42 us (11%)
    ppermute x18, waiting for transfers between devices, permute(): got = lax.ppermute(value, axis, pairs)  62.2 us
    ppermute x18, waiting for transfers between devices, swap(): return lax.ppermute(value, 'row', [(i, i ^ k) for i in range(RB)])  29.5 us
    pallas_call x1, Pallas kernels, backward_call(): call(backward_kernel, (width // tile,), [whole((PAD, D))] + narrow_specs(...  28.3 us
    convert_element_type x17, other arithmetic, add(): return total.astype(terms[0].dtype)  28.2 us
    ppermute x12, starting transfers between devices, send(): self.moved = lax.ppermute(self.value, 'dp', self.steps[0][1])  26.8 us
    ppermute x18, starting transfers between devices, swap(): return lax.ppermute(value, 'row', [(i, i ^ k) for i in range(RB)])  19.5 us
    ppermute x12, waiting for transfers between devices, send(): self.moved = lax.ppermute(self.value, 'dp', self.steps[0][1])  19.3 us
    ppermute x18, starting transfers between devices, permute(): got = lax.ppermute(value, axis, pairs)  18.3 us
  transfers between devices with their start and end apart: 54, of which 21 were waited for; matrix products, arithmetic and copies ran while one was open for 21% of the time, Pallas kernels for 27%

profile of v3, /device:TPU:0, one launch (start us, length us, event | category | flops | bytes accessed | tf_op | source)
XLA Modules:
  0.0 365.8 jit_solution(5597481309779960516)
XLA Ops:
  3.2 2.9 collective-permute-start
  8.6 4.9 %collective-permute-done = bf16[2,592,128]{2,1,0:T(8,128)(2,1)} collective-permute-done((bf16[2,592,128]{2,1,0:T(8,128)(2,1)S(1)}, bf16[2,592,128]{2,1,0:T(8,128)(2,1)}, u32[]{:S(2)}, u32[]{:S(2)}) %collective-permute-start) | collective-permute-done | bytes 303136 | tf_op jit(solution)/shard_map/ppermute | solution.py:462
  18.4 5.8 %collective-permute-done.6 = f32[8,128]{1,0:T(8,128)S(1)} collective-permute-done((f32[8,128]{1,0:T(8,128)S(1)}, f32[8,128]{1,0:T(8,128)S(1)}, u32[]{:S(2)}, u32[]{:S(2)}) %collective-permute-start.6) | collective-permute-done | bytes 4128 | tf_op jit(solution)/shard_map/ppermute | solution.py:462
  30.2 18.6 %collective-permute-done.18 = f32[8,128]{1,0:T(8,128)S(1)} collective-permute-done((f32[8,128]{1,0:T(8,128)S(1)}, f32[8,128]{1,0:T(8,128)S(1)}, u32[]{:S(2)}, u32[]{:S(2)}) %collective-permute-start.18) | collective-permute-done | bytes 4128 | tf_op jit(solution)/shard_map/ppermute | solution.py:462
  52.7 17.5 %collective-permute-done.13.rest_2_.rest_10_ = bf16[256,2048]{1,0:T(8,128)(2,1)} collective-permute-done((bf16[256,2048]{1,0:T(8,128)(2,1)}, bf16[256,2048]{1,0:T(8,128)(2,1)}, u32[]{:S(2)}, u32[]{:S(2)}) %collective-permute-start.13) | collective-permute-done | bytes 1048608 | tf_op jit(solution)/shard_map/ppermute | solution.py:462
  72.1 3.1 collective-permute-done.12.rest_1_.rest_9_
  78.5 2.8 collective-permute-done.10.rest_3_
  81.3 5.0 %collective-permute-done.8.rest_4_ = bf16[4,128,512]{2,1,0:T(8,128)(2,1)S(1)} collective-permute-done((bf16[4,128,512]{2,1,0:T(8,128)(2,1)S(1)}, bf16[4,128,512]{2,1,0:T(8,128)(2,1)S(1)}, u32[]{:S(2)}, u32[]{:S(2)}) %collective-permute-start.8) | collective-permute-done | bytes 524320 | tf_op jit(solution)/shard_map/ppermute | solution.py:462
  92.5 6.8 %shard_map.245 = (bf16[1024,592]{1,0:T(8,128)(2,1)}, bf16[592,1536]{1,0:T(8,128)(2,1)}) custom-call(bf16[592,1024]{1,0:T(8,128)(2,1)} %squeeze.68.x, f32[8,1024]{1,0:T(8,128)} %bitcast.101, bf16[4,256,512]{2,1,0:T(8,128)(2,1)} %copy-done.1, bf16[4,256,512]{2,1,0:T(8,128)(2,1)} %copy-done.3, bf16[4,256,512]{2,1,0:T(8,128)(2,1)} %copy-done.2, ...), custom_call_target="tpu_custom_call" | custom-call | flops 29097984 | bytes 115456 | tf_op jit(solution)/shard_map/pallas_call | solution.py:111
  99.3 9.2 %shard_map.246 = (bf16[592,512]{1,0:T(8,128)(2,1)}, bf16[8,592,592]{2,1,0:T(8,128)(2,1)}) custom-call(bf16[592,1536]{1,0:T(8,128)(2,1)} %get-tuple-element.131.q.k.v, bf16[592,1536]{1,0:T(8,128)(2,1)} %get-tuple-element.131.q.k.v, bf16[592,1536]{1,0:T(8,128)(2,1)} %get-tuple-element.131.q.k.v), custom_call_target="tpu_custom_call" | custom-call | flops 22429696 | bytes 87616 | tf_op jit(solution)/shard_map/pallas_call | solution.py:152
  108.4 3.2 shard_map.247.part
  111.7 2.8 collective-permute-done.9.rest_1_
  123.2 14.8 %shard_map.248 = (f32[592,1024]{1,0:T(8,128)}, bf16[1024,592]{1,0:T(8,128)(2,1)}, bf16[592,2048]{1,0:T(8,128)(2,1)}, bf16[592,2048]{1,0:T(8,128)(2,1)}, bf16[256...) custom-call(bf16[592,1024]{1,0:T(8,128)(2,1)} %squeeze.68.x, ...), custom_call_target="tpu_custom_call" | custom-call | flops 77594624 | bytes 339456 | tf_op jit(solution)/shard_map/pallas_call | solution.py:239
  140.9 28.3 %shard_map.249 = (bf16[592,1024]{1,0:T(8,128)(2,1)}, bf16[592,1024]{1,0:T(8,128)(2,1)}, f32[1,2048]{1,0:T(1,128)}, bf16[256,2048]{1,0:T(8,128)(2,1)}, bf16[256,2...) custom-call(bf16[592,1024]{1,0:T(8,128)(2,1)} %squeeze.67.rest_6_.cot, ...), custom_call_target="tpu_custom_call" | custom-call | flops 155189248 | bytes 348160 | tf_op jit(solution)/shard_map/pallas_call | solution.py:300
  177.8 7.4 %shard_map.250 = (f32[592,1024]{1,0:T(8,128)}, bf16[592,512]{1,0:T(8,128)(2,1)}, bf16[1024,592]{1,0:T(8,128)(2,1)}, f32[8,1024]{1,0:T(8,128)}) custom-call(bf16[592,1024]{1,0:T(8,128)(2,1)} %get-tuple-element.153.part, bf16[592,1024]{1,0:T(8,128)(2,1)} %copy-done.16, f32[592,1024]{1,0:T(8,128)} %get-tuple-element.154.resid, ...), custom_call_target="tpu_custom_call" | custom-call | flops 9699328 | bytes 177408 | tf_op jit(solution)/shard_map/pallas_call | solution.py:338
  190.7 3.2 collective-permute-start.30
  193.9 11.7 %shard_map.251 = (bf16[592,512]{1,0:T(8,128)(2,1)}, bf16[592,512]{1,0:T(8,128)(2,1)}, bf16[592,512]{1,0:T(8,128)(2,1)}) custom-call(bf16[592,1536]{1,0:T(8,128)(2,1)} %get-tuple-element.131.q.k.v, bf16[592,1536]{1,0:T(8,128)(2,1)} %get-tuple-element.131.q.k.v, bf16[592,1536]{1,0:T(8,128)(2,1)} %get-tuple-element.131.q.k.v, ...), custom_call_target="tpu_custom_call" | custom-call | flops 44859392 | bytes 87616 | tf_op jit(solution)/shard_map/pallas_call | solution.py:379
  205.6 10.5 %shard_map.252 = (bf16[592,1024]{1,0:T(8,128)(2,1)}, f32[3,1,512]{2,1,0:T(1,128)}, bf16[256,2048]{1,0:T(8,128)(2,1)}, bf16[256,2048]{1,0:T(8,128)(2,1)}, bf16[25...) custom-call(bf16[592,512]{1,0:T(8,128)(2,1)} %get-tuple-element.163.gq, ...), custom_call_target="tpu_custom_call" | custom-call | flops 67895296 | bytes 216320 | tf_op jit(solution)/shard_map/pallas_call | solution.py:419
  224.2 8.3 %collective-permute-done.28 = bf16[128,2048]{1,0:T(8,128)(2,1)S(1)} collective-permute-done((bf16[128,2048]{1,0:T(8,128)(2,1)S(1)}, bf16[128,2048]{1,0:T(8,128)(2,1)S(1)}, u32[]{:S(2)}, u32[]{:S(2)}) %collective-permute-start.28) | collective-permute-done | bytes 524320 | tf_op jit(solution)/shard_map/ppermute | solution.py:474
  232.5 2.7 collective-permute-done.29
  240.5 10.9 %collective-permute-done.32 = bf16[256,2048]{1,0:T(8,128)(2,1)S(1)} collective-permute-done((bf16[256,2048]{1,0:T(8,128)(2,1)S(1)}, bf16[256,2048]{1,0:T(8,128)(2,1)S(1)}, u32[]{:S(2)}, u32[]{:S(2)}) %collective-permute-start.32) | collective-permute-done | bytes 1048608 | tf_op jit(solution)/shard_map/ppermute | solution.py:474
  261.7 6.4 %shard_map.253 = (bf16[592,1024]{1,0:T(8,128)(2,1)}, f32[8,1024]{1,0:T(8,128)}) custom-call(bf16[592,1024]{1,0:T(8,128)(2,1)} %get-tuple-element.177.part, bf16[592,1024]{1,0:T(8,128)(2,1)} %copy-done.13, bf16[592,1024]{1,0:T(8,128)(2,1)} %squeeze.68.x, f32[592,1024]{1,0:T(8,128)} %get-tuple-element.185.grad_resid, bf16[592,1024]{1,0:T(8,128)(2,1)} %squeeze.67.rest_6_.cot, ...), custom_call_target="tpu_custom_call" | custom-call | flops 189440 | bytes 132608 | tf_op jit(solution)/shard_map/pallas_call | solution.py:443
  274.6 2.6 add_convert_fusion.3
  278.9 3.4 stack.144
  283.4 8.2 %collective-permute-start.44 = (bf16[128,2048]{1,0:T(8,128)(2,1)S(1)}, bf16[128,2048]{1,0:T(8,128)(2,1)}, u32[]{:S(2)}, u32[]{:S(2)}) collective-permute-start(bf16[128,2048]{1,0:T(8,128)(2,1)S(1)} %get-tuple-element.277), channel_id=1, source_target_pairs={{0,8},{24,16},{1,9},{25,17},{2,10},{26,18},{3,11},{27,19},{4,12},{... | collective-permute-start | bytes 1572872 | tf_op jit(solution)/shard_map/ppermute | solution.py:545
  297.9 4.8 %collective-permute-done.44 = bf16[128,2048]{1,0:T(8,128)(2,1)} collective-permute-done((bf16[128,2048]{1,0:T(8,128)(2,1)S(1)}, bf16[128,2048]{1,0:T(8,128)(2,1)}, u32[]{:S(2)}, u32[]{:S(2)}) %collective-permute-start.44) | collective-permute-done | bytes 524320 | tf_op jit(solution)/shard_map/ppermute | solution.py:545
  306.2 3.0 collective-permute-done.42
  316.2 2.6 add_convert_fusion
  334.5 8.4 %concatenate.48 = bf16[2,2308,128]{2,1,0:T(8,128)(2,1)S(1)} concatenate(bf16[2,577,128]{2,1,0:T(8,128)(2,1)} %get-tuple-element.273, bf16[2,577,128]{2,1,0:T(8,128)(2,1)} %get-tuple-element.272, bf16[2,577,128]{2,1,0:T(8,128)(2,1)} %get-tuple-element.271, bf16[2,577,128]{2,1,0:T(8,128)(2,1)} %get-tuple-element.270), dimensions={1} | concatenate | bytes 2363392 | tf_op jit(solution)/shard_map/concatenate | solution.py:616
  344.6 2.7 select_convert_fusion
  347.3 6.3 %collective-permute-done.51 = bf16[128,2048]{1,0:T(8,128)(2,1)} collective-permute-done((bf16[128,2048]{1,0:T(8,128)(2,1)}, bf16[128,2048]{1,0:T(8,128)(2,1)}, u32[]{:S(2)}, u32[]{:S(2)}) %collective-permute-start.51) | collective-permute-done | bytes 524320 | tf_op jit(solution)/shard_map/ppermute | solution.py:545
  354.7 5.2 %collective-permute-done.53 = bf16[144,2048]{1,0:T(8,128)(2,1)} collective-permute-done((bf16[144,2048]{1,0:T(8,128)(2,1)}, bf16[144,2048]{1,0:T(8,128)(2,1)}, u32[]{:S(2)}, u32[]{:S(2)}) %collective-permute-start.53) | collective-permute-done | bytes 589856 | tf_op jit(solution)/shard_map/ppermute | solution.py:545
  (260 shorter events, 130.2 us)
Async XLA Ops:
  14.9 33.8 %collective-permute-start.5 = (bf16[4,256,512]{2,1,0:T(8,128)(2,1)S(1)}, bf16[4,256,512]{2,1,0:T(8,128)(2,1)S(1)}, u32[]{:S(2)}, u32[]{:S(2)}) collective-permute-start(bf16[4,256,512]{2,1,0:T(8,128)(2,1)S(1)} %pad_maximum_fusion.4.rest_0_), channel_id=1, source_target_pairs={{0,4},{2,6},{4,0},{6,2},{1,5},{3,7},{5,1},{7,3},{8,12},{10,14},{12... | collective-permute-start | bytes 3145736 | tf_op jit(solution)/shard_map/ppermute | solution.py:462
  24.2 24.8 %collective-permute-start.7 = (bf16[4,256,512]{2,1,0:T(8,128)(2,1)S(1)}, bf16[4,256,512]{2,1,0:T(8,128)(2,1)S(1)}, u32[]{:S(2)}, u32[]{:S(2)}) collective-permute-start(bf16[4,256,512]{2,1,0:T(8,128)(2,1)S(1)} %pad_maximum_fusion.4.rest_0_), channel_id=1, source_target_pairs={{0,2},{2,0},{4,6},{6,4},{1,3},{3,1},{5,7},{7,5},{8,10},{10,8},{12,... | collective-permute-start | bytes 3145736 | tf_op jit(solution)/shard_map/ppermute | solution.py:462
  27.6 59.6 %collective-permute-start.3 = (bf16[2,592,4,128]{3,1,0,2:T(8,128)(2,1)}, bf16[2,592,4,128]{3,1,0,2:T(8,128)(2,1)}, u32[]{:S(2)}, u32[]{:S(2)}) collective-permute-start(bf16[2,592,4,128]{3,1,0,2:T(8,128)(2,1)} %pad_maximum_fusion.2), channel_id=1, source_target_pairs={{0,1},{1,0},{2,3},{3,2},{4,5},{5,4},{6,7},{7,6},{8,9},{9,8},{10,11... | collective-permute-start | bytes 3637256 | tf_op jit(solution)/shard_map/ppermute | solution.py:495
  27.6 21.2 %collective-permute-start.18 = (f32[8,128]{1,0:T(8,128)S(1)}, f32[8,128]{1,0:T(8,128)S(1)}, u32[]{:S(2)}, u32[]{:S(2)}) collective-permute-start(f32[8,128]{1,0:T(8,128)S(1)} %stack.133), channel_id=1, source_target_pairs={{0,6},{2,4},{4,2},{6,0},{1,7},{3,5},{5,3},{7,1},{8,14},{10,12},{12... | collective-permute-start | bytes 12296 | tf_op jit(solution)/shard_map/ppermute | solution.py:462
  29.7 40.5 %collective-permute-start.13 = (bf16[256,2048]{1,0:T(8,128)(2,1)}, bf16[256,2048]{1,0:T(8,128)(2,1)}, u32[]{:S(2)}, u32[]{:S(2)}) collective-permute-start(bf16[256,2048]{1,0:T(8,128)(2,1)} %rest_8_.1), channel_id=1, source_target_pairs={{0,4},{2,6},{4,0},{6,2},{1,5},{3,7},{5,1},{7,3},{8,12},{10,14},{12... | collective-permute-start | bytes 3145736 | tf_op jit(solution)/shard_map/ppermute | solution.py:462
  48.7 26.4 %collective-permute-start.12 = (bf16[256,2048]{1,0:T(8,128)(2,1)}, bf16[256,2048]{1,0:T(8,128)(2,1)}, u32[]{:S(2)}, u32[]{:S(2)}) collective-permute-start(bf16[256,2048]{1,0:T(8,128)(2,1)} %rest_8_.1), channel_id=1, source_target_pairs={{0,2},{2,0},{4,6},{6,4},{1,3},{3,1},{5,7},{7,5},{8,10},{10,8},{12,... | collective-permute-start | bytes 3145736 | tf_op jit(solution)/shard_map/ppermute | solution.py:462
  49.1 32.3 %collective-permute-start.10 = (bf16[4,128,512]{2,1,0:T(8,128)(2,1)S(1)}, bf16[4,128,512]{2,1,0:T(8,128)(2,1)S(1)}, u32[]{:S(2)}, u32[]{:S(2)}) collective-permute-start(bf16[4,128,512]{2,1,0:T(8,128)(2,1)S(1)} %slice.256), channel_id=1, source_target_pairs={{0,4},{2,6},{4,0},{6,2},{1,5},{3,7},{5,1},{7,3},{8,12},{10,14},{12... | collective-permute-start | bytes 1572872 | tf_op jit(solution)/shard_map/ppermute | solution.py:462
  50.0 36.3 %collective-permute-start.8 = (bf16[4,128,512]{2,1,0:T(8,128)(2,1)S(1)}, bf16[4,128,512]{2,1,0:T(8,128)(2,1)S(1)}, u32[]{:S(2)}, u32[]{:S(2)}) collective-permute-start(bf16[4,128,512]{2,1,0:T(8,128)(2,1)S(1)} %slice.255), channel_id=1, source_target_pairs={{0,2},{2,0},{4,6},{6,4},{1,3},{3,1},{5,7},{7,5},{8,10},{10,8},{12,... | collective-permute-start | bytes 1572872 | tf_op jit(solution)/shard_map/ppermute | solution.py:462
  77.0 34.6 %collective-permute-start.14 = (bf16[128,2048]{1,0:T(8,128)(2,1)}, bf16[128,2048]{1,0:T(8,128)(2,1)}, u32[]{:S(2)}, u32[]{:S(2)}) collective-permute-start(bf16[128,2048]{1,0:T(8,128)(2,1)} %slice.258), channel_id=1, source_target_pairs={{0,4},{2,6},{4,0},{6,2},{1,5},{3,7},{5,1},{7,3},{8,12},{10,14},{12... | collective-permute-start | bytes 1572872 | tf_op jit(solution)/shard_map/ppermute | solution.py:462
  77.0 34.6 %collective-permute-start.16 = (bf16[128,2048]{1,0:T(8,128)(2,1)}, bf16[128,2048]{1,0:T(8,128)(2,1)S(1)}, u32[]{:S(2)}, u32[]{:S(2)}) collective-permute-start(bf16[128,2048]{1,0:T(8,128)(2,1)} %slice.260), channel_id=1, source_target_pairs={{0,2},{2,0},{4,6},{6,4},{1,3},{3,1},{5,7},{7,5},{8,10},{10,8},{12,... | collective-permute-start | bytes 1572872 | tf_op jit(solution)/shard_map/ppermute | solution.py:462
  86.3 28.2 %collective-permute-start.9 = (bf16[2048,256]{1,0:T(8,128)(2,1)}, bf16[2048,256]{1,0:T(8,128)(2,1)}, u32[]{:S(2)}, u32[]{:S(2)}) collective-permute-start(bf16[2048,256]{1,0:T(8,128)(2,1)} %rest_0_.3), channel_id=1, source_target_pairs={{0,2},{2,0},{4,6},{6,4},{1,3},{3,1},{5,7},{7,5},{8,10},{10,8},{12,... | collective-permute-start | bytes 3145736 | tf_op jit(solution)/shard_map/ppermute | solution.py:462
  86.3 31.5 %collective-permute-start.11 = (bf16[2048,256]{1,0:T(8,128)(2,1)}, bf16[2048,256]{1,0:T(8,128)(2,1)}, u32[]{:S(2)}, u32[]{:S(2)}) collective-permute-start(bf16[2048,256]{1,0:T(8,128)(2,1)} %rest_0_.3), channel_id=1, source_target_pairs={{0,4},{2,6},{4,0},{6,2},{1,5},{3,7},{5,1},{7,3},{8,12},{10,14},{12... | collective-permute-start | bytes 3145736 | tf_op jit(solution)/shard_map/ppermute | solution.py:462
  116.4 21.7 %collective-permute-start.15 = (bf16[2048,128]{1,0:T(8,128)(2,1)}, bf16[2048,128]{1,0:T(8,128)(2,1)S(1)}, u32[]{:S(2)}, u32[]{:S(2)}) collective-permute-start(bf16[2048,128]{1,0:T(8,128)(2,1)} %slice.257), channel_id=1, source_target_pairs={{0,4},{2,6},{4,0},{6,2},{1,5},{3,7},{5,1},{7,3},{8,12},{10,14},{12... | collective-permute-start | bytes 1572872 | tf_op jit(solution)/shard_map/ppermute | solution.py:462
  119.7 18.4 %collective-permute-start.17 = (bf16[2048,128]{1,0:T(8,128)(2,1)}, bf16[2048,128]{1,0:T(8,128)(2,1)}, u32[]{:S(2)}, u32[]{:S(2)}) collective-permute-start(bf16[2048,128]{1,0:T(8,128)(2,1)} %slice.259), channel_id=1, source_target_pairs={{0,2},{2,0},{4,6},{6,4},{1,3},{3,1},{5,7},{7,5},{8,10},{10,8},{12,... | collective-permute-start | bytes 1572872 | tf_op jit(solution)/shard_map/ppermute | solution.py:462
  138.9 30.4 %collective-permute-start.22 = (bf16[256,2048]{1,0:T(8,128)(2,1)}, bf16[256,2048]{1,0:T(8,128)(2,1)S(1)}, u32[]{:S(2)}, u32[]{:S(2)}) collective-permute-start(bf16[256,2048]{1,0:T(8,128)(2,1)} %get-tuple-element.144), channel_id=1, source_target_pairs={{0,4},{2,6},{4,0},{6,2},{1,5},{3,7},{5,1},{7,3},{8,12},{10,14},{12... | collective-permute-start | bytes 3145736 | tf_op jit(solution)/shard_map/ppermute | solution.py:474
  139.8 29.5 %collective-permute-start.21 = (bf16[256,2048]{1,0:T(8,128)(2,1)}, bf16[256,2048]{1,0:T(8,128)(2,1)S(1)}, u32[]{:S(2)}, u32[]{:S(2)}) collective-permute-start(bf16[256,2048]{1,0:T(8,128)(2,1)} %get-tuple-element.142), channel_id=1, source_target_pairs={{0,2},{2,0},{4,6},{6,4},{1,3},{3,1},{5,7},{7,5},{8,10},{10,8},{12,... | collective-permute-start | bytes 3145736 | tf_op jit(solution)/shard_map/ppermute | solution.py:474
  174.7 41.5 %collective-permute-start.23 = (bf16[256,2048]{1,0:T(8,128)(2,1)}, bf16[256,2048]{1,0:T(8,128)(2,1)}, u32[]{:S(2)}, u32[]{:S(2)}) collective-permute-start(bf16[256,2048]{1,0:T(8,128)(2,1)} %get-tuple-element.150), channel_id=1, source_target_pairs={{0,2},{2,0},{4,6},{6,4},{1,3},{3,1},{5,7},{7,5},{8,10},{10,8},{12,... | collective-permute-start | bytes 3145736 | tf_op jit(solution)/shard_map/ppermute | solution.py:474
  176.2 40.0 %collective-permute-start.24 = (bf16[256,2048]{1,0:T(8,128)(2,1)}, bf16[256,2048]{1,0:T(8,128)(2,1)}, u32[]{:S(2)}, u32[]{:S(2)}) collective-permute-start(bf16[256,2048]{1,0:T(8,128)(2,1)} %get-tuple-element.152), channel_id=1, source_target_pairs={{0,4},{2,6},{4,0},{6,2},{1,5},{3,7},{5,1},{7,3},{8,12},{10,14},{12... | collective-permute-start | bytes 3145736 | tf_op jit(solution)/shard_map/ppermute | solution.py:474
  190.7 32.3 %collective-permute-start.30 = (bf16[256,2048]{1,0:T(8,128)(2,1)S(1)}, bf16[256,2048]{1,0:T(8,128)(2,1)S(1)}, u32[]{:S(2)}, u32[]{:S(2)}) collective-permute-start(bf16[256,2048]{1,0:T(8,128)(2,1)S(1)} %pad_maximum_fusion.5), channel_id=1, source_target_pairs={{0,8},{24,16},{1,9},{25,17},{2,10},{26,18},{3,11},{27,19},{4,12},{... | collective-permute-start | bytes 3145736 | tf_op jit(solution)/shard_map/ppermute | solution.py:545
  221.8 29.5 %collective-permute-start.32 = (bf16[256,2048]{1,0:T(8,128)(2,1)S(1)}, bf16[256,2048]{1,0:T(8,128)(2,1)S(1)}, u32[]{:S(2)}, u32[]{:S(2)}) collective-permute-start(bf16[256,2048]{1,0:T(8,128)(2,1)S(1)} %copy-done.42), channel_id=1, source_target_pairs={{0,2},{2,0},{4,6},{6,4},{1,3},{3,1},{5,7},{7,5},{8,10},{10,8},{12,... | collective-permute-start | bytes 3145736 | tf_op jit(solution)/shard_map/ppermute | solution.py:474
  222.4 31.4 %collective-permute-start.33 = (bf16[256,2048]{1,0:T(8,128)(2,1)S(1)}, bf16[256,2048]{1,0:T(8,128)(2,1)S(1)}, u32[]{:S(2)}, u32[]{:S(2)}) collective-permute-start(bf16[256,2048]{1,0:T(8,128)(2,1)S(1)} %copy-done.41), channel_id=1, source_target_pairs={{0,4},{2,6},{4,0},{6,2},{1,5},{3,7},{5,1},{7,3},{8,12},{10,14},{12... | collective-permute-start | bytes 3145736 | tf_op jit(solution)/shard_map/ppermute | solution.py:474
  238.0 30.8 %collective-permute-start.37 = (bf16[256,2048]{1,0:T(8,128)(2,1)}, bf16[256,2048]{1,0:T(8,128)(2,1)}, u32[]{:S(2)}, u32[]{:S(2)}) collective-permute-start(bf16[256,2048]{1,0:T(8,128)(2,1)} %pad_maximum_fusion.6), channel_id=1, source_target_pairs={{0,8},{24,16},{1,9},{25,17},{2,10},{26,18},{3,11},{27,19},{4,12},{... | collective-permute-start | bytes 3145736 | tf_op jit(solution)/shard_map/ppermute | solution.py:545
  240.4 20.3 %collective-permute-start.31 = (bf16[592,1024]{1,0:T(8,128)(2,1)S(1)}, bf16[592,1024]{1,0:T(8,128)(2,1)S(1)}, u32[]{:S(2)}, u32[]{:S(2)}) collective-permute-start(bf16[592,1024]{1,0:T(8,128)(2,1)S(1)} %copy-done.12), channel_id=1, source_target_pairs={{0,1},{1,0},{2,3},{3,2},{4,5},{5,4},{6,7},{7,6},{8,9},{9,8},{10,11... | collective-permute-start | bytes 3637256 | tf_op jit(solution)/shard_map/ppermute | solution.py:484
  259.2 35.5 %collective-permute-start.45 = (bf16[256,2048]{1,0:T(8,128)(2,1)}, bf16[256,2048]{1,0:T(8,128)(2,1)}, u32[]{:S(2)}, u32[]{:S(2)}) collective-permute-start(bf16[256,2048]{1,0:T(8,128)(2,1)} %add_convert_fusion.2), channel_id=1, source_target_pairs={{8,0},{16,24},{9,1},{17,25},{10,2},{18,26},{11,3},{19,27},{12,4},{... | collective-permute-start | bytes 3145736 | tf_op jit(solution)/shard_map/ppermute | solution.py:545
  272.7 19.0 %collective-permute-start.39 = (f32[3840]{0:T(1024)S(1)}, f32[3840]{0:T(1024)S(1)}, u32[]{:S(2)}, u32[]{:S(2)}) collective-permute-start(f32[3840]{0:T(1024)S(1)} %get-tuple-element.202), channel_id=1, source_target_pairs={{0,4},{2,6},{4,0},{6,2},{1,5},{3,7},{5,1},{7,3},{8,12},{10,14},{12... | collective-permute-start | bytes 46088 | tf_op jit(solution)/shard_map/ppermute | solution.py:474
  273.2 18.4 %collective-permute-start.40 = (f32[3840]{0:T(1024)S(1)}, f32[3840]{0:T(1024)S(1)}, u32[]{:S(2)}, u32[]{:S(2)}) collective-permute-start(f32[3840]{0:T(1024)S(1)} %get-tuple-element.203), channel_id=1, source_target_pairs={{0,6},{2,4},{4,2},{6,0},{1,7},{3,5},{5,3},{7,1},{8,14},{10,12},{12... | collective-permute-start | bytes 46088 | tf_op jit(solution)/shard_map/ppermute | solution.py:474
  277.2 29.0 %collective-permute-start.43 = (bf16[256,2048]{1,0:T(8,128)(2,1)}, bf16[256,2048]{1,0:T(8,128)(2,1)}, u32[]{:S(2)}, u32[]{:S(2)}) collective-permute-start(bf16[256,2048]{1,0:T(8,128)(2,1)} %add_convert_fusion.3), channel_id=1, source_target_pairs={{8,16},{16,8},{9,17},{17,9},{10,18},{18,10},{11,19},{19,11},{12,20... | collective-permute-start | bytes 3145736 | tf_op jit(solution)/shard_map/ppermute | solution.py:545
  283.4 19.3 %collective-permute-start.44 = (bf16[128,2048]{1,0:T(8,128)(2,1)S(1)}, bf16[128,2048]{1,0:T(8,128)(2,1)}, u32[]{:S(2)}, u32[]{:S(2)}) collective-permute-start(bf16[128,2048]{1,0:T(8,128)(2,1)S(1)} %get-tuple-element.277), channel_id=1, source_target_pairs={{0,8},{24,16},{1,9},{25,17},{2,10},{26,18},{3,11},{27,19},{4,12},{... | collective-permute-start | bytes 1572872 | tf_op jit(solution)/shard_map/ppermute | solution.py:545
  294.7 21.5 %collective-permute-start.41 = (bf16[592,1024]{1,0:T(8,128)(2,1)}, bf16[592,1024]{1,0:T(8,128)(2,1)}, u32[]{:S(2)}, u32[]{:S(2)}) collective-permute-start(bf16[592,1024]{1,0:T(8,128)(2,1)} %get-tuple-element.207), channel_id=1, source_target_pairs={{0,1},{1,0},{2,3},{3,2},{4,5},{5,4},{6,7},{7,6},{8,9},{9,8},{10,11... | collective-permute-start | bytes 3637256 | tf_op jit(solution)/shard_map/ppermute | solution.py:484
  314.9 29.7 %collective-permute-start.52 = (bf16[256,2048]{1,0:T(8,128)(2,1)S(1)}, bf16[256,2048]{1,0:T(8,128)(2,1)}, u32[]{:S(2)}, u32[]{:S(2)}) collective-permute-start(bf16[256,2048]{1,0:T(8,128)(2,1)S(1)} %add_convert_fusion.1), channel_id=1, source_target_pairs={{8,0},{16,24},{9,1},{17,25},{10,2},{18,26},{11,3},{19,27},{12,4},{... | collective-permute-start | bytes 3145736 | tf_op jit(solution)/shard_map/ppermute | solution.py:545
  326.9 26.7 %collective-permute-start.51 = (bf16[128,2048]{1,0:T(8,128)(2,1)}, bf16[128,2048]{1,0:T(8,128)(2,1)}, u32[]{:S(2)}, u32[]{:S(2)}) collective-permute-start(bf16[128,2048]{1,0:T(8,128)(2,1)} %add_convert_fusion.7), channel_id=1, source_target_pairs={{8,0},{16,24},{9,1},{17,25},{10,2},{18,26},{11,3},{19,27},{12,4},{... | collective-permute-start | bytes 1572872 | tf_op jit(solution)/shard_map/ppermute | solution.py:545
  330.3 29.5 %collective-permute-start.53 = (bf16[144,2048]{1,0:T(8,128)(2,1)}, bf16[144,2048]{1,0:T(8,128)(2,1)}, u32[]{:S(2)}, u32[]{:S(2)}) collective-permute-start(bf16[144,2048]{1,0:T(8,128)(2,1)} %add_convert_fusion.5), channel_id=1, source_target_pairs={{8,0},{16,24},{9,1},{17,25},{10,2},{18,26},{11,3},{19,27},{12,4},{... | collective-permute-start | bytes 1769480 | tf_op jit(solution)/shard_map/ppermute | solution.py:545
  (65 other events, 612.2 us)

commit v4 on v3

--- a/solution.py
+++ b/solution.py
@@ -11,6 +11,9 @@
 PAD = 592
 RB = 4
 KB = D // RB
+PLANE = 96
+SHARED = 80
+TOP = 304
 
 NORM_EPSILON = 1e-05
 SIGMOID_SLOPE = 1.702
@@ -60,6 +63,27 @@
     )
 
 
+PIECES = (TOP, PAD - TOP)
+
+
+def piece_specs():
+    return [pl.BlockSpec((rows, D), lambda *step: (0, 0)) for rows in PIECES]
+
+
+def piece_shapes():
+    return [sds((rows, D)) for rows in PIECES]
+
+
+def store_pieces(refs, value):
+    refs[0][...] = value[:TOP].astype(BF16)
+    refs[1][...] = value[TOP:].astype(BF16)
+
+
+def load_sum(pieces):
+    top, bottom, other_top, other_bottom = [piece[...].astype(F32) for piece in pieces]
+    return jnp.concatenate([top + other_top, bottom + other_bottom], axis=0)
+
+
 def row_mask(shape):
     return lax.broadcasted_iota(jnp.int32, shape, 0) < SEQ
 
@@ -80,7 +104,7 @@
 
 
 def qkv_kernel(x, vec, *rest):
-    weights, (bias, normed_t, qkv, normed) = rest[:5], rest[5:]
+    weights, (bias, normed_t, qkv, normed, buffer) = rest[:9], rest[9:]
 
     @pl.when(pl.program_id(0) == 0)
     def _():
@@ -90,35 +114,55 @@
         normed_t[...] = value.T.astype(BF16)
 
     total = bias[0]
-    for k, w in enumerate(joined(weights)):
+    for k, w in enumerate(joined(weights, buffer)):
         total = total + mm(normed[:, k * KB : (k + 1) * KB], w)
     qkv[...] = total.astype(BF16)
 
 
-def attn_specs(width, at):
-    full = pl.BlockSpec((1, KB, width), lambda j: (at(j), 0, 0))
-    half = pl.BlockSpec((1, KB // 2, width), lambda j: (at(j), 0, 0))
-    return [full] * 3 + [half] * 2
-
-
-def joined(weights):
-    blocks = [w[...].reshape(w.shape[-2:]) for w in weights]
-    return blocks[:3] + [jnp.concatenate(blocks[3:], axis=0)]
+BLOCK_ROWS = (KB, PLANE + SHARED, PLANE + SHARED, PLANE, SHARED, SHARED, SHARED, SHARED)
+
+
+def weight_specs(tile, at):
+    pieces = [pl.BlockSpec((rows, tile), lambda *step: (0, at(*step))) for rows in BLOCK_ROWS]
+    return [pl.BlockSpec(memory_space=pltpu.SMEM)] + pieces
+
+
+def plain_specs(tile, at):
+    half = pl.BlockSpec((KB // 2, tile), lambda *step: (0, at(*step)))
+    return [pl.BlockSpec((KB, tile), lambda *step: (0, at(*step)))] * 3 + [half] * 2
+
+
+def weight_buffer(tile):
+    return pltpu.VMEM((RB - 1, KB, tile), BF16)
+
+
+def joined(pieces, buffer):
+    plane, own, near_x, near_y, far_plane, far_shared, other_x, other_y, other_far = pieces
+    mine = pl.multiple_of(PLANE + SHARED * plane[0], 16)
+    others = pl.multiple_of(PLANE + SHARED * (1 - plane[0]), 16)
+    for k, (near, other) in enumerate(((near_x, other_x), (near_y, other_y))):
+        buffer[k, :PLANE] = near[:PLANE]
+        buffer[k, pl.ds(mine, SHARED)] = near[PLANE:]
+        buffer[k, pl.ds(others, SHARED)] = other[...]
+    buffer[2, :PLANE] = far_plane[...]
+    buffer[2, pl.ds(mine, SHARED)] = far_shared[...]
+    buffer[2, pl.ds(others, SHARED)] = other_far[...]
+    return [own[...], buffer[0], buffer[1], buffer[2]]
 
 
 def qkv_call(x, vec, blocks, bias):
-    width = blocks[0].shape[2]
+    width = bias.shape[2]
     return call(
         qkv_kernel,
         (3,),
         [whole((PAD, D)), whole(vec.shape)]
-        + attn_specs(width, lambda j: j)
+        + weight_specs(width, lambda j: j)
         + [pl.BlockSpec((1, 1, width), lambda j: (j, 0, 0))],
         [whole((D, PAD)), pl.BlockSpec((PAD, width), lambda j: (0, j))],
         [sds((D, PAD)), sds((PAD, 3 * width))],
         2 * PAD * D * 3 * width,
         2 * D * 3 * width + 4 * PAD * D + 6 * PAD * width,
-        [pltpu.VMEM((PAD, D), BF16)],
+        [pltpu.VMEM((PAD, D), BF16), weight_buffer(width)],
     )(x, vec, *blocks, bias)
 
 
@@ -162,9 +206,11 @@
 
 
 def combine_kernel(mixed, *rest):
-    part = rest[5]
-    for k, w in enumerate(joined(rest[:5])):
-        part[:, k * KB : (k + 1) * KB] = mm_nt(mixed[...], w).astype(BF16)
+    top, bottom, buffer = rest[9:]
+    for k, w in enumerate(joined(rest[:9], buffer)):
+        term = mm_nt(mixed[...], w).astype(BF16)
+        top[:, k * KB : (k + 1) * KB] = term[:TOP]
+        bottom[:, k * KB : (k + 1) * KB] = term[TOP:]
 
 
 def combine_call(mixed, blocks):
@@ -172,11 +218,12 @@
     return call(
         combine_kernel,
         (1,),
-        [whole((PAD, width))] + attn_specs(width, lambda i: 3),
-        whole((PAD, D)),
-        sds((PAD, D)),
+        [whole((PAD, width))] + weight_specs(width, lambda i: 3),
+        piece_specs(),
+        piece_shapes(),
         2 * PAD * D * width,
         2 * (PAD * D + width * D + PAD * width),
+        [weight_buffer(width)],
     )(mixed, *blocks)
 
 
@@ -203,15 +250,16 @@
     return [sds((KB, width))] * 3 + [sds((half, width))] * 2
 
 
-def forward_kernel(x, part, sib, vec, *rest):
-    weights, (thresholds, cot), rest = rest[:5], rest[5:7], rest[7:]
+def forward_kernel(x, *rest):
+    parts, vec, rest = rest[:4], rest[4], rest[5:]
+    weights, (thresholds, cot), rest = rest[:9], rest[9:11], rest[11:]
     resid, normed_t, hidden, slope = rest[:4]
     deltas = rest[4:9]
-    normed, cot_t = rest[9:]
+    normed, cot_t, buffer = rest[9:]
 
     @pl.when(pl.program_id(0) == 0)
     def _():
-        total = x[...].astype(F32) + (part[...].astype(F32) + sib[...].astype(F32)) + vec[BASELINE : BASELINE + 1]
+        total = x[...].astype(F32) + load_sum(parts) + vec[BASELINE : BASELINE + 1]
         total = jnp.where(row_mask(total.shape), total, 0.0)
         resid[...] = total
         standard, _r = standardize(total)
@@ -221,7 +269,7 @@
         cot_t[...] = cot[...].astype(F32).T.astype(BF16)
 
     expanded = thresholds[...]
-    for k, w in enumerate(joined(weights)):
+    for k, w in enumerate(joined(weights, buffer)):
         expanded = expanded + mm(normed[:, k * KB : (k + 1) * KB], w)
     gate = jax.nn.sigmoid(SIGMOID_SLOPE * expanded)
     active = (expanded * gate).astype(BF16)
@@ -230,26 +278,25 @@
     split_rows(mm(cot_t[...], active), deltas)
 
 
-def forward_call(x, part, sib, vec, blocks, thresholds, cot):
-    width = blocks[0].shape[1]
+def forward_call(x, parts, vec, blocks, thresholds, cot):
+    width = thresholds.shape[1]
     tile = min(512, width)
     cols = pl.BlockSpec((PAD, tile), lambda t: (0, t))
-    half = pl.BlockSpec((KB // 2, tile), lambda t: (0, t))
-    wspecs = [pl.BlockSpec((KB, tile), lambda t: (0, t))] * 3 + [half] * 2
     return call(
         forward_kernel,
         (width // tile,),
-        [whole((PAD, D))] * 3
+        [whole((PAD, D))]
+        + piece_specs() * 2
         + [whole(vec.shape)]
-        + wspecs
+        + weight_specs(tile, lambda t: t)
         + [pl.BlockSpec((1, tile), lambda t: (0, t)), whole((PAD, D))],
         [whole((PAD, D)), whole((D, PAD)), cols, cols] + delta_specs(tile, lambda t: (0, t)),
         [sds((PAD, D), F32), sds((D, PAD)), sds((PAD, width)), sds((PAD, width))] + delta_shapes(width),
         4 * PAD * D * width,
         4 * D * width + 14 * PAD * D + 4 * PAD * width,
-        [pltpu.VMEM((PAD, D), BF16), pltpu.VMEM((D, PAD), BF16)],
+        [pltpu.VMEM((PAD, D), BF16), pltpu.VMEM((D, PAD), BF16), weight_buffer(tile)],
         transcendentals=PAD * width,
-    )(x, part, sib, vec, *blocks, thresholds, cot)
+    )(x, *parts, vec, *blocks, thresholds, cot)
 
 
 def accumulate(total, at, term):
@@ -265,32 +312,27 @@
 
 
 def backward_kernel(cot, *rest):
-    narrow, (slope, hidden, normed_t), wide, rest = rest[:5], rest[5:8], rest[8:13], rest[13:]
-    part, out, thresholds_sum = rest[:3]
-    deltas, (total, out_total) = rest[3:8], rest[8:]
+    narrow, (slope, hidden, normed_t), wide, rest = rest[:5], rest[5:8], rest[8:17], rest[17:]
+    part, out, thresholds_sum = rest[:2], rest[2:4], rest[4]
+    deltas, (total, out_total, wide_buffer) = rest[5:10], rest[10:]
     grad = None
     blocks = [n[...] for n in narrow]
-    blocks = blocks[:3] + [jnp.concatenate(blocks[3:], axis=1)]
+    blocks = blocks[:3] + [jnp.concatenate(blocks[3:], axis=0)]
     for k, n in enumerate(blocks):
         at = slice(k * KB, (k + 1) * KB)
-        term = mm_nt(cot[:, at], n)
+        term = mm(cot[:, at], n)
         grad = term if grad is None else grad + term
-        accumulate(out_total, at, mm(hidden[...], n))
+        accumulate(out_total, at, mm_nt(hidden[...], n))
     grad = (grad * slope[...].astype(F32)).astype(BF16)
     thresholds_sum[...] = jnp.sum(grad.astype(F32), axis=0, keepdims=True)
     split_rows(mm(normed_t[...], grad), deltas)
-    for k, w in enumerate(joined(wide)):
+    for k, w in enumerate(joined(wide, wide_buffer)):
         accumulate(total, slice(k * KB, (k + 1) * KB), mm_nt(grad, w))
 
     @pl.when(pl.program_id(0) == pl.num_programs(0) - 1)
     def _():
-        part[...] = total[...].astype(BF16)
-        out[...] = out_total[...].astype(BF16)
-
-
-def narrow_specs(tile):
-    half = pl.BlockSpec((tile, KB // 2), lambda t: (t, 0))
-    return [pl.BlockSpec((tile, KB), lambda t: (t, 0))] * 3 + [half] * 2
+        store_pieces(part, total[...])
+        store_pieces(out, out_total[...])
 
 
 def backward_call(cot, narrow_blocks, slope, hidden, normed_t, wide_blocks):
@@ -301,21 +343,21 @@
         backward_kernel,
         (width // tile,),
         [whole((PAD, D))]
-        + narrow_specs(tile)
+        + plain_specs(tile, lambda t: t)
         + [cols, cols, whole((D, PAD))]
-        + [pl.BlockSpec((KB, tile), lambda t: (0, t))] * 3
-        + [pl.BlockSpec((KB // 2, tile), lambda t: (0, t))] * 2,
-        [whole((PAD, D))] * 2 + [pl.BlockSpec((1, tile), lambda t: (0, t))] + delta_specs(tile, lambda t: (0, t)),
-        [sds((PAD, D))] * 2 + [sds((1, width), F32)] + delta_shapes(width),
+        + weight_specs(tile, lambda t: t),
+        piece_specs() * 2 + [pl.BlockSpec((1, tile), lambda t: (0, t))] + delta_specs(tile, lambda t: (0, t)),
+        piece_shapes() * 2 + [sds((1, width), F32)] + delta_shapes(width),
         8 * PAD * D * width,
         6 * D * width + 8 * PAD * D + 4 * PAD * width,
-        [pltpu.VMEM((PAD, D), F32)] * 2,
+        [pltpu.VMEM((PAD, D), F32)] * 2 + [weight_buffer(tile)],
     )(cot, *narrow_blocks, slope, hidden, normed_t, *wide_blocks)
 
 
-def resid_kernel(part, sib, resid, cot, vec, *rest):
-    weights, (grad_resid, grad_mixed, grad_t, sums) = rest[:5], rest[5:]
-    upstream = part[...].astype(F32) + sib[...].astype(F32)
+def resid_kernel(*rest):
+    parts, (resid, cot, vec), rest = rest[:4], rest[4:7], rest[7:]
+    weights, (grad_resid, grad_mixed, grad_t, sums, buffer) = rest[:9], rest[9:]
+    upstream = load_sum(parts)
     standard, reciprocal = standardize(resid[...])
     sums[0:1] = jnp.sum(upstream * standard, axis=0, keepdims=True)
     sums[1:2] = jnp.sum(upstream, axis=0, keepdims=True)
@@ -326,24 +368,25 @@
     grad_resid[...] = grad
     rounded = grad.astype(BF16)
     total = None
-    for k, w in enumerate(joined(weights)):
+    for k, w in enumerate(joined(weights, buffer)):
         term = mm(rounded[:, k * KB : (k + 1) * KB], w)
         total = term if total is None else total + term
     grad_mixed[...] = total.astype(BF16)
     grad_t[...] = grad.T.astype(BF16)
 
 
-def resid_call(part, sib, resid, cot, vec, blocks):
-    width = blocks[0].shape[2]
+def resid_call(parts, resid, cot, vec, blocks):
+    width = blocks[1].shape[1] // 4
     return call(
         resid_kernel,
         (1,),
-        [whole((PAD, D))] * 4 + [whole(vec.shape)] + attn_specs(width, lambda i: 3),
+        piece_specs() * 2 + [whole((PAD, D))] * 2 + [whole(vec.shape)] + weight_specs(width, lambda i: 3),
         [whole((PAD, D)), whole((PAD, width)), whole((D, PAD)), whole((8, D))],
         [sds((PAD, D), F32), sds((PAD, width)), sds((D, PAD)), sds((8, D), F32)],
         2 * PAD * D * width,
         16 * PAD * D + 2 * width * D + 2 * PAD * width,
-    )(part, sib, resid, cot, vec, *blocks)
+        [weight_buffer(width)],
+    )(*parts, resid, cot, vec, *blocks)
 
 
 def attend_back_kernel(q, k, v, upstream, probs, grad_q, grad_k, grad_v):
@@ -388,22 +431,22 @@
 
 
 def project_kernel(gq, gk, gv, normed_t, grad_t, mixed, *rest):
-    weights, (part, sums), deltas, total = rest[:5], rest[5:7], rest[7:12], rest[12]
+    weights, part, sums, deltas, (total, buffer) = rest[:9], rest[9:11], rest[11], rest[12:17], rest[17:]
     step = pl.program_id(0)
 
     def one(j, g):
         grad = g[...]
         sums[0] = jnp.sum(grad.astype(F32), axis=0, keepdims=True)
         split_rows(mm(normed_t[...], grad), deltas)
-        for k, w in enumerate(joined(weights)):
+        for k, w in enumerate(joined(weights, buffer)):
             at = slice(k * KB, (k + 1) * KB)
             term = mm_nt(grad, w)
             if j == 0:
                 total[:, at] = term
-            elif j == 1:
+            else:
                 total[:, at] += term
-            else:
-                part[:, at] = (total[:, at] + term).astype(BF16)
+        if j == 2:
+            store_pieces(part, total[...])
 
     for j, g in enumerate((gq, gk, gv)):
         pl.when(step == j)(lambda j=j, g=g: one(j, g))
@@ -419,55 +462,66 @@
     return call(
         project_kernel,
         (4,),
-        [whole((PAD, width))] * 3 + [whole((D, PAD))] * 2 + [whole((PAD, width))] + attn_specs(width, at),
-        [whole((PAD, D)), pl.BlockSpec((1, 1, width), lambda j: (at(j), 0, 0))]
+        [whole((PAD, width))] * 3 + [whole((D, PAD))] * 2 + [whole((PAD, width))] + weight_specs(width, at),
+        piece_specs()
+        + [pl.BlockSpec((1, 1, width), lambda j: (at(j), 0, 0))]
         + delta_specs(width, lambda j: (0, j)),
-        [sds((PAD, D)), sds((3, 1, width), F32)] + delta_shapes(4 * width),
+        piece_shapes() + [sds((3, 1, width), F32)] + delta_shapes(4 * width),
         4 * PAD * D * 3 * width + 2 * PAD * D * width,
         4 * D * 4 * width + 6 * PAD * D + 6 * PAD * width,
-        [pltpu.VMEM((PAD, D), F32)],
+        [pltpu.VMEM((PAD, D), F32), weight_buffer(width)],
     )(*grads, normed_t, grad_t, mixed, *blocks)
 
 
-def tokens_kernel(part, sib, x, grad_resid, cot, vec, delta, sums):
-    upstream = part[...].astype(F32) + sib[...].astype(F32)
-    standard, reciprocal = standardize(x[...].astype(F32))
+def share(refs, at, value):
+    owners, _rows, features = refs.shape
+    for i in range(owners):
+        refs[i, at : at + PAD] = value[:, i * features : (i + 1) * features].astype(BF16)
+
+
+def tokens_kernel(*refs):
+    parts, ffn_parts, (x, resid, grad_resid, cot, vec, deltas, sums) = refs[:4], refs[4:8], refs[8:]
+    upstream = load_sum(parts)
+    tokens = x[...].astype(F32)
+    standard, reciprocal = standardize(tokens)
     sums[0:1] = jnp.sum(upstream * standard, axis=0, keepdims=True)
     sums[1:2] = jnp.sum(upstream, axis=0, keepdims=True)
     sums[2:8] = jnp.zeros((6, D), F32)
+    share(deltas, 0, load_sum(ffn_parts) + vec[RESIDUE : RESIDUE + 1] + (resid[...] - tokens))
     grad = grad_resid[...] + norm_backward(upstream, standard, reciprocal, vec[STRETCH : STRETCH + 1])
-    delta[...] = (grad - cot[...].astype(F32)).astype(BF16)
-
-
-def tokens_call(part, sib, x, grad_resid, cot, vec):
+    share(deltas, PAD, grad - cot[...].astype(F32))
+
+
+def tokens_call(parts, ffn_parts, x, resid, grad_resid, cot, vec, features):
     return call(
         tokens_kernel,
         (1,),
-        [whole((PAD, D))] * 5 + [whole(vec.shape)],
-        [whole((PAD, D)), whole((8, D))],
-        [sds((PAD, D)), sds((8, D), F32)],
-        20 * PAD * D,
-        14 * PAD * D,
-    )(part, sib, x, grad_resid, cot, vec)
-
-
-class Links:
-    def __init__(self):
-        self.sent = {1: [], 2: [], 3: [], "dp": []}
-
-    def permute(self, value, axis, pairs, link):
-        line = self.sent[link]
-        if len(line) >= DEPTH:
-            value = lax.optimization_barrier((value, line[-DEPTH]))[0]
-        got = lax.ppermute(value, axis, pairs)
-        line.append(got)
-        return got
-
-    def swap(self, value, k):
-        return self.permute(value, "row", [(i, i ^ k) for i in range(RB)], k)
-
-    def along(self, value, pairs):
-        return self.permute(value, "dp", pairs, "dp")
+        piece_specs() * 4 + [whole((PAD, D))] * 4 + [whole(vec.shape)],
+        [whole((D // features, 2 * PAD, features)), whole((8, D))],
+        [sds((D // features, 2 * PAD, features)), sds((8, D), F32)],
+        24 * PAD * D,
+        24 * PAD * D,
+    )(*parts, *ffn_parts, x, resid, grad_resid, cot, vec)
+
+
+def images_kernel(got, tokens, cot, layer, delta):
+    for j in range(RB):
+        at = slice(j * SEQ, (j + 1) * SEQ)
+        layer[at] = got[j, :SEQ].astype(F32) + tokens[at].astype(F32)
+        delta[at] = got[j, PAD : PAD + SEQ].astype(F32) + cot[at].astype(F32)
+
+
+def images_call(got, tokens, cot):
+    rows, features = tokens.shape
+    return call(
+        images_kernel,
+        (1,),
+        [whole(got.shape), whole((rows, features)), whole((rows, features))],
+        [whole((rows, features))] * 2,
+        [sds((rows, features), F32)] * 2,
+        4 * rows * features,
+        16 * rows * features,
+    )(got, tokens, cot)
 
 
 def swap(value, k):
@@ -489,21 +543,44 @@
     return total.astype(BF16)
 
 
-def col_gather(value):
+def col_gather(values):
     size = lax.axis_size("col")
+    lanes = values[0].shape[1]
+    wide = jnp.concatenate(values, axis=1)
     if size == 2:
-        other = lax.ppermute(value, "col", [(0, 1), (1, 0)])
+        other = lax.ppermute(wide, "col", [(0, 1), (1, 0)])
         first = lax.axis_index("col") == 0
-        return jnp.stack([jnp.where(first, value, other), jnp.where(first, other, value)], axis=-2)
-    return lax.all_gather(value, "col", axis=value.ndim - 1)
-
-
-def gather_far(links, near, axis, *earlier):
-    size = near[1].shape[axis] // 2
-    near_x, near_y = [after(block, *earlier) for block in near[1:3]] if earlier else near[1:3]
-    first = lax.slice_in_dim(near_x, 0, size, axis=axis)
-    second = lax.slice_in_dim(near_y, size, 2 * size, axis=axis)
-    return [links.swap(first, 2), links.swap(second, 1)]
+        columns = [jnp.where(first, wide, other), jnp.where(first, other, wide)]
+    else:
+        columns = list(lax.all_gather(wide, "col"))
+    parts = [column[:, k * lanes : (k + 1) * lanes] for k in range(len(values)) for column in columns]
+    return jnp.concatenate(parts, axis=1)
+
+
+class Gather:
+    def __init__(self, clock, weight, *earlier):
+        self.clock = clock
+        self.plane = lax.axis_index("dp") % 2
+        self.weight = weight
+        shared = lax.dynamic_slice_in_dim(weight, PLANE + SHARED * self.plane, SHARED, axis=0)
+        mine = after(jnp.concatenate([weight[:PLANE], shared]), *earlier)
+        self.near = [swap(mine, 1), swap(mine, 2)]
+
+    def across(self, value):
+        return lax.ppermute(value, "dp", [(i, i ^ 1) for i in range(lax.axis_size("dp"))])
+
+    def relay(self):
+        near_x, near_y = self.near = self.clock(*self.near)
+        self.far = [swap(near_x[:PLANE], 2), swap(near_y[PLANE:], 1)]
+        self.other = [self.across(near_x[PLANE:]), self.across(near_y[PLANE:])]
+
+    def hand_over(self, *earlier):
+        *self.far, self.other[0] = self.clock(*self.far, self.other[0], *earlier)[:3]
+        self.other.append(self.across(self.far[1]))
+
+    def pieces(self):
+        self.other[1:] = self.clock(*self.other[1:])
+        return [self.plane.astype(jnp.int32)[None], self.weight, *self.near, *self.far, *self.other]
 
 
 def add(*terms):
@@ -600,7 +677,7 @@
     features = tokens.shape[1]
     width = projector.shape[2]
 
-    links = Links()
+    clock = Clock()
 
     def pick(stack, index, axis=0):
         return lax.dynamic_index_in_dim(stack, index, axis, keepdims=False)
@@ -608,102 +685,114 @@
     def padded(value):
         return jnp.pad(value.reshape(RB, SEQ, features), ((0, 0), (0, PAD - SEQ), (0, 0)))
 
-    def images_out(values, clock):
-        mine = pick(values.reshape(-1, PAD, RB, columns, features), lax.axis_index("col"), 3)
-        mine = mine[:, :SEQ]
-        sent = clock(*[swap(mine[:, :, k], k) for k in range(1, RB)])
-        got = jnp.stack([mine[:, :, 0], *sent])
-        return jnp.concatenate([pick(got, row ^ j) for j in range(RB)], axis=1)
-
     vectors = jnp.stack([stretch, lifting, baseline, dilation, elevation, residue, residue, residue])
-    vec = jnp.stack([vectors] + [links.swap(vectors, k) for k in range(1, RB)], axis=1)
-    vec = col_gather(vec).reshape(8, D)
-    both = jnp.stack([padded(tokens), padded(cotangent)])
-    near = [pick(both, row, 1)] + [links.swap(pick(both, row ^ k, 1), k) for k in range(1, RB)]
-    both = col_gather(jnp.stack(near, axis=2)).reshape(2, PAD, D)
-    x, cot = both[0], both[1]
-    attn = after(jnp.concatenate([projector, combiner.T[None]]), near[1], near[2])
-    attn_w = [attn, links.swap(attn, 1), links.swap(attn, 2)]
-    wide_w = [widener, links.swap(widener, 1), links.swap(widener, 2)]
-    attn_w += gather_far(links, attn_w, 1)
-    wide_w += gather_far(links, wide_w, 0)
-    narrow_w = [narrower, links.swap(narrower, 1), links.swap(narrower, 2)]
-    narrow_w += gather_far(links, narrow_w, 1)
+    coarse = lax.optimization_barrier(vectors.astype(BF16))
+    fine = (vectors - coarse.astype(F32)).astype(BF16)
+    images = jnp.concatenate([padded(tokens), padded(cotangent)], axis=1)
+    to = [jnp.concatenate([pick(images, row ^ k), coarse, fine]) for k in range(RB)]
+    near = clock(*[swap(to[k], k) for k in range(1, RB)])
+    attn_w = Gather(clock, jnp.concatenate([*projector, combiner.T], axis=1), *near)
+    got = clock(col_gather([to[0], *near]))[0]
+    x, cot = got[:PAD], got[PAD : 2 * PAD]
+    vec = got[2 * PAD : 2 * PAD + 8].astype(F32) + got[2 * PAD + 8 :].astype(F32)
+    attn_w.relay()
+    attn_w.hand_over()
+    wide_w = Gather(clock, widener, *attn_w.far)
+    attn_w = attn_w.pieces()
+    wide_w.relay()
 
     bias = jnp.stack([offsets[0], jnp.zeros((width,), F32), offsets[1]])[:, None]
     normed_one_t, qkv = qkv_call(x, vec, attn_w, bias)
+    wide_w.hand_over(qkv)
+    narrow = after(narrower.T, *wide_w.far)
+    near_n = [swap(narrow, 1), swap(narrow, 2)]
     mixed, probs = attend_call(qkv)
-    part = combine_call(mixed, attn_w)
-    out = forward_call(x, part, sibling(after(part, *wide_w[3:])), vec, wide_w, thresholds[None], cot)
+    parts = combine_call(mixed, attn_w)
+    others = [sibling(part) for part in parts]
+    wide_w = wide_w.pieces()
+    near_n = clock(*near_n)
+    far_n = [swap(near_n[0][: KB // 2], 2), swap(near_n[1][KB // 2 :], 1)]
+    others = clock(*others)
+    out = forward_call(x, [*parts, *others], vec, wide_w, thresholds[None], cot)
     resid, normed_two_t, hidden, slope = out[:4]
-    blocks_n = afters(out[4:], *narrow_w[3:])
+    *far_n, slope = clock(*far_n, slope)
+    blocks_n = afters(out[4:], *far_n)
     came_n = first_sends(blocks_n)
-
-    clock = Clock()
+    narrow_w = [narrow, *near_n, *far_n]
+
     out = backward_call(cot, narrow_w, slope, hidden, normed_two_t, wide_w)
-    part, ffn_part, thresholds_sum = out[:3]
-    blocks_w = out[3:]
-    *came_n, part = clock(*came_n, part)
+    parts, ffn_parts, thresholds_sum = out[:2], out[2:4], out[4]
+    blocks_w = out[5:]
+    *came_n, top = clock(*came_n, parts[0])
+    parts = [top, parts[1]]
     terms = last_terms(blocks_n, came_n)
     last_n = last_sends(terms)
-    came_w = first_sends(afters(blocks_w, *terms))
-    grad_resid, grad_mixed, grad_t, sums_two = resid_call(part, sibling(part), resid, cot, vec, attn_w)
+    came_w = list(first_sends(afters(blocks_w, *terms)))
+    others = [sibling(part) for part in parts]
+    grad_resid, grad_mixed, grad_t, sums_two = resid_call([*parts, *others], resid, cot, vec, attn_w)
     *last_n, grad_mixed = clock(*last_n, grad_mixed)
     halves = jnp.concatenate(own_sums(blocks_n, came_n, last_n))
     sum_n = LineSum(clock, halves)
+    ffn_others = [sibling(after(part, *last_n)) for part in ffn_parts]
     grads = attend_back_call(qkv, after(grad_mixed, halves), probs)
     out = project_call(grads, normed_one_t, grad_t, mixed, attn_w)
-    part, grad_sums = out[:2]
-    *came_w, part = clock(*came_w, part)
+    parts, grad_sums = out[:2], out[2]
+    came_w[0], came_w[1], top, *ffn_others = clock(*came_w, parts[0], *ffn_others)
+    parts = [top, parts[1]]
     terms = last_terms(blocks_w, came_w)
-    last_w = last_sends(terms)
-    sum_n.advance()
-    blocks_p = afters(out[2:], *terms)
-    came_p = first_sends(blocks_p)
-    last_w = clock(*last_w)
-    sum_w = LineSum(clock, jnp.concatenate(own_sums(blocks_w, came_w, last_w)))
-    other = sibling(after(part, *last_w))
+    last_w = list(last_sends(terms))
+    blocks_p = afters(out[3:], *terms)
+    came_p = list(first_sends(blocks_p))
+    others = clock(*[sibling(part) for part in parts])
+    deltas, sums_one = tokens_call(
+        [*parts, *others], [*ffn_parts, *ffn_others], x, resid, grad_resid, cot, vec, features
+    )
+    featured = jnp.concatenate([sums_one[:2], sums_two[:4]]).reshape(6, RB, columns, features)
+    featured = pick(featured, lax.axis_index("col"), 2)
+    shared = jnp.concatenate([grad_sums[0, 0], grad_sums[2, 0], thresholds_sum[0]])
+    size = 6 * features + shared.shape[0]
+    lines = -(-size // (16 * features)) * 16
+    mine = pick(deltas.reshape(RB, columns, 2 * PAD, features), lax.axis_index("col"), 1)
+    fill = jnp.zeros((lines * features - size,), F32)
+    to = []
+    for j in range(RB):
+        small = pick(featured, row ^ j, 1).reshape(-1)
+        small = jnp.concatenate([small, shared, fill]).reshape(lines, features)
+        to.append(jnp.concatenate([pick(mine, row ^ j), small.astype(BF16)]))
+    last_w[0], last_w[1], to = clock(*last_w, jnp.stack(to))
+    sum_w = [LineSum(clock, half) for half in own_sums(blocks_w, came_w, last_w)]
     sum_n.advance()
     came_p = clock(*came_p)
     last_p = last_sends(last_terms(blocks_p, came_p))
-    other = clock(other)[0]
-    delta, sums_one = tokens_call(part, other, x, grad_resid, cot, vec)
-    sum_w.advance()
+    sum_n.advance()
+    sum_w[0].advance()
+    sum_w[1].advance()
     last_p = clock(*last_p)
     halves_p = own_sums(blocks_p, came_p, last_p)
-    sum_p = [LineSum(clock, halves_p[0])]
-
-    featured = jnp.concatenate([sums_one[:2], sums_two[:4]]).reshape(6, RB, columns, features)
-    featured = pick(featured, lax.axis_index("col"), 2)
-    shared = jnp.concatenate([grad_sums[0, 0], grad_sums[2, 0], thresholds_sum[0]])
-    pack = [jnp.concatenate([featured[:, k].reshape(-1), shared]) for k in range(RB)]
-    sent = clock(*[swap(after(pack[k], *halves_p), k) for k in range(1, RB)])
-    small = add(pack[0], *sent).astype(BF16)
-    size, line = small.shape[0], 4 * width
-    lines = -(-size // (16 * line)) * 16
-    small = jnp.pad(small, (0, lines * line - size)).reshape(lines, line)
-    sum_p.append(LineSum(clock, jnp.concatenate([halves_p[1], small])))
-    ffn_other = sibling(after(ffn_part, *sent))
+    sum_p = [LineSum(clock, half) for half in halves_p]
+    got = lax.all_to_all(after(to, *halves_p), "row", 0, 0)
+    sum_w[0].advance()
     sum_n.advance()
+    sum_w[1].advance()
     sum_p[0].advance()
-    sum_w.advance()
-    sum_p[1].advance()
-    ffn_other = clock(ffn_other)[0]
-    ffn = ffn_part.astype(F32) + ffn_other.astype(F32) + vec[RESIDUE]
-    layer = (ffn + (resid - x.astype(F32))).astype(BF16)
     sum_p[0].advance()
     sum_p[1].advance()
-    outs = images_out(jnp.stack([layer, delta]), clock)
-    layer_output = outs[0] + tokens.astype(F32)
-    tokens_delta = outs[1] + cotangent.astype(F32)
-    for line_sum in (sum_n, sum_w, *sum_p):
+    got = clock(got)[0]
+    small = got[:, 2 * PAD :].astype(F32)
+    sum_s = LineSum(clock, sum([small[j] for j in range(1, RB)], small[0]))
+    narrower_delta = clock(sum_n.value.astype(F32).T)[0]
+    sum_w[0].advance()
+    sum_w[1].advance()
+    sum_p[1].advance()
+    sum_s.advance()
+    layer_output, tokens_delta = images_call(got, tokens, cotangent)
+    sum_s.advance()
+    for line_sum in (sum_n, sum_s, *sum_w, *sum_p):
         while line_sum.steps:
             line_sum.advance()
-    narrower_delta = sum_n.value.astype(F32).T
-    widener_delta = sum_w.value.astype(F32)
-    first, second = [line_sum.value for line_sum in sum_p]
-    small = second[KB // 2 :].reshape(-1)[:size].astype(F32)
-    total_p = jnp.concatenate([first, second[: KB // 2]]).astype(F32)
+    widener_delta = jnp.concatenate([line_sum.value for line_sum in sum_w]).astype(F32)
+    small = sum_s.value.reshape(-1)[:size]
+    total_p = jnp.concatenate([line_sum.value for line_sum in sum_p]).astype(F32)
     projector_delta = jnp.stack([total_p[:, j * width : (j + 1) * width] for j in range(3)])
     combiner_delta = total_p[:, 3 * width :].T
 

time: 371 us -> 357 us (0.962)
  waiting for transfers between devices: 111 us -> 91.2 us
  starting transfers between devices: 64.8 us -> 77.5 us
  local copies, waits for them, and re-layouts: 42 us -> 33.4 us
  Pallas kernels: 98.3 us -> 104 us
  other arithmetic: 47.8 us -> 43.6 us
    ppermute x20 -> x7, waiting for transfers between devices: 62.3 us -> 10.2 us  [the longest x6 9.6 us: across(): lax.ppermute(value, 'dp', [(i, i ^ 1) for i in range(lax.axis_size('dp'))])]
    ppermute x18 -> x27, waiting for transfers between devices: 29.5 us -> 52.2 us  [swap(): return lax.ppermute(value, 'row', [(i, i ^ k) for i in range(RB)])]
    ppermute x20 -> x7, starting transfers between devices: 18.4 us -> 7.21 us  [the longest x6 7.2 us: across(): lax.ppermute(value, 'dp', [(i, i ^ 1) for i in range(lax.axis_size('dp'))])]
    ppermute x12 -> x18, waiting for transfers between devices: 19.3 us -> 28.7 us  [send(): self.moved = lax.ppermute(self.value, 'dp', self.steps[0][1])]
    ppermute x18 -> x27, starting transfers between devices: 19.5 us -> 28.7 us  [swap(): return lax.ppermute(value, 'row', [(i, i ^ k) for i in range(RB)])]
    ppermute x12 -> x18, starting transfers between devices: 26.8 us -> 35.8 us  [send(): self.moved = lax.ppermute(self.value, 'dp', self.steps[0][1])]
    unnamed x91 -> x125, local copies, waits for them, and re-layouts: 7.12 us -> 15.2 us
    concatenate x1 -> x5, local copies, waits for them, and re-layouts: 8.36 us -> 1.17 us  [the longest x4 1.07 us: per_device(): small = jnp.concatenate([small, shared, fill]).reshape(lines, features)]
  transfers between devices with their start and end apart: 54 -> 61, of which waited for: 21 -> 23; matrix products, arithmetic and copies ran while one was open for 21% -> 18% of each run, Pallas kernels for 27% -> 30%
where the time goes in v4:
time: 357 us; the launch traced here: 352 us
  Pallas kernels  104 us (29%)
  waiting for transfers between devices  91.2 us (26%)
  starting transfers between devices  77.5 us (22%)
  other arithmetic  43.6 us (12%)
  local copies, waits for them, and re-layouts  33.4 us (9%)
    ppermute x27, waiting for transfers between devices, swap(): return lax.ppermute(value, 'row', [(i, i ^ k) for i in range(RB)])  52.2 us
    ppermute x18, starting transfers between devices, send(): self.moved = lax.ppermute(self.value, 'dp', self.steps[0][1])  35.8 us
    ppermute x27, starting transfers between devices, swap(): return lax.ppermute(value, 'row', [(i, i ^ k) for i in range(RB)])  28.7 us
    ppermute x18, waiting for transfers between devices, send(): self.moved = lax.ppermute(self.value, 'dp', self.steps[0][1])  28.7 us
    convert_element_type x19, other arithmetic, add(): return total.astype(terms[0].dtype)  28.4 us
    pallas_call x1, Pallas kernels, backward_call(): call(backward_kernel, (width // tile,), [whole((PAD, D))] + plain_specs(t...  28 us
    unnamed x125, local copies, waits for them, and re-layouts  15.2 us
    pallas_call x1, Pallas kernels, forward_call(): call(forward_kernel, (width // tile,), [whole((PAD, D))] + piece_specs()...  14.9 us
  transfers between devices with their start and end apart: 61, of which 23 were waited for; matrix products, arithmetic and copies ran while one was open for 18% of the time, Pallas kernels for 30%

profile of v4, /device:TPU:0, one launch (start us, length us, event | category | flops | bytes accessed | tf_op | source)
XLA Modules:
  0.0 351.8 jit_solution(11503404493857570745)
XLA Ops:
  3.6 3.0 collective-permute-start
  8.2 6.6 %collective-permute-done = bf16[1200,128]{1,0:T(8,128)(2,1)S(1)} collective-permute-done((bf16[1200,128]{1,0:T(8,128)(2,1)S(1)}, bf16[1200,128]{1,0:T(8,128)(2,1)S(1)}, u32[]{:S(2)}, u32[]{:S(2)}) %collective-permute-start) | collective-permute-done | bytes 307232 | tf_op jit(solution)/shard_map/ppermute | solution.py:528
  14.7 7.2 %collective-permute-done.1 = bf16[1200,128]{1,0:T(8,128)(2,1)S(1)} collective-permute-done((bf16[1200,128]{1,0:T(8,128)(2,1)S(1)}, bf16[1200,128]{1,0:T(8,128)(2,1)S(1)}, u32[]{:S(2)}, u32[]{:S(2)}) %collective-permute-start.1) | collective-permute-done | bytes 307232 | tf_op jit(solution)/shard_map/ppermute | solution.py:528
  30.1 12.9 %collective-permute-done.4.rest_2_.rest_9_ = bf16[176,2048]{1,0:T(8,128)(2,1)S(1)} collective-permute-done((bf16[176,2048]{1,0:T(8,128)(2,1)S(1)}, bf16[176,2048]{1,0:T(8,128)(2,1)S(1)}, u32[]{:S(2)}, u32[]{:S(2)}) %collective-permute-start.4) | collective-permute-done | bytes 720928 | tf_op jit(solution)/shard_map/ppermute | solution.py:528
  49.6 5.1 %collective-permute-done.7.rest_5_.rest_12_ = bf16[80,2048]{1,0:T(8,128)(2,1)} collective-permute-done((bf16[80,2048]{1,0:T(8,128)(2,1)}, bf16[80,2048]{1,0:T(8,128)(2,1)}, u32[]{:S(2)}, u32[]{:S(2)}) %collective-permute-start.7) | collective-permute-done | bytes 327712 | tf_op jit(solution)/shard_map/ppermute | solution.py:528
  60.8 2.8 copy.32
  63.6 5.3 %collective-permute-done.11.rest_7_.rest_14_ = bf16[80,2048]{1,0:T(8,128)(2,1)S(1)} collective-permute-done((bf16[80,2048]{1,0:T(8,128)(2,1)}, bf16[80,2048]{1,0:T(8,128)(2,1)S(1)}, u32[]{:S(2)}, u32[]{:S(2)}) %collective-permute-start.11) | collective-permute-done | bytes 327712 | tf_op jit(solution)/shard_map/ppermute | solution.py:570
  68.9 3.5 collective-permute-done.12.rest_8_.rest_15_
  80.4 3.2 fusion.8
  83.6 7.0 %shard_map.245 = (bf16[1024,592]{1,0:T(8,128)(2,1)}, bf16[592,1536]{1,0:T(8,128)(2,1)}) custom-call(bf16[592,1024]{1,0:T(8,128)(2,1)} %get-tuple-element.300.x.refs_8_, f32[8,1024]{1,0:T(8,128)} %convert_add_fusion.vec.rest_4_.rest_6_.refs_12_, s32[1]{0:T(128)} %bitcast.15.rest_0_.rest_5_.rest_8_.rest_7_, bf16[256,2048]{1,0:T(8,128)(2,1)} %copy-done, ...), custom_call_target="tpu_custom_call" | custom-call | flops 29097984 | bytes 115456 | tf_op jit(solution)/shard_map/pallas_call | solution.py:155
  95.3 9.2 %shard_map.246 = (bf16[592,512]{1,0:T(8,128)(2,1)}, bf16[8,592,592]{2,1,0:T(8,128)(2,1)}) custom-call(bf16[592,1536]{1,0:T(8,128)(2,1)} %get-tuple-element.157.q.k.v, bf16[592,1536]{1,0:T(8,128)(2,1)} %get-tuple-element.157.q.k.v, bf16[592,1536]{1,0:T(8,128)(2,1)} %get-tuple-element.157.q.k.v), custom_call_target="tpu_custom_call" | custom-call | flops 22429696 | bytes 87616 | tf_op jit(solution)/shard_map/pallas_call | solution.py:196
  104.5 3.2 shard_map.247
  108.3 4.5 %collective-permute-done.16.rest_1_ = bf16[256,2048]{1,0:T(8,128)(2,1)S(1)} collective-permute-done((bf16[256,2048]{1,0:T(8,128)(2,1)S(1)}, bf16[256,2048]{1,0:T(8,128)(2,1)S(1)}, u32[]{:S(2)}, u32[]{:S(2)}) %collective-permute-start.16) | collective-permute-done | bytes 1048608 | tf_op jit(solution)/shard_map/ppermute | solution.py:528
  118.0 14.9 %shard_map.248 = (f32[592,1024]{1,0:T(8,128)}, bf16[1024,592]{1,0:T(8,128)(2,1)}, bf16[592,2048]{1,0:T(8,128)(2,1)}, bf16[592,2048]{1,0:T(8,128)(2,1)}, bf16[256...) custom-call(bf16[592,1024]{1,0:T(8,128)(2,1)} %get-tuple-element.300, ...), custom_call_target="tpu_custom_call" | custom-call | flops 77594624 | bytes 339456 | tf_op jit(solution)/shard_map/pallas_call | solution.py:285
  135.9 28.0 %shard_map.249 = (bf16[304,1024]{1,0:T(8,128)(2,1)}, bf16[288,1024]{1,0:T(8,128)(2,1)}, bf16[304,1024]{1,0:T(8,128)(2,1)}, bf16[288,1024]{1,0:T(8,128)(2,1)}, f3...) custom-call(bf16[592,1024]{1,0:T(8,128)(2,1)} %get-tuple-element.301, ...), custom_call_target="tpu_custom_call" | custom-call | flops 155189248 | bytes 348160 | tf_op jit(solution)/shard_map/pallas_call | solution.py:342
  173.9 7.4 %shard_map.250 = (f32[592,1024]{1,0:T(8,128)}, bf16[592,512]{1,0:T(8,128)(2,1)}, bf16[1024,592]{1,0:T(8,128)(2,1)}, f32[8,1024]{1,0:T(8,128)}) custom-call(bf16[304,1024]{1,0:T(8,128)(2,1)} %get-tuple-element.193.rest_0_, bf16[288,1024]{1,0:T(8,128)(2,1)} %get-tuple-element.194.rest_1_, bf16[304,1024]{1,0:T(8,128)(2,1)} %copy-done.30, ...), custom_call_target="tpu_custom_call" | custom-call | flops 9699328 | bytes 177408 | tf_op jit(solution)/shard_map/pallas_call | solution.py:380
  182.0 2.9 collective-permute-done.28
  190.6 11.7 %shard_map.251 = (bf16[592,512]{1,0:T(8,128)(2,1)}, bf16[592,512]{1,0:T(8,128)(2,1)}, bf16[592,512]{1,0:T(8,128)(2,1)}) custom-call(bf16[592,1536]{1,0:T(8,128)(2,1)} %get-tuple-element.157.q.k.v, bf16[592,1536]{1,0:T(8,128)(2,1)} %get-tuple-element.157.q.k.v, bf16[592,1536]{1,0:T(8,128)(2,1)} %get-tuple-element.157.q.k.v, ...), custom_call_target="tpu_custom_call" | custom-call | flops 44859392 | bytes 87616 | tf_op jit(solution)/shard_map/pallas_call | solution.py:422
  202.3 10.7 %shard_map.252 = (bf16[304,1024]{1,0:T(8,128)(2,1)}, bf16[288,1024]{1,0:T(8,128)(2,1)}, f32[3,1,512]{2,1,0:T(1,128)}, bf16[256,2048]{1,0:T(8,128)(2,1)}, bf16[25...) custom-call(bf16[592,512]{1,0:T(8,128)(2,1)} %get-tuple-element.204.gq, ...), custom_call_target="tpu_custom_call" | custom-call | flops 67895296 | bytes 216320 | tf_op jit(solution)/shard_map/pallas_call | solution.py:462
  222.5 8.6 %shard_map.253 = (bf16[8,1184,128]{2,1,0:T(8,128)(2,1)}, f32[8,1024]{1,0:T(8,128)}) custom-call(bf16[304,1024]{1,0:T(8,128)(2,1)} %get-tuple-element.217.refs_0_, bf16[288,1024]{1,0:T(8,128)(2,1)} %get-tuple-element.218.refs_1_, bf16[304,1024]{1,0:T(8,128)(2,1)} %collective-permute-done.36.refs_2_, bf16[288,1024]{1,0:T(8,128)(2,1)} %collective-permute-done.37.refs_3_, ...), custom_call_target="tpu_custom_call" | custom-call | flops 227328 | bytes 227328 | tf_op jit(solution)/shard_map/pallas_call | solution.py:496
  242.4 5.1 %collective-permute-start.44 = (bf16[128,2048]{1,0:T(8,128)(2,1)S(1)}, bf16[128,2048]{1,0:T(8,128)(2,1)S(1)}, u32[]{:S(2)}, u32[]{:S(2)}) collective-permute-start(bf16[128,2048]{1,0:T(8,128)(2,1)S(1)} %get-tuple-element.318), channel_id=1, source_target_pairs={{0,8},{24,16},{1,9},{25,17},{2,10},{26,18},{3,11},{27,19},{4,12},{... | collective-permute-start | bytes 1572872 | tf_op jit(solution)/shard_map/ppermute | solution.py:622
  248.9 4.3 %collective-permute-done.39 = bf16[256,2048]{1,0:T(8,128)(2,1)} collective-permute-done((bf16[256,2048]{1,0:T(8,128)(2,1)}, bf16[256,2048]{1,0:T(8,128)(2,1)}, u32[]{:S(2)}, u32[]{:S(2)}) %collective-permute-start.39) | collective-permute-done | bytes 1048608 | tf_op jit(solution)/shard_map/ppermute | solution.py:528
  253.2 2.8 collective-permute-done.38
  262.3 6.4 %collective-permute-done.43 = bf16[128,2048]{1,0:T(8,128)(2,1)S(1)} collective-permute-done((bf16[128,2048]{1,0:T(8,128)(2,1)S(1)}, bf16[128,2048]{1,0:T(8,128)(2,1)S(1)}, u32[]{:S(2)}, u32[]{:S(2)}) %collective-permute-start.43) | collective-permute-done | bytes 524320 | tf_op jit(solution)/shard_map/ppermute | solution.py:622
  275.9 5.5 %collective-permute-start.47 = (bf16[128,2048]{1,0:T(8,128)(2,1)}, bf16[128,2048]{1,0:T(8,128)(2,1)}, u32[]{:S(2)}, u32[]{:S(2)}) collective-permute-start(bf16[128,2048]{1,0:T(8,128)(2,1)} %get-tuple-element.317), channel_id=1, source_target_pairs={{0,8},{24,16},{1,9},{25,17},{2,10},{26,18},{3,11},{27,19},{4,12},{... | collective-permute-start | bytes 1572872 | tf_op jit(solution)/shard_map/ppermute | solution.py:622
  283.5 3.5 %all-to-all-start = ((bf16[4,1216,128]{2,1,0:T(8,128)(2,1)}), bf16[4,1216,128]{2,1,0:T(8,128)(2,1)S(1)}, u32[]{:S(2)}, u32[]{:S(2)}) async-start(bf16[4,1216,128]{2,1,0:T(8,128)(2,1)} %pad_maximum_fusion.1), calls=%async_computation | async-start | bytes 2490368 | tf_op jit(solution)/shard_map/all_to_all | solution.py:773
  290.4 5.4 %collective-permute-done.49 = bf16[256,2048]{1,0:T(8,128)(2,1)} collective-permute-done((bf16[256,2048]{1,0:T(8,128)(2,1)S(1)}, bf16[256,2048]{1,0:T(8,128)(2,1)}, u32[]{:S(2)}, u32[]{:S(2)}) %collective-permute-start.49) | collective-permute-done | bytes 1048608 | tf_op jit(solution)/shard_map/ppermute | solution.py:622
  310.0 6.1 %collective-permute-done.55 = bf16[128,2048]{1,0:T(8,128)(2,1)} collective-permute-done((bf16[128,2048]{1,0:T(8,128)(2,1)}, bf16[128,2048]{1,0:T(8,128)(2,1)}, u32[]{:S(2)}, u32[]{:S(2)}) %collective-permute-start.55) | collective-permute-done | bytes 524320 | tf_op jit(solution)/shard_map/ppermute | solution.py:622
  316.1 5.8 %collective-permute-start.53 = (f32[32,128]{1,0:T(8,128)S(1)}, f32[32,128]{1,0:T(8,128)S(1)}, u32[]{:S(2)}, u32[]{:S(2)}) collective-permute-start(f32[32,128]{1,0:T(8,128)S(1)} %fusion.3), channel_id=1, source_target_pairs={{0,8},{24,16},{1,9},{25,17},{2,10},{26,18},{3,11},{27,19},{4,12},{... | collective-permute-start | bytes 49160 | tf_op jit(solution)/shard_map/ppermute | solution.py:622
  327.3 3.3 shard_map.254
  335.2 6.9 %collective-permute-done.58 = f32[32,128]{1,0:T(8,128)S(1)} collective-permute-done((f32[32,128]{1,0:T(8,128)S(1)}, f32[32,128]{1,0:T(8,128)S(1)}, u32[]{:S(2)}, u32[]{:S(2)}) %collective-permute-start.58) | collective-permute-done | bytes 16416 | tf_op jit(solution)/shard_map/ppermute | solution.py:622
  345.0 3.8 %collective-permute-done.59 = bf16[128,2048]{1,0:T(8,128)(2,1)S(1)} collective-permute-done((bf16[128,2048]{1,0:T(8,128)(2,1)S(1)}, bf16[128,2048]{1,0:T(8,128)(2,1)S(1)}, u32[]{:S(2)}, u32[]{:S(2)}) %collective-permute-start.59) | collective-permute-done | bytes 524320 | tf_op jit(solution)/shard_map/ppermute | solution.py:622
  (316 shorter events, 133.0 us)
Async XLA Ops:
  24.3 18.6 %collective-permute-start.4 = (bf16[176,2048]{1,0:T(8,128)(2,1)S(1)}, bf16[176,2048]{1,0:T(8,128)(2,1)S(1)}, u32[]{:S(2)}, u32[]{:S(2)}) collective-permute-start(bf16[176,2048]{1,0:T(8,128)(2,1)S(1)} %pad_maximum_fusion.6), channel_id=1, source_target_pairs={{0,2},{2,0},{4,6},{6,4},{1,3},{3,1},{5,7},{7,5},{8,10},{10,8},{12,... | collective-permute-start | bytes 2162696 | tf_op jit(solution)/shard_map/ppermute | solution.py:528
  25.6 18.3 %collective-permute-start.5 = (bf16[176,2048]{1,0:T(8,128)(2,1)S(1)}, bf16[176,2048]{1,0:T(8,128)(2,1)S(1)}, u32[]{:S(2)}, u32[]{:S(2)}) collective-permute-start(bf16[176,2048]{1,0:T(8,128)(2,1)S(1)} %pad_maximum_fusion.6), channel_id=1, source_target_pairs={{0,4},{2,6},{4,0},{6,2},{1,5},{3,7},{5,1},{7,3},{8,12},{10,14},{12... | collective-permute-start | bytes 2162696 | tf_op jit(solution)/shard_map/ppermute | solution.py:528
  56.3 16.3 %collective-permute-start.10 = (bf16[176,2048]{1,0:T(8,128)(2,1)}, bf16[176,2048]{1,0:T(8,128)(2,1)S(1)}, u32[]{:S(2)}, u32[]{:S(2)}) collective-permute-start(bf16[176,2048]{1,0:T(8,128)(2,1)} %pad_maximum_fusion.5), channel_id=1, source_target_pairs={{0,4},{2,6},{4,0},{6,2},{1,5},{3,7},{5,1},{7,3},{8,12},{10,14},{12... | collective-permute-start | bytes 2162696 | tf_op jit(solution)/shard_map/ppermute | solution.py:528
  56.8 16.0 %collective-permute-start.9 = (bf16[176,2048]{1,0:T(8,128)(2,1)}, bf16[176,2048]{1,0:T(8,128)(2,1)S(1)}, u32[]{:S(2)}, u32[]{:S(2)}) collective-permute-start(bf16[176,2048]{1,0:T(8,128)(2,1)} %pad_maximum_fusion.5), channel_id=1, source_target_pairs={{0,2},{2,0},{4,6},{6,4},{1,3},{3,1},{5,7},{7,5},{8,10},{10,8},{12,... | collective-permute-start | bytes 2162696 | tf_op jit(solution)/shard_map/ppermute | solution.py:528
  74.4 16.3 %collective-permute-start.13 = (bf16[96,2048]{1,0:T(8,128)(2,1)}, bf16[96,2048]{1,0:T(8,128)(2,1)S(1)}, u32[]{:S(2)}, u32[]{:S(2)}) collective-permute-start(bf16[96,2048]{1,0:T(8,128)(2,1)} %slice.223), channel_id=1, source_target_pairs={{0,4},{2,6},{4,0},{6,2},{1,5},{3,7},{5,1},{7,3},{8,12},{10,14},{12... | collective-permute-start | bytes 1179656 | tf_op jit(solution)/shard_map/ppermute | solution.py:528
  91.6 21.2 %collective-permute-start.16 = (bf16[256,2048]{1,0:T(8,128)(2,1)S(1)}, bf16[256,2048]{1,0:T(8,128)(2,1)S(1)}, u32[]{:S(2)}, u32[]{:S(2)}) collective-permute-start(bf16[256,2048]{1,0:T(8,128)(2,1)S(1)} %bitcast.84), channel_id=1, source_target_pairs={{0,2},{2,0},{4,6},{6,4},{1,3},{3,1},{5,7},{7,5},{8,10},{10,8},{12,... | collective-permute-start | bytes 3145736 | tf_op jit(solution)/shard_map/ppermute | solution.py:528
  92.8 22.2 %collective-permute-start.17 = (bf16[256,2048]{1,0:T(8,128)(2,1)S(1)}, bf16[256,2048]{1,0:T(8,128)(2,1)S(1)}, u32[]{:S(2)}, u32[]{:S(2)}) collective-permute-start(bf16[256,2048]{1,0:T(8,128)(2,1)S(1)} %bitcast.85), channel_id=1, source_target_pairs={{0,4},{2,6},{4,0},{6,2},{1,5},{3,7},{5,1},{7,3},{8,12},{10,14},{12... | collective-permute-start | bytes 3145736 | tf_op jit(solution)/shard_map/ppermute | solution.py:528
  115.9 17.0 %collective-permute-start.20 = (bf16[128,2048]{1,0:T(8,128)(2,1)}, bf16[128,2048]{1,0:T(8,128)(2,1)S(1)}, u32[]{:S(2)}, u32[]{:S(2)}) collective-permute-start(bf16[128,2048]{1,0:T(8,128)(2,1)} %slice.231), channel_id=1, source_target_pairs={{0,4},{2,6},{4,0},{6,2},{1,5},{3,7},{5,1},{7,3},{8,12},{10,14},{12... | collective-permute-start | bytes 1572872 | tf_op jit(solution)/shard_map/ppermute | solution.py:528
  116.7 16.2 %collective-permute-start.21 = (bf16[128,2048]{1,0:T(8,128)(2,1)}, bf16[128,2048]{1,0:T(8,128)(2,1)S(1)}, u32[]{:S(2)}, u32[]{:S(2)}) collective-permute-start(bf16[128,2048]{1,0:T(8,128)(2,1)} %slice.232), channel_id=1, source_target_pairs={{0,2},{2,0},{4,6},{6,4},{1,3},{3,1},{5,7},{7,5},{8,10},{10,8},{12,... | collective-permute-start | bytes 1572872 | tf_op jit(solution)/shard_map/ppermute | solution.py:528
  133.0 31.0 %collective-permute-start.25 = (bf16[256,2048]{1,0:T(8,128)(2,1)}, bf16[256,2048]{1,0:T(8,128)(2,1)S(1)}, u32[]{:S(2)}, u32[]{:S(2)}) collective-permute-start(bf16[256,2048]{1,0:T(8,128)(2,1)} %get-tuple-element.184), channel_id=1, source_target_pairs={{0,4},{2,6},{4,0},{6,2},{1,5},{3,7},{5,1},{7,3},{8,12},{10,14},{12... | collective-permute-start | bytes 3145736 | tf_op jit(solution)/shard_map/ppermute | solution.py:528
  134.5 29.5 %collective-permute-start.24 = (bf16[256,2048]{1,0:T(8,128)(2,1)}, bf16[256,2048]{1,0:T(8,128)(2,1)S(1)}, u32[]{:S(2)}, u32[]{:S(2)}) collective-permute-start(bf16[256,2048]{1,0:T(8,128)(2,1)} %get-tuple-element.182), channel_id=1, source_target_pairs={{0,2},{2,0},{4,6},{6,4},{1,3},{3,1},{5,7},{7,5},{8,10},{10,8},{12,... | collective-permute-start | bytes 3145736 | tf_op jit(solution)/shard_map/ppermute | solution.py:528
  170.5 43.2 %collective-permute-start.27 = (bf16[256,2048]{1,0:T(8,128)(2,1)}, bf16[256,2048]{1,0:T(8,128)(2,1)}, u32[]{:S(2)}, u32[]{:S(2)}) collective-permute-start(bf16[256,2048]{1,0:T(8,128)(2,1)} %get-tuple-element.192), channel_id=1, source_target_pairs={{0,4},{2,6},{4,0},{6,2},{1,5},{3,7},{5,1},{7,3},{8,12},{10,14},{12... | collective-permute-start | bytes 3145736 | tf_op jit(solution)/shard_map/ppermute | solution.py:528
  171.6 42.2 %collective-permute-start.26 = (bf16[256,2048]{1,0:T(8,128)(2,1)}, bf16[256,2048]{1,0:T(8,128)(2,1)}, u32[]{:S(2)}, u32[]{:S(2)}) collective-permute-start(bf16[256,2048]{1,0:T(8,128)(2,1)} %get-tuple-element.190), channel_id=1, source_target_pairs={{0,2},{2,0},{4,6},{6,4},{1,3},{3,1},{5,7},{7,5},{8,10},{10,8},{12,... | collective-permute-start | bytes 3145736 | tf_op jit(solution)/shard_map/ppermute | solution.py:528
  184.9 28.9 %collective-permute-start.33 = (bf16[288,1024]{1,0:T(8,128)(2,1)}, bf16[288,1024]{1,0:T(8,128)(2,1)}, u32[]{:S(2)}, u32[]{:S(2)}) collective-permute-start(bf16[288,1024]{1,0:T(8,128)(2,1)} %get-tuple-element.213.refs_5_), channel_id=1, source_target_pairs={{0,1},{1,0},{2,3},{3,2},{4,5},{5,4},{6,7},{7,6},{8,9},{9,8},{10,11... | collective-permute-start | bytes 1769480 | tf_op jit(solution)/shard_map/ppermute | solution.py:538
  184.9 28.9 %collective-permute-start.32 = (bf16[304,1024]{1,0:T(8,128)(2,1)}, bf16[304,1024]{1,0:T(8,128)(2,1)}, u32[]{:S(2)}, u32[]{:S(2)}) collective-permute-start(bf16[304,1024]{1,0:T(8,128)(2,1)} %get-tuple-element.211.refs_4_), channel_id=1, source_target_pairs={{0,1},{1,0},{2,3},{3,2},{4,5},{5,4},{6,7},{7,6},{8,9},{9,8},{10,11... | collective-permute-start | bytes 1867784 | tf_op jit(solution)/shard_map/ppermute | solution.py:538
  187.4 51.6 %collective-permute-start.40 = (bf16[256,2048]{1,0:T(8,128)(2,1)S(1)}, bf16[256,2048]{1,0:T(8,128)(2,1)S(1)}, u32[]{:S(2)}, u32[]{:S(2)}) collective-permute-start(bf16[256,2048]{1,0:T(8,128)(2,1)S(1)} %pad_maximum_fusion.4), channel_id=1, source_target_pairs={{0,8},{24,16},{1,9},{25,17},{2,10},{26,18},{3,11},{27,19},{4,12},{... | collective-permute-start | bytes 3145736 | tf_op jit(solution)/shard_map/ppermute | solution.py:622
  216.5 22.6 %collective-permute-start.35 = (bf16[128,2048]{1,0:T(8,128)(2,1)}, bf16[128,2048]{1,0:T(8,128)(2,1)}, u32[]{:S(2)}, u32[]{:S(2)}) collective-permute-start(bf16[128,2048]{1,0:T(8,128)(2,1)} %add_convert_fusion.16), channel_id=1, source_target_pairs={{0,4},{2,6},{4,0},{6,2},{1,5},{3,7},{5,1},{7,3},{8,12},{10,14},{12... | collective-permute-start | bytes 1572872 | tf_op jit(solution)/shard_map/ppermute | solution.py:528
  219.6 19.5 %collective-permute-start.34 = (bf16[128,2048]{1,0:T(8,128)(2,1)}, bf16[128,2048]{1,0:T(8,128)(2,1)}, u32[]{:S(2)}, u32[]{:S(2)}) collective-permute-start(bf16[128,2048]{1,0:T(8,128)(2,1)} %add_convert_fusion.17), channel_id=1, source_target_pairs={{0,2},{2,0},{4,6},{6,4},{1,3},{3,1},{5,7},{7,5},{8,10},{10,8},{12,... | collective-permute-start | bytes 1572872 | tf_op jit(solution)/shard_map/ppermute | solution.py:528
  220.2 32.9 %collective-permute-start.39 = (bf16[256,2048]{1,0:T(8,128)(2,1)}, bf16[256,2048]{1,0:T(8,128)(2,1)}, u32[]{:S(2)}, u32[]{:S(2)}) collective-permute-start(bf16[256,2048]{1,0:T(8,128)(2,1)} %get-tuple-element.235), channel_id=1, source_target_pairs={{0,4},{2,6},{4,0},{6,2},{1,5},{3,7},{5,1},{7,3},{8,12},{10,14},{12... | collective-permute-start | bytes 3145736 | tf_op jit(solution)/shard_map/ppermute | solution.py:528
  221.1 34.8 %collective-permute-start.38 = (bf16[256,2048]{1,0:T(8,128)(2,1)}, bf16[256,2048]{1,0:T(8,128)(2,1)}, u32[]{:S(2)}, u32[]{:S(2)}) collective-permute-start(bf16[256,2048]{1,0:T(8,128)(2,1)} %get-tuple-element.233), channel_id=1, source_target_pairs={{0,2},{2,0},{4,6},{6,4},{1,3},{3,1},{5,7},{7,5},{8,10},{10,8},{12,... | collective-permute-start | bytes 3145736 | tf_op jit(solution)/shard_map/ppermute | solution.py:528
  239.5 20.5 %collective-permute-start.45 = (bf16[256,2048]{1,0:T(8,128)(2,1)S(1)}, bf16[256,2048]{1,0:T(8,128)(2,1)S(1)}, u32[]{:S(2)}, u32[]{:S(2)}) collective-permute-start(bf16[256,2048]{1,0:T(8,128)(2,1)S(1)} %add_convert_fusion.1), channel_id=1, source_target_pairs={{8,16},{16,8},{9,17},{17,9},{10,18},{18,10},{11,19},{19,11},{12,20... | collective-permute-start | bytes 3145736 | tf_op jit(solution)/shard_map/ppermute | solution.py:622
  242.4 18.1 %collective-permute-start.44 = (bf16[128,2048]{1,0:T(8,128)(2,1)S(1)}, bf16[128,2048]{1,0:T(8,128)(2,1)S(1)}, u32[]{:S(2)}, u32[]{:S(2)}) collective-permute-start(bf16[128,2048]{1,0:T(8,128)(2,1)S(1)} %get-tuple-element.318), channel_id=1, source_target_pairs={{0,8},{24,16},{1,9},{25,17},{2,10},{26,18},{3,11},{27,19},{4,12},{... | collective-permute-start | bytes 1572872 | tf_op jit(solution)/shard_map/ppermute | solution.py:622
  247.5 21.2 %collective-permute-start.43 = (bf16[128,2048]{1,0:T(8,128)(2,1)S(1)}, bf16[128,2048]{1,0:T(8,128)(2,1)S(1)}, u32[]{:S(2)}, u32[]{:S(2)}) collective-permute-start(bf16[128,2048]{1,0:T(8,128)(2,1)S(1)} %get-tuple-element.319), channel_id=1, source_target_pairs={{0,8},{24,16},{1,9},{25,17},{2,10},{26,18},{3,11},{27,19},{4,12},{... | collective-permute-start | bytes 1572872 | tf_op jit(solution)/shard_map/ppermute | solution.py:622
  260.7 26.4 %collective-permute-start.50 = (bf16[128,2048]{1,0:T(8,128)(2,1)S(1)}, bf16[128,2048]{1,0:T(8,128)(2,1)}, u32[]{:S(2)}, u32[]{:S(2)}) collective-permute-start(bf16[128,2048]{1,0:T(8,128)(2,1)S(1)} %add_convert_fusion.8), channel_id=1, source_target_pairs={{8,16},{16,8},{9,17},{17,9},{10,18},{18,10},{11,19},{19,11},{12,20... | collective-permute-start | bytes 1572872 | tf_op jit(solution)/shard_map/ppermute | solution.py:622
  268.7 27.2 %collective-permute-start.49 = (bf16[256,2048]{1,0:T(8,128)(2,1)S(1)}, bf16[256,2048]{1,0:T(8,128)(2,1)}, u32[]{:S(2)}, u32[]{:S(2)}) collective-permute-start(bf16[256,2048]{1,0:T(8,128)(2,1)S(1)} %add_convert_fusion), channel_id=1, source_target_pairs={{8,0},{16,24},{9,1},{17,25},{10,2},{18,26},{11,3},{19,27},{12,4},{... | collective-permute-start | bytes 3145736 | tf_op jit(solution)/shard_map/ppermute | solution.py:622
  271.8 24.1 %collective-permute-start.48 = (bf16[128,2048]{1,0:T(8,128)(2,1)S(1)}, bf16[128,2048]{1,0:T(8,128)(2,1)}, u32[]{:S(2)}, u32[]{:S(2)}) collective-permute-start(bf16[128,2048]{1,0:T(8,128)(2,1)S(1)} %add_convert_fusion.9), channel_id=1, source_target_pairs={{8,16},{16,8},{9,17},{17,9},{10,18},{18,10},{11,19},{19,11},{12,20... | collective-permute-start | bytes 1572872 | tf_op jit(solution)/shard_map/ppermute | solution.py:622
  275.9 21.9 %collective-permute-start.47 = (bf16[128,2048]{1,0:T(8,128)(2,1)}, bf16[128,2048]{1,0:T(8,128)(2,1)}, u32[]{:S(2)}, u32[]{:S(2)}) collective-permute-start(bf16[128,2048]{1,0:T(8,128)(2,1)} %get-tuple-element.317), channel_id=1, source_target_pairs={{0,8},{24,16},{1,9},{25,17},{2,10},{26,18},{3,11},{27,19},{4,12},{... | collective-permute-start | bytes 1572872 | tf_op jit(solution)/shard_map/ppermute | solution.py:622
  281.5 21.2 %collective-permute-start.46 = (bf16[128,2048]{1,0:T(8,128)(2,1)}, bf16[128,2048]{1,0:T(8,128)(2,1)}, u32[]{:S(2)}, u32[]{:S(2)}) collective-permute-start(bf16[128,2048]{1,0:T(8,128)(2,1)} %get-tuple-element.316), channel_id=1, source_target_pairs={{0,8},{24,16},{1,9},{25,17},{2,10},{26,18},{3,11},{27,19},{4,12},{... | collective-permute-start | bytes 1572872 | tf_op jit(solution)/shard_map/ppermute | solution.py:622
  283.5 22.0 %all-to-all-start = ((bf16[4,1216,128]{2,1,0:T(8,128)(2,1)}), bf16[4,1216,128]{2,1,0:T(8,128)(2,1)S(1)}, u32[]{:S(2)}, u32[]{:S(2)}) async-start(bf16[4,1216,128]{2,1,0:T(8,128)(2,1)} %pad_maximum_fusion.1), calls=%async_computation | async-start | bytes 2490368 | tf_op jit(solution)/shard_map/all_to_all | solution.py:773
  289.2 19.0 %collective-permute-start.56 = (bf16[128,2048]{1,0:T(8,128)(2,1)}, bf16[128,2048]{1,0:T(8,128)(2,1)}, u32[]{:S(2)}, u32[]{:S(2)}) collective-permute-start(bf16[128,2048]{1,0:T(8,128)(2,1)} %add_convert_fusion.3), channel_id=1, source_target_pairs={{8,0},{16,24},{9,1},{17,25},{10,2},{18,26},{11,3},{19,27},{12,4},{... | collective-permute-start | bytes 1572872 | tf_op jit(solution)/shard_map/ppermute | solution.py:622
  299.9 16.2 %collective-permute-start.55 = (bf16[128,2048]{1,0:T(8,128)(2,1)}, bf16[128,2048]{1,0:T(8,128)(2,1)}, u32[]{:S(2)}, u32[]{:S(2)}) collective-permute-start(bf16[128,2048]{1,0:T(8,128)(2,1)} %add_convert_fusion.4), channel_id=1, source_target_pairs={{8,0},{16,24},{9,1},{17,25},{10,2},{18,26},{11,3},{19,27},{12,4},{... | collective-permute-start | bytes 1572872 | tf_op jit(solution)/shard_map/ppermute | solution.py:622
  323.0 20.9 %collective-permute-start.52 = (bf16[128,2048]{1,0:T(8,128)(2,1)}, bf16[128,2048]{1,0:T(8,128)(2,1)}, u32[]{:S(2)}, u32[]{:S(2)}) collective-permute-start(bf16[128,2048]{1,0:T(8,128)(2,1)} %add_convert_fusion.6), channel_id=1, source_target_pairs={{8,0},{16,24},{9,1},{17,25},{10,2},{18,26},{11,3},{19,27},{12,4},{... | collective-permute-start | bytes 1572872 | tf_op jit(solution)/shard_map/ppermute | solution.py:622
  (79 other events, 767.0 us)
